TPU v7x, 256 devices: a whole 4x4x8 slice. The times are simulated.
256 devices in a mesh: sample: 32 (over z, y), head: 8 (over x, core).
Axes of the slice: x: 4, y: 4, z: 8, core: 2. Of those that a mesh axis runs over, the one named last changes fastest.
Arguments:
- child_stream: bfloat16 [32768, 1024], P('sample'), may hold values from -6 to 6
- cache_keys: bfloat16 [32768, 8, 1024], P('sample', None, 'head'), may hold values from -102 to 102
- cache_values: bfloat16 [32768, 8, 1024], P('sample', None, 'head'), may hold values from -6 to 6
- child_counts: int32 [32768], P('sample'), may hold values from 0 to 4, as said below
- child_slots: int32 [32768, 4], P('sample'), may hold values from -1 to 32767, as said below
- w_qkv: bfloat16 [3, 1024, 1024], P(None, None, 'head'), may hold values from -0.1875 to 0.1875
- w_out: bfloat16 [1024, 1024], P('head'), may hold values from -0.1875 to 0.1875
- w_up: bfloat16 [1024, 4096], P(None, 'head'), may hold values from -0.1875 to 0.1875
- w_down: bfloat16 [4096, 1024], P('head'), may hold values from -0.09375 to 0.09375
Outputs:
- layer_out: bfloat16 [32768, 1024], P('sample', 'head')
- new_kv: bfloat16 [32768, 2, 1024], P('sample', None, 'head')
Inputs may be any that keep to these rules, and one draw needn't show every extreme that they name: `child_counts`: the counts of the 1024 parents of one index of sample sum to 1024. `child_slots`: entry k of parent r names the slot of its k-th child for k < child_counts[r] and is -1 otherwise; every slot is named exactly once; slot j belongs to index j // 1024 of sample; the children that the parents of one index send to the slots of one index number 48 or 16, each for half of the indices in every row and every column of such pairs.
All inputs are finite; a program needn't handle non-finite values.
Results may differ from a plain program's by a relative error of at most 0.02.
Values may be sent and summed in bfloat16 or wider, within the bound.
No kernel may reach another device: no remote copies, remote signals or barrier semaphores. Data moves between devices by JAX's collectives and lax.ppermute only.
A program may use at most 128 MiB of HBM per device.

v0:
```python
import jax
import jax.numpy as jnp
from jax import lax
from jax.sharding import PartitionSpec as P

HD = 64


def rms_rows(stream):
    return stream * lax.rsqrt(jnp.mean(stream * stream, axis=-1, keepdims=True) + 1e-05)


def attend_items(queries, own_keys, own_values, key_rows, value_rows, head_size):
    item_count = queries.shape[0]
    head_count = queries.shape[1] // head_size
    token_positions = key_rows.shape[1]
    score_scale = 1.0 / head_size**0.5
    per_head_queries = queries.reshape(item_count, head_count, head_size)
    per_head_keys = key_rows.reshape(item_count, token_positions, head_count, head_size)
    per_head_values = value_rows.reshape(item_count, token_positions, head_count, head_size)
    current_keys = own_keys.reshape(item_count, head_count, head_size)
    current_values = own_values.reshape(item_count, head_count, head_size)
    stored_prefix_entries = (
        jnp.einsum(
            "okg,otkg->okt", per_head_queries, per_head_keys, preferred_element_type=jnp.float32
        )
        * score_scale
    )
    self_entry = (
        jnp.einsum(
            "ezl,ezl->ez", per_head_queries, current_keys, preferred_element_type=jnp.float32
        )
        * score_scale
    )
    scores = jnp.concatenate([stored_prefix_entries, self_entry[:, :, None]], axis=-1)
    highest = jnp.max(scores, axis=-1, keepdims=True)
    expo = jnp.exp(scores - highest)
    attention_weight = (expo / jnp.sum(expo, axis=-1, keepdims=True)).astype(jnp.bfloat16)
    attention_blend = jnp.einsum(
        "fet,ftes->fes",
        attention_weight[:, :, :token_positions],
        per_head_values,
        preferred_element_type=jnp.float32,
    )
    attention_blend = attention_blend + jnp.einsum(
        "is,isk->isk",
        attention_weight[:, :, token_positions],
        current_values,
        preferred_element_type=jnp.float32,
    )
    return attention_blend.reshape(item_count, head_count * head_size).astype(jnp.bfloat16)


def send_plan(counts, slots, peer_count, capacity):
    row_count = counts.shape[0]
    is_live = jnp.arange(4, dtype=jnp.int32)[None, :] < counts[:, None]
    owners = jnp.where(is_live, slots // row_count, peer_count).reshape(-1)
    onehot = (owners[:, None] == jnp.arange(peer_count, dtype=jnp.int32)[None, :]).astype(jnp.int32)
    ranking = jnp.sum(jnp.cumsum(onehot, axis=0) * onehot, axis=1) - 1
    position = jnp.where(owners < peer_count, owners * capacity + ranking, peer_count * capacity)
    parents = jnp.repeat(jnp.arange(row_count, dtype=jnp.int32), 4)
    local_slot = (slots % row_count).reshape(-1)
    send_parent = (
        jnp.zeros((peer_count * capacity,), jnp.int32).at[position].set(parents, mode="drop")
    )
    send_slot = (
        jnp.full((peer_count * capacity,), -1, jnp.int32).at[position].set(local_slot, mode="drop")
    )
    return (send_parent, send_slot)


def body(
    child_stream, cache_keys, cache_values, child_counts, child_slots, w_qkv, w_out, w_up, w_down
):
    row_count = child_stream.shape[0]
    peer_count = lax.axis_size("sample")
    head_groups = lax.axis_size("head")
    capacity = 3 * row_count // (2 * peer_count)
    stream = child_stream.astype(jnp.float32)
    normed = rms_rows(stream).astype(jnp.bfloat16)
    projected = jnp.einsum("rd,tdc->trc", normed, w_qkv, preferred_element_type=jnp.float32).astype(
        jnp.bfloat16
    )
    queries = projected[0]
    own_keys = projected[1]
    own_values = projected[2]
    new_kv = jnp.stack([own_keys, own_values], axis=1)
    send_parent, send_slot = send_plan(child_counts, child_slots, peer_count, capacity)
    recv_slot = lax.all_to_all(send_slot, "sample", split_axis=0, concat_axis=0, tiled=True)
    safe_slot = jnp.clip(recv_slot, 0, row_count - 1)
    item_queries = queries[safe_slot]
    item_keys = own_keys[safe_slot]
    item_values = own_values[safe_slot]
    moved_keys, moved_values = (
        lax.all_to_all(cache_keys[send_parent], "sample", split_axis=0, concat_axis=0, tiled=True),
        lax.all_to_all(
            cache_values[send_parent], "sample", split_axis=0, concat_axis=0, tiled=True
        ),
    )
    context = attend_items(item_queries, item_keys, item_values, moved_keys, moved_values, HD)
    target = jnp.where(recv_slot >= 0, recv_slot, row_count)
    attended = (
        jnp.zeros((row_count, queries.shape[1]), jnp.bfloat16).at[target].set(context, mode="drop")
    )
    partial_value = jnp.dot(attended, w_out, preferred_element_type=jnp.float32)
    feature_width = stream.shape[1] // head_groups
    stream_part = lax.dynamic_slice_in_dim(
        stream, lax.axis_index("head") * feature_width, feature_width, 1
    )
    hidden_part = (
        stream_part
        + lax.psum_scatter(
            partial_value.astype(jnp.bfloat16), "head", scatter_dimension=1, tiled=True
        ).astype(jnp.float32)
    ).astype(jnp.bfloat16)
    hidden = lax.all_gather(hidden_part, "head", axis=1, tiled=True)
    normed_two = rms_rows(hidden.astype(jnp.float32)).astype(jnp.bfloat16)
    activated = jax.nn.gelu(jnp.dot(normed_two, w_up, preferred_element_type=jnp.float32)).astype(
        jnp.bfloat16
    )
    down = jnp.dot(activated, w_down, preferred_element_type=jnp.float32)
    layer_out = (
        hidden_part.astype(jnp.float32)
        + lax.psum_scatter(
            down.astype(jnp.bfloat16), "head", scatter_dimension=1, tiled=True
        ).astype(jnp.float32)
    ).astype(jnp.bfloat16)
    return (layer_out, new_kv)


def solution(mesh):
    in_specs = (
        P("sample", None),
        P("sample", None, "head"),
        P("sample", None, "head"),
        P("sample"),
        P("sample", None),
        P(None, None, "head"),
        P("head", None),
        P(None, "head"),
        P("head", None),
    )
    out_specs = (P("sample", "head"), P("sample", None, "head"))
    return jax.shard_map(body, mesh=mesh, in_specs=in_specs, out_specs=out_specs, check_vma=False)
```

profile of v0, /device:TPU:1, one launch (start us, length us, event | category | flops | bytes accessed | tf_op | source)
XLA Modules:
  0.0 369.5 jit_solution(8621793423149060798)
XLA Ops:
  7.2 0.9 broadcast_multiply_fusion.1
  8.9 9.2 %reduce-window.6 = s32[32,32,128]{2,1,0:T(8,128)S(1)} reduce-window(s32[32,32,128]{2,1,0:T(8,128)S(1)} %fusion.30, s32[]{:T(128)} %constant.23.clone.1), window={size=1x1x128 pad=0_0x0_0x127_0}, to_apply=%region_0.0 | reduce-window | flops 16646144 | bytes 1048580 | tf_op jit(solution)/shard_map/reduce-window
  18.2 0.8 slice_reduce_fusion
  19.4 0.3 fusion.29
  19.7 0.3 copy.33
  20.0 0.3 lt.78
  20.6 0.3 mul.80
  21.5 15.5 %scatter_custom_fusion = s32[1536]{0:T(1024)S(1)} fusion(s32[4096]{0:T(1024)S(1)} %bitcast.80, s32[4096]{0:T(1024)S(1)} %reshape.223, s32[]{:T(128)} %constant.28.clone.1), kind=kCustom, calls=%fused_computation.91 | custom fusion | bytes 6148 | tf_op jit(solution)/shard_map/scatter | solution.py:67
  37.0 0.7 all_to_all.14
  37.7 12.0 %all-to-all-start = ((s32[32,48,1]{1,2,0:T(1,128)}), s32[32,48,1]{1,2,0:T(1,128)S(1)}, u32[]{:S(2)}, u32[]{:S(2)}) async-start(s32[32,48,1]{1,2,0:T(1,128)} %bitcast.5), calls=%async_computation | async-start | bytes 32768 | tf_op jit(solution)/shard_map/all_to_all | solution.py:89
  50.0 15.5 %scatter_custom_fusion.1 = s32[1536]{0:T(1024)S(1)} fusion(s32[4096]{0:T(1024)S(1)} %bitcast.81, s32[4096]{0:T(1024)S(1)} %reshape.231, s32[]{:T(128)} %constant.23.clone.1), kind=kCustom, calls=%fused_computation.88 | custom fusion | bytes 6148 | tf_op jit(solution)/shard_map/scatter | solution.py:64
  65.6 5.0 %gather_fusion.1 = bf16[1536,8,128]{2,1,0:T(8,128)(2,1)} fusion(bf16[1024,8,128]{2,1,0:T(8,128)(2,1)S(1)} %copy-done, s32[2048]{0:T(1024)S(1)} %pad_clamp_fusion), kind=kCustom, calls=%fused_computation.1 | custom fusion | bytes 6297600 | tf_op jit(solution)/shard_map/gather | solution.py:95
  70.6 9.3 %all-to-all-start.1 = ((bf16[1536,8,128]{2,1,0:T(8,128)(2,1)}), bf16[1536,8,128]{2,1,0:T(8,128)(2,1)}, u32[]{:S(2)}, u32[]{:S(2)}) async-start(bf16[1536,8,128]{2,1,0:T(8,128)(2,1)} %gather_fusion.1), calls=%async_computation.1 | async-start | bytes 6291456 | tf_op jit(solution)/shard_map/all_to_all | solution.py:95
  79.9 5.5 %gather_fusion.3 = bf16[1536,8,128]{2,1,0:T(8,128)(2,1)} fusion(bf16[1024,8,128]{2,1,0:T(8,128)(2,1)} %param.11, s32[2048]{0:T(1024)S(1)} %pad_clamp_fusion), kind=kCustom, calls=%fused_computation.3 | custom fusion | bytes 6297600 | tf_op jit(solution)/shard_map/gather | solution.py:97
  85.4 65.3 %all-to-all-done.1 = bf16[1536,8,128]{2,1,0:T(8,128)(2,1)} async-done(((bf16[1536,8,128]{2,1,0:T(8,128)(2,1)}), bf16[1536,8,128]{2,1,0:T(8,128)(2,1)}, u32[]{:S(2)}, u32[]{:S(2)}) %all-to-all-start.1) | async-done | bytes 3145760 | tf_op jit(solution)/shard_map/all_to_all | solution.py:95
  150.7 6.8 %all-to-all-start.2 = ((bf16[1536,8,128]{2,1,0:T(8,128)(2,1)}), bf16[1536,8,128]{2,1,0:T(8,128)(2,1)}, u32[]{:S(2)}, u32[]{:S(2)}) async-start(bf16[1536,8,128]{2,1,0:T(8,128)(2,1)} %gather_fusion.3), calls=%async_computation.2 | async-start | bytes 6291456 | tf_op jit(solution)/shard_map/all_to_all | solution.py:96
  157.8 2.2 multiply_reduce_fusion.2
  160.0 1.3 fusion.21
  161.3 0.9 slice_bitcast_fusion.3
  162.2 0.5 broadcast.234
  162.8 0.7 reduce.17
  163.6 3.2 gather_fusion
  167.0 4.1 %gather_fusion.2 = bf16[1536,128]{1,0:T(8,128)(2,1)} fusion(bf16[1024,128]{1,0:T(8,128)(2,1)S(1)} %get-tuple-element.17, s32[2048]{0:T(1024)S(1)} %pad_clamp_fusion.1), kind=kCustom, calls=%fused_computation.2 | custom fusion | bytes 792576 | tf_op jit(solution)/shard_map/gather | solution.py:92
  171.1 1.2 copy.41
  172.2 4.1 %gather_fusion.4 = bf16[1536,128]{1,0:T(8,128)(2,1)} fusion(bf16[1024,128]{1,0:T(8,128)(2,1)S(1)} %get-tuple-element.16, s32[2048]{0:T(1024)S(1)} %pad_clamp_fusion.1), kind=kCustom, calls=%fused_computation.4 | custom fusion | bytes 792576 | tf_op jit(solution)/shard_map/gather | solution.py:93
  176.3 2.1 copy.43
  178.5 1.0 bitcast_convert_fusion
  179.5 5.1 %copy.61 = bf16[1536,8,128]{0,2,1:T(8,128)(2,1)} copy(bf16[1536,8,128]{2,1,0:T(8,128)(2,1)} %all-to-all-done.1) | data formatting | bytes 6291456
  184.6 2.7 multiply_reduce_fusion.1
  187.7 39.4 %all-to-all-done.2 = bf16[1536,8,128]{2,1,0:T(8,128)(2,1)} async-done(((bf16[1536,8,128]{2,1,0:T(8,128)(2,1)}), bf16[1536,8,128]{2,1,0:T(8,128)(2,1)}, u32[]{:S(2)}, u32[]{:S(2)}) %all-to-all-start.2) | async-done | bytes 3145760 | tf_op jit(solution)/shard_map/all_to_all | solution.py:96
  227.0 5.0 %copy.63 = bf16[1536,8,128]{0,2,1:T(8,128)(2,1)} copy(bf16[1536,8,128]{2,1,0:T(8,128)(2,1)} %all-to-all-done.2) | data formatting | bytes 6291456
  232.0 2.7 multiply_reduce_fusion
  235.1 4.5 %scatter_custom_fusion.2 = bf16[1024,128]{1,0:T(8,128)(2,1)S(1)} fusion(s32[1536]{0:T(1024)S(1)} %get-tuple-element.11, bf16[1536,128]{1,0:T(8,128)(2,1)S(1)} %copy.44, bf16[]{:T(256)} %constant.27.clone.1), kind=kCustom, calls=%fused_computation.54 | custom fusion | bytes 262146 | tf_op jit(solution)/shard_map/scatter | solution.py:103
  239.6 2.0 convolution_convert_fusion.1
  241.6 3.9 %copy.64 = bf16[1024,1024]{0,1:T(8,128)(2,1)} copy(bf16[1024,1024]{1,0:T(8,128)(2,1)} %convolution_convert_fusion.1) | data formatting | bytes 4194304
  245.7 4.0 %convert_element_type.56 = f32[1024,1024]{1,0:T(8,128)} convert(bf16[1024,1024]{1,0:T(8,128)(2,1)} %param.9) | non-fusion elementwise | flops 1048576 | bytes 6291456 | tf_op jit(solution)/shard_map/convert_element_type | solution.py:79
  249.6 30.5 %reduce-scatter.7.cloned.1.call-done = bf16[128,1024]{1,0:T(8,128)(2,1)} async-done(((bf16[1024,1024]{1,0:T(8,128)(2,1)}), bf16[128,1024]{1,0:T(8,128)(2,1)}) %reduce-scatter.7.cloned.1.call-update) | async-done | bytes 262160
  280.2 1.1 copy.65
  281.3 1.8 add_convert_fusion.2
  283.4 31.5 %all-gather.2.cloned.1.call-done = bf16[1024,1024]{1,0:T(8,128)(2,1)} async-done(((bf16[1024,128]{1,0:T(8,128)(2,1)}), bf16[1024,1024]{1,0:T(8,128)(2,1)}) %all-gather.2.cloned.1.call-update) | async-done | bytes 2097168 | tf_op jit(solution)/shard_map/all_gather | solution.py:116
  314.9 2.1 fusion
  317.0 5.8 %convolution_convert_fusion = bf16[1024,1024]{1,0:T(8,128)(2,1)} fusion(bf16[512,1024]{1,0:T(8,128)(2,1)S(1)} %copy-done.8, bf16[1024,512]{1,0:T(8,128)(2,1)} %param.16, bf16[1024,1024]{1,0:T(8,128)(2,1)} %all-gather.2.cloned.1.call-done, f32[1024]{0:T(1024)S(1)} %add_rsqrt_fusion), kind=kOutput, calls=%fused_computation.31 | convolution fusion | flops 2156396544 | bytes 6295552 | tf_op jit(solution)/shard_map/dot_general | solution.py:121
  322.8 4.0 %copy.66 = bf16[1024,1024]{0,1:T(8,128)(2,1)} copy(bf16[1024,1024]{1,0:T(8,128)(2,1)} %convolution_convert_fusion) | data formatting | bytes 4194304
  326.8 0.9 copy-done.5
  327.8 1.3 copy.45
  329.2 31.9 %reduce-scatter.9.cloned.1.call-done = bf16[128,1024]{1,0:T(8,128)(2,1)} async-done(((bf16[1024,1024]{1,0:T(8,128)(2,1)}), bf16[128,1024]{1,0:T(8,128)(2,1)}) %reduce-scatter.9.cloned.1.call-update) | async-done | bytes 262160
  361.1 1.1 copy.67
  362.2 0.8 add_convert_fusion.1
  (58 shorter events, 4.1 us)
Async XLA Ops:
  7.2 58.4 %copy-start = (bf16[1024,8,128]{2,1,0:T(8,128)(2,1)S(1)}, bf16[1024,8,128]{2,1,0:T(8,128)(2,1)}, u32[]{:S(2)}) copy-start(bf16[1024,8,128]{2,1,0:T(8,128)(2,1)} %param.10) | copy-start | bytes 6291460
  37.7 32.9 %all-to-all-start = ((s32[32,48,1]{1,2,0:T(1,128)}), s32[32,48,1]{1,2,0:T(1,128)S(1)}, u32[]{:S(2)}, u32[]{:S(2)}) async-start(s32[32,48,1]{1,2,0:T(1,128)} %bitcast.5), calls=%async_computation | async-start | bytes 32768 | tf_op jit(solution)/shard_map/all_to_all | solution.py:89
  70.6 80.1 %all-to-all-start.1 = ((bf16[1536,8,128]{2,1,0:T(8,128)(2,1)}), bf16[1536,8,128]{2,1,0:T(8,128)(2,1)}, u32[]{:S(2)}, u32[]{:S(2)}) async-start(bf16[1536,8,128]{2,1,0:T(8,128)(2,1)} %gather_fusion.1), calls=%async_computation.1 | async-start | bytes 6291456 | tf_op jit(solution)/shard_map/all_to_all | solution.py:95
  150.7 9.3 %copy-start.9 = (bf16[3,1024,128]{2,1,0:T(8,128)(2,1)S(1)}, bf16[3,1024,128]{2,1,0:T(8,128)(2,1)}, u32[]{:S(2)}) copy-start(bf16[3,1024,128]{2,1,0:T(8,128)(2,1)} %param.14) | copy-start | bytes 2359300
  150.7 76.4 %all-to-all-start.2 = ((bf16[1536,8,128]{2,1,0:T(8,128)(2,1)}), bf16[1536,8,128]{2,1,0:T(8,128)(2,1)}, u32[]{:S(2)}, u32[]{:S(2)}) async-start(bf16[1536,8,128]{2,1,0:T(8,128)(2,1)} %gather_fusion.3), calls=%async_computation.2 | async-start | bytes 6291456 | tf_op jit(solution)/shard_map/all_to_all | solution.py:96
  157.5 122.7 %reduce-scatter.7.cloned.1.call-start = ((), (), s32[]{:S(2)}) async-start(), calls=%async_computation.6 | async-start | bytes 2359296
  157.7 2.3 copy-start.1
  179.5 5.1 %copy-start.3 = (f32[1536,2,64]{0,2,1:T(8,128)S(1)}, f32[1536,2,64]{0,2,1:T(8,128)}, u32[]{:S(2)}) copy-start(f32[1536,2,64]{0,2,1:T(8,128)} %bitcast_convert_fusion) | copy-start | bytes 2359300
  232.0 2.7 copy-start.2
  234.7 4.9 %copy-start.7 = (bf16[128,1024]{1,0:T(8,128)(2,1)S(1)}, bf16[128,1024]{1,0:T(8,128)(2,1)}, u32[]{:S(2)}) copy-start(bf16[128,1024]{1,0:T(8,128)(2,1)} %param.15) | copy-start | bytes 786436
  245.6 69.3 %all-gather.2.cloned.1.call-start = ((), (), s32[]{:S(2)}) async-start(), calls=%async_computation.5 | async-start | bytes 2359296 | tf_op jit(solution)/shard_map/all_gather | solution.py:116
  249.6 67.4 %copy-start.8 = (bf16[512,1024]{1,0:T(8,128)(2,1)S(1)}, bf16[512,1024]{1,0:T(8,128)(2,1)}, u32[]{:S(2)}) copy-start(bf16[512,1024]{1,0:T(8,128)(2,1)} %param.17) | copy-start | bytes 3145732
  283.1 77.9 %reduce-scatter.9.cloned.1.call-start = ((), (), s32[]{:S(2)}) async-start(), calls=%async_computation.7 | async-start | bytes 2359296
  326.8 0.9 copy-start.5
  326.8 1.0 copy-start.6
  326.8 35.4 %copy-start.4 = (bf16[1024,128]{1,0:T(8,128)(2,1)S(1)}, bf16[1024,128]{1,0:T(8,128)(2,1)}, u32[]{:S(2)}) copy-start(bf16[1024,128]{1,0:T(8,128)(2,1)} %add_convert_fusion.2) | copy-start | bytes 786436
Sparse Core Ops, SparseCore 0:
  245.7 34.4 reduce-scatter.6
  283.2 31.6 all-gather.1
  326.9 34.1 reduce-scatter.8
where the time goes:
time: 372 us; the launch traced here: 369 us
  waiting for transfers between devices  199 us (53%)
  local copies, waits for them, and re-layouts  89.3 us (24%)
  other arithmetic  29.5 us (8%)
  starting transfers between devices  28.7 us (8%)
  between operations  14.2 us (4%)
  matrix products  9.14 us (2%)
    all_to_all x1, waiting for transfers between devices, body(): lax.all_to_all(cache_keys[send_parent], 'sample', split_axis=0, concat_ax...  65.3 us
    unnamed x5, waiting for transfers between devices  62.5 us
    all_to_all x1, waiting for transfers between devices, body(): lax.all_to_all(cache_values[send_parent], 'sample', split_axis=0, concat_...  39.4 us
    all_gather x1, waiting for transfers between devices, body(): hidden = lax.all_gather(hidden_part, 'head', axis=1, tiled=True)  31.5 us
    unnamed x27, local copies, waits for them, and re-layouts  22.6 us
    scatter x1, local copies, waits for them, and re-layouts, send_plan(): jnp.full((peer_count * capacity,), -1, jnp.int32).at[position]  15.5 us
    scatter x1, local copies, waits for them, and re-layouts, send_plan(): jnp.zeros((peer_count * capacity,), jnp.int32).at[position]  15.5 us
    all_to_all x1, starting transfers between devices, body(): lax.all_to_all(send_slot, 'sample', split_axis=0, concat_axis=0, tiled=True)  12 us
  transfers between devices with their start and end apart: 6, of which 5 were waited for; matrix products, arithmetic and copies ran while one was open for 17% of the time, Pallas kernels for 0%

commit v1 on v0

v1 whole, which is shorter than its diff:
```python
import functools

import jax
import jax.numpy as jnp
from jax import lax
from jax.experimental import pallas as pl
from jax.experimental.pallas import tpu as pltpu
from jax.sharding import Mesh, PartitionSpec as P

HD = 64
PEERS = 32
CAP = 48
ROWS = 1024
ITEMS = PEERS * CAP
MSG = 64
SAMPLE = ("z", "y")
HEAD = ("x", "core")
VLIM = 48 * 1024 * 1024
F32 = jnp.float32
BF = jnp.bfloat16
NT = (((1,), (1,)), ((), ()))
TN = (((0,), (0,)), ((), ()))


def iota(shape, dim):
    return lax.broadcasted_iota(jnp.int32, shape, dim)


def call(kernel, out, cost, **kw):
    return pl.pallas_call(
        kernel,
        out_shape=out,
        compiler_params=pltpu.CompilerParams(vmem_limit_bytes=VLIM),
        cost_estimate=pl.CostEstimate(flops=cost[0], bytes_accessed=cost[1], transcendentals=0),
        **kw,
    )


def sds(shape, dtype):
    return jax.ShapeDtypeStruct(shape, dtype)


def plan_kernel(cnt_ref, slot_ref, send_ref, par_ref):
    width = 256
    blocks = ROWS // width
    cnt = cnt_ref[...]
    tri = (iota((width, width), 0) <= iota((width, width), 1)).astype(F32).astype(BF)
    ow = iota((PEERS, width), 0)
    groups = []
    for k in range(4):
        for b in range(blocks):
            sl = slot_ref[k : k + 1, b * width : (b + 1) * width]
            live = cnt[:, b * width : (b + 1) * width] > k
            owner = jnp.where(live, sl // ROWS, -1)
            member = (ow == owner).astype(F32)
            groups.append((sl, live, member, b))
    stacked = jnp.concatenate([g[2].astype(BF) for g in groups], axis=0)
    inc = jnp.dot(stacked, tri, preferred_element_type=F32)
    base = jnp.zeros((PEERS, 1), F32)
    total = jnp.zeros((5 * PEERS, CAP), F32)
    parent = iota((1, width), 1)
    for g, (sl, live, member, b) in enumerate(groups):
        run = inc[g * PEERS : (g + 1) * PEERS]
        rank = jnp.sum(member * (run + (base - 1.0)), axis=0, keepdims=True)
        base = base + run[:, width - 1 : width]
        rank = jnp.where(live, rank.astype(jnp.int32), -1)
        place = (iota((CAP, width), 0) == rank).astype(F32).astype(BF)
        local = sl % ROWS
        par = parent + b * width
        left = jnp.concatenate(
            [
                member * (local // 32).astype(F32),
                member * (local % 32).astype(F32),
                member,
                member * (par // 32).astype(F32),
                member * (par % 32).astype(F32),
            ],
            axis=0,
        ).astype(BF)
        total = total + lax.dot_general(left, place, NT, preferred_element_type=F32)
    whole = total.astype(jnp.int32)
    have = whole[2 * PEERS : 3 * PEERS] > 0
    send = jnp.where(have, whole[:PEERS] * 32 + whole[PEERS : 2 * PEERS], -1)
    pars = jnp.where(have, whole[3 * PEERS : 4 * PEERS] * 32 + whole[4 * PEERS :], -1)
    fill = jnp.full((PEERS, 128 - CAP), -1, jnp.int32)
    send_ref[...] = jnp.concatenate([send, fill], axis=1)
    par_ref[...] = jnp.concatenate([pars, fill], axis=1)


def column(lists, count, depth):
    shape = (count, depth, 128)
    picked = jnp.where(
        iota(shape, 1) == iota(shape, 2), jnp.broadcast_to(lists[:, None, :], shape), 0.0
    )
    return jnp.sum(picked, axis=2, keepdims=True).reshape(count * depth, 1)


def expand_kernel(par_ref, k_ref, v_ref, out_ref):
    peers = par_ref.shape[0]
    col = column(par_ref[...].astype(F32), peers, CAP)
    hot = (col == iota((peers * CAP, ROWS), 1).astype(F32)).astype(F32).astype(BF)
    out_ref[:, :ROWS] = jnp.dot(hot, k_ref[...], preferred_element_type=F32).astype(BF)
    out_ref[:, ROWS:] = jnp.dot(hot, v_ref[...], preferred_element_type=F32).astype(BF)


def query_kernel(recv_ref, q_ref, out_ref):
    peers = recv_ref.shape[0]
    col = column(recv_ref[...].astype(F32), peers, CAP)
    hot = (col == iota((peers * CAP, ROWS), 1).astype(F32)).astype(F32).astype(BF)
    out_ref[...] = jnp.dot(hot, q_ref[...], preferred_element_type=F32).astype(BF)


def place_kernel(recv_ref, q_ref, k_ref, back_ref, src_ref, mask_ref, own_ref):
    slot = recv_ref[...]
    high = jnp.where(slot >= 0, slot // 32, -1)
    low = slot % 32
    acc = jnp.zeros((64, 32), F32)
    where_c = iota((32, 128), 1).astype(F32)
    for s in range(PEERS):
        a = (iota((32, 128), 0) == high[s : s + 1, :]).astype(F32)
        b = (iota((32, 128), 0) == low[s : s + 1, :]).astype(F32).astype(BF)
        left = jnp.concatenate([a * float(s), a * where_c], axis=0).astype(BF)
        acc = acc + lax.dot_general(left, b, NT, preferred_element_type=F32)
    wide = jnp.concatenate([acc, jnp.zeros((64, 96), F32)], axis=1)
    src = column(wide[:32], 32, 32)
    place = column(wide[32:], 32, 32)
    pos = src * float(CAP) + place
    lane = iota((ROWS, 128), 1).astype(F32)
    src_ref[...] = (lane == src).astype(F32).astype(BF)
    mask_ref[...] = (lane == place).astype(F32)
    for t in range(ITEMS // 256):
        items = (iota((ROWS, 256), 1) + t * 256).astype(F32)
        back_ref[:, t * 256 : (t + 1) * 256] = (items == pos).astype(F32).astype(BF)
    prod = q_ref[...].astype(F32) * k_ref[...].astype(F32) * (1.0 / HD**0.5)
    s0 = jnp.sum(prod[:, :HD], axis=1, keepdims=True)
    s1 = jnp.sum(prod[:, HD:], axis=1, keepdims=True)
    own_ref[...] = jnp.where(iota((ROWS, 128), 1) < HD, s0, s1)


def attend_kernel(q_ref, kv_ref, out_ref):
    n = q_ref.shape[0]
    peers = n // CAP
    sel_p = iota((16, ROWS), 1) // 128
    sel_h = (iota((16, ROWS), 1) % 128) // HD
    sel = (iota((16, ROWS), 0) == sel_h * 8 + sel_p).astype(F32).astype(BF)
    q = q_ref[...].astype(F32)
    highs, lows = [], []
    for p in range(8):
        prod = q * kv_ref[:, p * 128 : (p + 1) * 128].astype(F32)
        high = prod.astype(BF)
        highs.append(high)
        lows.append((prod - high.astype(F32)).astype(BF))
    score = lax.dot_general(sel, jnp.concatenate(highs, axis=1), NT, preferred_element_type=F32)
    score = score + lax.dot_general(
        sel, jnp.concatenate(lows, axis=1), NT, preferred_element_type=F32
    )
    score = score * (1.0 / HD**0.5)
    weights, rows = [], []
    for h in range(2):
        part = score[h * 8 : (h + 1) * 8]
        top = jnp.max(part, axis=0, keepdims=True)
        expo = jnp.exp(part - top)
        norm = jnp.sum(expo, axis=0, keepdims=True)
        weights.append(expo / norm)
        lse = top + jnp.log(norm)
        for _ in range(3):
            piece = lse.astype(BF).astype(F32)
            rows.append(piece)
            lse = lse - piece
    weight = jnp.concatenate(weights, axis=0).astype(BF)
    wide = lax.dot_general(weight, sel, TN, preferred_element_type=F32)
    ctx = wide[:, :128] * kv_ref[:, ROWS : ROWS + 128].astype(F32)
    for p in range(1, 8):
        ctx = ctx + wide[:, p * 128 : (p + 1) * 128] * kv_ref[
            :, ROWS + p * 128 : ROWS + (p + 1) * 128
        ].astype(F32)
    out_ref[:, :CAP, :] = ctx.astype(BF).reshape(peers, CAP, 128)
    tail = jnp.concatenate(rows + [jnp.zeros((10, n), F32)], axis=0)
    for o in range(peers):
        piece = tail[:, o * CAP : (o + 1) * CAP]
        piece = jnp.concatenate([piece, jnp.zeros((16, 128 - CAP), F32)], axis=1)
        out_ref[o, CAP:, :] = piece.astype(BF)


def merge_kernel(msg_ref, back_ref, src_ref, mask_ref, own_ref, v_ref, out_ref):
    rows = back_ref.shape[0]
    ctx = msg_ref[:, :CAP, :].reshape(ITEMS, 128)
    ctx = jnp.dot(back_ref[...], ctx, preferred_element_type=F32)
    cols = []
    src = src_ref[:, :PEERS]
    for h in range(2):
        lse = jnp.zeros((rows, 128), F32)
        for j in range(3):
            part = msg_ref[:, CAP + h * 3 + j, :].reshape(PEERS, 128)
            lse = lse + jnp.dot(src, part, preferred_element_type=F32)
        cols.append(jnp.sum(lse * mask_ref[...], axis=1, keepdims=True))
    lse = jnp.where(iota((rows, 128), 1) < HD, cols[0], cols[1])
    own = own_ref[...]
    top = jnp.maximum(lse, own)
    a = jnp.exp(lse - top)
    b = jnp.exp(own - top)
    out_ref[...] = ((a * ctx + b * v_ref[...].astype(F32)) / (a + b)).astype(BF)


def ffn_kernel(head_ref, *refs):
    pieces = refs[:8]
    x_ref, wo_ref, wu_ref, wd_ref = refs[8:12]
    same_ref, other_ref, part_ref = refs[12:15]
    att, hid, down = refs[15:18]
    for i in range(8):
        at = pl.multiple_of(head_ref[i] * 128, 128)
        att[:, pl.ds(at, 128)] = pieces[i][...]
    x = x_ref[...].astype(F32)
    hidden = (x + jnp.dot(att[...], wo_ref[...], preferred_element_type=F32)).astype(BF)
    hid[...] = hidden
    hf = hidden.astype(F32)
    scale = lax.rsqrt(jnp.mean(hf * hf, axis=-1, keepdims=True) + 1e-05)
    normed = (hf * scale).astype(BF)
    up = jnp.dot(normed, wu_ref[...], preferred_element_type=F32)
    act = jax.nn.gelu(up).astype(BF)
    down[...] = jnp.dot(act, wd_ref[...], preferred_element_type=F32).astype(BF)
    part_ref[...] = hid[:, pl.ds(pl.multiple_of(head_ref[0] * 128, 128), 128)]
    for i in range(4):
        at = pl.multiple_of(head_ref[i] * 128, 128)
        same_ref[i] = down[:, pl.ds(at, 128)]
        at = pl.multiple_of(head_ref[4 + i] * 128, 128)
        other_ref[i] = down[:, pl.ds(at, 128)]


def shift(x, axis, by, size):
    return lax.ppermute(x, axis, [(i, (i + by) % size) for i in range(size)])


def rms_rows(stream):
    return stream * lax.rsqrt(jnp.mean(stream * stream, axis=-1, keepdims=True) + 1e-05)


def body(stream_in, keys, values, counts, slots, w_qkv, w_out, w_up, w_down):
    wo_full = lax.all_gather(w_out, HEAD, axis=0, tiled=True)
    send, par = call(
        plan_kernel,
        (sds((PEERS, 128), jnp.int32), sds((PEERS, 128), jnp.int32)),
        (4 * 10**8, 10**6),
    )(counts.reshape(1, ROWS), slots.T)
    recv = lax.all_to_all(
        send.reshape(PEERS, 1, 128), SAMPLE, split_axis=0, concat_axis=0, tiled=True
    ).reshape(PEERS, 128)

    stream = stream_in.astype(F32)
    normed = rms_rows(stream).astype(BF)
    projected = jnp.einsum("rd,tdc->trc", normed, w_qkv, preferred_element_type=F32).astype(BF)
    query, own_key, own_value = projected[0], projected[1], projected[2]
    new_kv = jnp.stack([own_key, own_value], axis=1)

    kv = call(
        expand_kernel,
        sds((ITEMS, 2 * ROWS), BF),
        (2 * ITEMS * ROWS * ROWS * 2, 12 * 10**6),
        grid=(4,),
        in_specs=[
            pl.BlockSpec((8, 128), lambda i: (i, 0)),
            pl.BlockSpec((ROWS, ROWS), lambda i: (0, 0)),
            pl.BlockSpec((ROWS, ROWS), lambda i: (0, 0)),
        ],
        out_specs=pl.BlockSpec((8 * CAP, 2 * ROWS), lambda i: (i, 0)),
    )(par, keys.reshape(ROWS, ROWS), values.reshape(ROWS, ROWS))

    q_send = call(
        query_kernel,
        sds((ITEMS, 128), BF),
        (2 * ITEMS * ROWS * 128, 10**6),
        grid=(4,),
        in_specs=[
            pl.BlockSpec((8, 128), lambda i: (i, 0)),
            pl.BlockSpec((ROWS, 128), lambda i: (0, 0)),
        ],
        out_specs=pl.BlockSpec((8 * CAP, 128), lambda i: (i, 0)),
    )(recv, query)
    q_recv = lax.all_to_all(q_send, SAMPLE, split_axis=0, concat_axis=0, tiled=True)

    back, src, mask, own = call(
        place_kernel,
        (
            sds((ROWS, ITEMS), BF),
            sds((ROWS, 128), BF),
            sds((ROWS, 128), F32),
            sds((ROWS, 128), F32),
        ),
        (10**9, 6 * 10**6),
    )(recv, query, own_key)

    msg = call(
        attend_kernel,
        sds((PEERS, MSG, 128), BF),
        (2 * ITEMS * ROWS * 128, 8 * 10**6),
        grid=(4,),
        in_specs=[
            pl.BlockSpec((8 * CAP, 128), lambda i: (i, 0)),
            pl.BlockSpec((8 * CAP, 2 * ROWS), lambda i: (i, 0)),
        ],
        out_specs=pl.BlockSpec((8, MSG, 128), lambda i: (i, 0, 0)),
    )(q_recv, kv)
    answer = lax.all_to_all(msg, SAMPLE, split_axis=0, concat_axis=0, tiled=True)

    whole = lambda *shape: pl.BlockSpec(shape, lambda i: (0,) * len(shape))
    attended = call(
        merge_kernel,
        sds((ROWS, 128), BF),
        (2 * ITEMS * ROWS * 128, 5 * 10**6),
        grid=(4,),
        in_specs=[
            whole(PEERS, MSG, 128),
            pl.BlockSpec((256, ITEMS), lambda i: (i, 0)),
            pl.BlockSpec((256, 128), lambda i: (i, 0)),
            pl.BlockSpec((256, 128), lambda i: (i, 0)),
            pl.BlockSpec((256, 128), lambda i: (i, 0)),
            pl.BlockSpec((256, 128), lambda i: (i, 0)),
        ],
        out_specs=pl.BlockSpec((256, 128), lambda i: (i, 0)),
    )(answer, back, src, mask, own, own_value)

    near = [attended] + [shift(attended, "x", d, 4) for d in (1, 3, 2)]
    far = [shift(piece, "core", 1, 2) for piece in near]
    x = lax.axis_index("x")
    core = lax.axis_index("core")
    xs = jnp.stack([x, (x + 3) % 4, (x + 1) % 4, (x + 2) % 4])
    heads = jnp.concatenate([xs * 2 + core, xs * 2 + 1 - core]).astype(jnp.int32)

    rows = lambda *shape: pl.BlockSpec(shape, lambda i, h: (i,) + (0,) * (len(shape) - 1))
    fixed = lambda *shape: pl.BlockSpec(shape, lambda i, h: (0,) * len(shape))
    blocks = lambda: pl.BlockSpec((4, 256, 128), lambda i, h: (0, i, 0))
    same, other, hidden_part = call(
        ffn_kernel,
        (sds((4, ROWS, 128), BF), sds((4, ROWS, 128), BF), sds((ROWS, 128), BF)),
        (4 * 10**9, 12 * 10**6),
        grid_spec=pltpu.PrefetchScalarGridSpec(
            num_scalar_prefetch=1,
            grid=(4,),
            in_specs=[rows(256, 128)] * 8
            + [rows(256, ROWS), fixed(ROWS, ROWS), fixed(ROWS, 512), fixed(512, ROWS)],
            out_specs=(blocks(), blocks(), rows(256, 128)),
            scratch_shapes=[
                pltpu.VMEM((256, ROWS), BF),
                pltpu.VMEM((256, ROWS), BF),
                pltpu.VMEM((256, ROWS), BF),
            ],
        ),
    )(heads, *near, *far, stream_in, wo_full, w_up, w_down)

    swapped = shift(other, "core", 1, 2)
    pair = same.astype(F32) + swapped.astype(F32)
    sums = pair.astype(BF)
    got = [shift(sums[1], "x", 3, 4), shift(sums[2], "x", 1, 4), shift(sums[3], "x", 2, 4)]
    total = pair[0] + got[0].astype(F32) + got[1].astype(F32) + got[2].astype(F32)
    layer_out = (hidden_part.astype(F32) + total).astype(BF)
    return (layer_out, new_kv)


def solution(mesh):
    grid = Mesh(mesh.devices.reshape(8, 4, 4, 2), ("z", "y", "x", "core"))
    in_specs = (
        P(SAMPLE, None),
        P(SAMPLE, None, HEAD),
        P(SAMPLE, None, HEAD),
        P(SAMPLE),
        P(SAMPLE, None),
        P(None, None, HEAD),
        P(HEAD, None),
        P(None, HEAD),
        P(HEAD, None),
    )
    out_specs = (P(SAMPLE, HEAD), P(SAMPLE, None, HEAD))
    return jax.shard_map(body, mesh=grid, in_specs=in_specs, out_specs=out_specs, check_vma=False)
```

time: 372 us -> 144 us (0.39)
  waiting for transfers between devices: 199 us -> 30.6 us
  local copies, waits for them, and re-layouts: 89.3 us -> 12.1 us
  Pallas kernels: 0 us -> 34.8 us
  other arithmetic: 29.5 us -> 3.42 us
  starting transfers between devices: 28.7 us -> 46.9 us
  matrix products: 9.14 us -> 1.29 us
    all_to_all x3, waiting for transfers between devices: 105 us -> 16 us  [the longest x1 11.8 us: body(): lax.all_to_all(msg, SAMPLE, split_axis=0, concat_axis=0, tiled=True)]
    unnamed x5 -> x1, waiting for transfers between devices: 62.5 us -> 0.68 us
    scatter x3 -> x0, local copies, waits for them, and re-layouts: 35.5 us -> none  [the longest x1 15.5 us: send_plan(): jnp.full((peer_count * capacity,), -1, jnp.int32).at[position]]
    pallas_call x0 -> x7, Pallas kernels: none -> 34.8 us  [the longest x1 10.7 us: body(): call(ffn_kernel, (sds((4, ROWS, 128), BF), sds((4, ROWS, 128), BF), sds((...]
    all_gather x1, waiting for transfers between devices: 31.5 us -> 0.01 us  [body(): wo_full = lax.all_gather(w_out, HEAD, axis=0, tiled=True)]
    gather x7 -> x0, local copies, waits for them, and re-layouts: 23.1 us -> none  [the longest x1 5.47 us: body(): cache_values[send_parent]]
    ppermute x0 -> x11, starting transfers between devices: none -> 20.4 us  [shift(): return lax.ppermute(x, axis, [(i, (i + by) % size) for i in range(size)])]
    unnamed x27 -> x19, local copies, waits for them, and re-layouts: 22.6 us -> 7.56 us
  transfers between devices with their start and end apart: 6 -> 15, of which waited for: 5 -> 7; matrix products, arithmetic and copies ran while one was open for 17% -> 7% of each run, Pallas kernels for 0% -> 16%
where the time goes in v1:
time: 144 us; the launch traced here: 143 us
  starting transfers between devices  46.9 us (33%)
  Pallas kernels  34.8 us (24%)
  waiting for transfers between devices  30.6 us (21%)
  between operations  14.2 us (10%)
  local copies, waits for them, and re-layouts  12.1 us (8%)
  other arithmetic  3.42 us (2%)
    ppermute x11, starting transfers between devices, shift(): return lax.ppermute(x, axis, [(i, (i + by) % size) for i in range(size)])  20.4 us
    ppermute x11, waiting for transfers between devices, shift(): return lax.ppermute(x, axis, [(i, (i + by) % size) for i in range(size)])  14 us
    all_to_all x1, starting transfers between devices, body(): lax.all_to_all(send.reshape(PEERS, 1, 128), SAMPLE, split_axis=0, concat_...  12 us
    all_to_all x1, waiting for transfers between devices, body(): lax.all_to_all(msg, SAMPLE, split_axis=0, concat_axis=0, tiled=True)  11.8 us
    pallas_call x1, Pallas kernels, body(): call(ffn_kernel, (sds((4, ROWS, 128), BF), sds((4, ROWS, 128), BF), sds((...  10.7 us
    pallas_call x1, Pallas kernels, body(): call(expand_kernel, sds((ITEMS, 2 * ROWS), BF), (2 * ITEMS * ROWS * ROWS...  8.69 us
    all_to_all x1, starting transfers between devices, body(): lax.all_to_all(msg, SAMPLE, split_axis=0, concat_axis=0, tiled=True)  8.57 us
    unnamed x19, local copies, waits for them, and re-layouts  7.56 us
  transfers between devices with their start and end apart: 15, of which 7 were waited for; matrix products, arithmetic and copies ran while one was open for 7% of the time, Pallas kernels for 16%

profile of v1, /device:TPU:1, one launch (start us, length us, event | category | flops | bytes accessed | tf_op | source)
XLA Modules:
  0.0 143.3 jit_solution(4341532428158027150)
XLA Ops:
  7.2 0.0 copy-start
  7.2 0.8 copy-done.4
  8.0 0.7 copy-done.5
  8.7 1.5 %shard_map.104 = (s32[32,128]{1,0:T(8,128)}, s32[32,128]{1,0:T(8,128)S(1)}) custom-call(s32[1,1024]{1,0:T(1,128)S(1)} %bitcast.60, s32[4,1024]{1,0:T(4,128)S(1)} %bitcast.59), custom_call_target="tpu_custom_call" | custom-call | flops 400000000 | bytes 1000000 | tf_op jit(solution)/shard_map/pallas_call | solution.py:240
  10.1 12.0 %all-to-all-start = ((s32[32,1,128]{2,1,0:T(1,128)}), s32[32,1,128]{2,1,0:T(1,128)S(1)}, u32[]{:S(2)}, u32[]{:S(2)}) async-start(s32[32,1,128]{2,1,0:T(1,128)} %bitcast.7), calls=%async_computation | async-start | bytes 32768 | tf_op jit(solution)/shard_map/all_to_all | solution.py:245
  22.2 0.0 all-gather.2.cloned.1.call-start
  22.2 0.7 all-gather.2.cloned.1.call-update
  22.9 2.1 %fusion = f32[1024]{0:T(1024)S(1)} fusion(bf16[1024,1024]{1,0:T(8,128)(2,1)} %refs_8_.1), kind=kLoop, calls=%fused_computation.2 | loop fusion | flops 3144704 | bytes 2101248 | tf_op jit(solution)/shard_map/reduce_sum | solution.py:235
  25.0 1.3 fusion.9
  26.3 1.0 slice_bitcast_fusion.7
  27.3 3.4 %all-to-all-done = s32[32,1,128]{2,1,0:T(1,128)S(1)} async-done(((s32[32,1,128]{2,1,0:T(1,128)}), s32[32,1,128]{2,1,0:T(1,128)S(1)}, u32[]{:S(2)}, u32[]{:S(2)}) %all-to-all-start) | async-done | bytes 16416 | tf_op jit(solution)/shard_map/all_to_all | solution.py:245
  30.7 2.6 %shard_map.105 = bf16[1536,128]{1,0:T(8,128)(2,1)} custom-call(s32[32,128]{1,0:T(8,128)S(1)} %bitcast.57, bf16[1024,128]{1,0:T(8,128)(2,1)S(1)} %get-tuple-element.35.q_ref), custom_call_target="tpu_custom_call" | custom-call | flops 402653184 | bytes 1000000 | tf_op jit(solution)/shard_map/pallas_call | solution.py:268
  33.3 5.8 %all-to-all-start.1 = ((bf16[32,48,128]{2,1,0:T(8,128)(2,1)}), bf16[32,48,128]{2,1,0:T(8,128)(2,1)S(1)}, u32[]{:S(2)}, u32[]{:S(2)}) async-start(bf16[32,48,128]{2,1,0:T(8,128)(2,1)} %bitcast.12), calls=%async_computation.1 | async-start | bytes 786432 | tf_op jit(solution)/shard_map/all_to_all | solution.py:279
  39.2 3.6 %copy_bitcast_fusion = (bf16[1024,1024]{1,0:T(8,128)(2,1)S(1)}, bf16[1024,1024]{1,0:T(8,128)(2,1)S(1)}) fusion(bf16[128,8,8,128]{3,2,1,0:T(8,128)(2,1)} %bitcast.61, bf16[128,8,8,128]{3,2,1,0:T(8,128)(2,1)} %bitcast.62), kind=kLoop, calls=%fused_computation.6 | loop fusion | bytes 8388608 | tf_op jit(solution)/shard_map/reshape | solution.py:266
  42.7 8.7 %shard_map.106.kv_ref = bf16[1536,2048]{1,0:T(8,128)(2,1)} custom-call(s32[32,128]{1,0:T(8,128)S(1)} %get-tuple-element.12.par_ref, bf16[1024,1024]{1,0:T(8,128)(2,1)S(1)} %get-tuple-element.37.k_ref, bf16[1024,1024]{1,0:T(8,128)(2,1)S(1)} %get-tuple-element.36.v_ref), custom_call_target="tpu_custom_call" | custom-call | flops 6442450944 | bytes 12000000 | tf_op jit(solution)/shard_map/pallas_call | solution.py:255
  51.4 0.8 all-to-all-done.1
  52.2 7.3 %shard_map.107 = bf16[32,64,128]{2,1,0:T(8,128)(2,1)} custom-call(bf16[1536,128]{1,0:T(8,128)(2,1)S(1)} %bitcast.56, bf16[1536,2048]{1,0:T(8,128)(2,1)} %shard_map.106.kv_ref), custom_call_target="tpu_custom_call" | custom-call | flops 402653184 | bytes 8000000 | tf_op jit(solution)/shard_map/pallas_call | solution.py:292
  59.6 8.6 %all-to-all-start.2 = ((bf16[32,64,128]{2,1,0:T(8,128)(2,1)}), bf16[32,64,128]{2,1,0:T(8,128)(2,1)S(1)}, u32[]{:S(2)}, u32[]{:S(2)}) async-start(bf16[32,64,128]{2,1,0:T(8,128)(2,1)} %shard_map.107), calls=%async_computation.2 | async-start | bytes 1048576 | tf_op jit(solution)/shard_map/all_to_all | solution.py:303
  68.1 1.6 %shard_map.108 = (bf16[1024,1536]{1,0:T(8,128)(2,1)S(1)}, bf16[1024,128]{1,0:T(8,128)(2,1)S(1)}, f32[1024,128]{1,0:T(8,128)S(1)}, f32[1024,128]{1,0:T(8,128)S(1)}) custom-call(s32[32,128]{1,0:T(8,128)S(1)} %bitcast.58, bf16[1024,128]{1,0:T(8,128)(2,1)S(1)} %get-tuple-element.35.q_ref, bf16[1024,128]{1,0:T(8,128)(2,1)S(1)} %get-tuple-element.34.k_ref), custom_call_target="tpu_custom_call" | custom-call | flops 1000000000 | bytes 6000000 | tf_op jit(solution)/shard_map/pallas_call | solution.py:281
  69.7 1.6 %copy-done.1 = bf16[1024,1536]{1,0:T(8,128)(2,1)} copy-done((bf16[1024,1536]{1,0:T(8,128)(2,1)}, bf16[1024,1536]{1,0:T(8,128)(2,1)S(1)}, u32[]{:S(2)}) %copy-start.1) | copy-done | bytes 3145752
  71.4 11.8 %all-to-all-done.2.msg_ref = bf16[32,64,128]{2,1,0:T(8,128)(2,1)S(1)} async-done(((bf16[32,64,128]{2,1,0:T(8,128)(2,1)}), bf16[32,64,128]{2,1,0:T(8,128)(2,1)S(1)}, u32[]{:S(2)}, u32[]{:S(2)}) %all-to-all-start.2) | async-done | bytes 524320 | tf_op jit(solution)/shard_map/all_to_all | solution.py:303
  83.2 1.9 %copy-done.2 = bf16[1024,1536]{1,0:T(8,128)(2,1)S(1)} copy-done((bf16[1024,1536]{1,0:T(8,128)(2,1)S(1)}, bf16[1024,1536]{1,0:T(8,128)(2,1)}, u32[]{:S(2)}) %copy-start.2) | copy-done | bytes 3145752
  85.0 2.4 %shard_map.109.refs_0_ = bf16[1024,128]{1,0:T(8,128)(2,1)S(1)} custom-call(bf16[32,64,128]{2,1,0:T(8,128)(2,1)S(1)} %all-to-all-done.2.msg_ref, bf16[1024,1536]{1,0:T(8,128)(2,1)S(1)} %copy-done.2, bf16[1024,128]{1,0:T(8,128)(2,1)S(1)} %get-tuple-element.14.src_ref, f32[1024,128]{1,0:T(8,128)S(1)} %get-tuple-element.15.mask_ref, ...), custom_call_target="tpu_custom_call" | custom-call | flops 402653184 | bytes 5000000 | tf_op jit(solution)/shard_map/pallas_call | solution.py:306
  87.4 1.3 collective-permute-start
  88.7 1.5 %collective-permute-start.1 = (bf16[1024,128]{1,0:T(8,128)(2,1)S(1)}, bf16[1024,128]{1,0:T(8,128)(2,1)S(1)}, u32[]{:S(2)}, u32[]{:S(2)}) collective-permute-start(bf16[1024,128]{1,0:T(8,128)(2,1)S(1)} %shard_map.109.refs_0_), channel_id=1, source_target_pairs={{0,6},{2,0},{4,2},{6,4},{1,7},{3,1},{5,3},{7,5},{8,14},{10,8},{12,... | collective-permute-start | bytes 786440 | tf_op jit(solution)/shard_map/ppermute | solution.py:231
  90.2 1.5 %collective-permute-start.2 = (bf16[1024,128]{1,0:T(8,128)(2,1)S(1)}, bf16[1024,128]{1,0:T(8,128)(2,1)S(1)}, u32[]{:S(2)}, u32[]{:S(2)}) collective-permute-start(bf16[1024,128]{1,0:T(8,128)(2,1)S(1)} %shard_map.109.refs_0_), channel_id=1, source_target_pairs={{0,4},{2,6},{4,0},{6,2},{1,5},{3,7},{5,1},{7,3},{8,12},{10,14},{12... | collective-permute-start | bytes 786440 | tf_op jit(solution)/shard_map/ppermute | solution.py:231
  91.7 0.1 broadcast_add_fusion
  91.8 4.8 %collective-permute-start.3 = (bf16[1024,128]{1,0:T(8,128)(2,1)S(1)}, bf16[1024,128]{1,0:T(8,128)(2,1)S(1)}, u32[]{:S(2)}, u32[]{:S(2)}) collective-permute-start(bf16[1024,128]{1,0:T(8,128)(2,1)S(1)} %shard_map.109.refs_0_), channel_id=1, source_target_pairs={{0,1},{1,0},{2,3},{3,2},{4,5},{5,4},{6,7},{7,6},{8,9},{9,8},{10,11... | collective-permute-start | bytes 786440 | tf_op jit(solution)/shard_map/ppermute | solution.py:231
  96.6 0.0 collective-permute-done.refs_1_
  96.6 4.6 %collective-permute-start.4 = (bf16[1024,128]{1,0:T(8,128)(2,1)S(1)}, bf16[1024,128]{1,0:T(8,128)(2,1)S(1)}, u32[]{:S(2)}, u32[]{:S(2)}) collective-permute-start(bf16[1024,128]{1,0:T(8,128)(2,1)S(1)} %collective-permute-done.refs_1_), channel_id=1, source_target_pairs={{0,1},{1,0},{2,3},{3,2},{4,5},{5,4},{6,7},{7,6},{8,9},{9,8},{10,11... | collective-permute-start | bytes 786440 | tf_op jit(solution)/shard_map/ppermute | solution.py:231
  101.2 0.0 collective-permute-start.5
  101.2 2.8 %collective-permute-start.6 = (bf16[1024,128]{1,0:T(8,128)(2,1)S(1)}, bf16[1024,128]{1,0:T(8,128)(2,1)S(1)}, u32[]{:S(2)}, u32[]{:S(2)}) collective-permute-start(bf16[1024,128]{1,0:T(8,128)(2,1)S(1)} %collective-permute-done.2.refs_3_), channel_id=1, source_target_pairs={{0,1},{1,0},{2,3},{3,2},{4,5},{5,4},{6,7},{7,6},{8,9},{9,8},{10,11... | collective-permute-start | bytes 786440 | tf_op jit(solution)/shard_map/ppermute | solution.py:231
  104.0 0.1 pad_add_fusion.head_ref
  104.1 1.1 collective-permute-done.6.refs_7_
  105.2 1.2 copy-done.3
  106.4 10.7 %shard_map.110 = (bf16[4,1024,128]{2,1,0:T(8,128)(2,1)S(1)}, bf16[4,1024,128]{2,1,0:T(8,128)(2,1)S(1)}, bf16[1024,128]{1,0:T(8,128)(2,1)S(1)}) custom-call(s32[8]{0:T(128)S(1)} %pad_add_fusion.head_ref, bf16[1024,128]{1,0:T(8,128)(2,1)S(1)} %shard_map.109.refs_0_, bf16[1024,128]{1,0:T(8,128)(2,1)S(1)} %collective-permute-done.refs_1_, ...), custom_call_target="tpu_custom_call" | custom-call | flops 4000000000 | bytes 12000000 | tf_op jit(solution)/shard_map/pallas_call | solution.py:332
  117.1 0.5 collective-permute-start.7
  117.5 2.3 %collective-permute-done.7 = bf16[4,1024,128]{2,1,0:T(8,128)(2,1)S(1)} collective-permute-done((bf16[4,1024,128]{2,1,0:T(8,128)(2,1)S(1)}, bf16[4,1024,128]{2,1,0:T(8,128)(2,1)S(1)}, u32[]{:S(2)}, u32[]{:S(2)}) %collective-permute-start.7) | collective-permute-done | bytes 1048608 | tf_op jit(solution)/shard_map/ppermute | solution.py:231
  119.8 0.3 fusion.17
  120.1 0.1 slice_bitcast_fusion.3
  120.2 0.8 collective-permute-start.10
  121.0 2.0 %collective-permute-start.9 = (bf16[1024,128]{1,0:T(8,128)(2,1)S(1)}, bf16[1024,128]{1,0:T(8,128)(2,1)S(1)}, u32[]{:S(2)}, u32[]{:S(2)}) collective-permute-start(bf16[1024,128]{1,0:T(8,128)(2,1)S(1)} %get-tuple-element.30), channel_id=1, source_target_pairs={{0,2},{2,4},{4,6},{6,0},{1,3},{3,5},{5,7},{7,1},{8,10},{10,12},{12... | collective-permute-start | bytes 786440 | tf_op jit(solution)/shard_map/ppermute | solution.py:231
  122.9 0.7 collective-permute-start.8
  123.7 0.1 pad_maximum_fusion
  123.7 1.3 copy.13
  125.0 4.3 %collective-permute-done.10 = bf16[1024,128]{1,0:T(8,128)(2,1)S(1)} collective-permute-done((bf16[1024,128]{1,0:T(8,128)(2,1)S(1)}, bf16[1024,128]{1,0:T(8,128)(2,1)S(1)}, u32[]{:S(2)}, u32[]{:S(2)}) %collective-permute-start.10) | collective-permute-done | bytes 262176 | tf_op jit(solution)/shard_map/ppermute | solution.py:231
  129.3 6.3 %collective-permute-done.9 = bf16[1024,128]{1,0:T(8,128)(2,1)S(1)} collective-permute-done((bf16[1024,128]{1,0:T(8,128)(2,1)S(1)}, bf16[1024,128]{1,0:T(8,128)(2,1)S(1)}, u32[]{:S(2)}, u32[]{:S(2)}) %collective-permute-start.9) | collective-permute-done | bytes 262176 | tf_op jit(solution)/shard_map/ppermute | solution.py:231
  135.6 0.9 fusion.16
  (21 shorter events, 0.0 us)
Async XLA Ops:
  7.2 17.8 %copy-start = (bf16[3,1024,128]{2,1,0:T(8,128)(2,1)S(1)}, bf16[3,1024,128]{2,1,0:T(8,128)(2,1)}, u32[]{:S(2)}) copy-start(bf16[3,1024,128]{2,1,0:T(8,128)(2,1)} %param.14) | copy-start | bytes 2359300
  7.2 0.8 copy-start.4
  8.0 0.7 copy-start.5
  8.7 16.4 %copy-start.6 = (bf16[1024,1024]{1,0:T(8,128)(2,1)S(1)}, bf16[1024,1024]{1,0:T(8,128)(2,1)}, u32[]{:S(2)}) copy-start(bf16[1024,1024]{1,0:T(8,128)(2,1)} %refs_8_.1) | copy-start | bytes 6291460
  10.1 20.6 %all-to-all-start = ((s32[32,1,128]{2,1,0:T(1,128)}), s32[32,1,128]{2,1,0:T(1,128)S(1)}, u32[]{:S(2)}, u32[]{:S(2)}) async-start(s32[32,1,128]{2,1,0:T(1,128)} %bitcast.7), calls=%async_computation | async-start | bytes 32768 | tf_op jit(solution)/shard_map/all_to_all | solution.py:245
  22.2 83.0 %all-gather.2.cloned.1.call-start = ((), (), s32[]{:S(2)}) async-start(), calls=%async_computation.3 | async-start | bytes 2359296 | tf_op jit(solution)/shard_map/all_gather | solution.py:239
  33.3 18.9 %all-to-all-start.1 = ((bf16[32,48,128]{2,1,0:T(8,128)(2,1)}), bf16[32,48,128]{2,1,0:T(8,128)(2,1)S(1)}, u32[]{:S(2)}, u32[]{:S(2)}) async-start(bf16[32,48,128]{2,1,0:T(8,128)(2,1)} %bitcast.12), calls=%async_computation.1 | async-start | bytes 786432 | tf_op jit(solution)/shard_map/all_to_all | solution.py:279
  59.6 23.6 %all-to-all-start.2 = ((bf16[32,64,128]{2,1,0:T(8,128)(2,1)}), bf16[32,64,128]{2,1,0:T(8,128)(2,1)S(1)}, u32[]{:S(2)}, u32[]{:S(2)}) async-start(bf16[32,64,128]{2,1,0:T(8,128)(2,1)} %shard_map.107), calls=%async_computation.2 | async-start | bytes 1048576 | tf_op jit(solution)/shard_map/all_to_all | solution.py:303
  69.7 1.6 %copy-start.1 = (bf16[1024,1536]{1,0:T(8,128)(2,1)}, bf16[1024,1536]{1,0:T(8,128)(2,1)S(1)}, u32[]{:S(2)}) copy-start(bf16[1024,1536]{1,0:T(8,128)(2,1)S(1)} %get-tuple-element.13.back_ref) | copy-start | bytes 9437188
  83.2 1.9 %copy-start.2 = (bf16[1024,1536]{1,0:T(8,128)(2,1)S(1)}, bf16[1024,1536]{1,0:T(8,128)(2,1)}, u32[]{:S(2)}) copy-start(bf16[1024,1536]{1,0:T(8,128)(2,1)} %copy-done.1) | copy-start | bytes 9437188
  87.4 9.2 %collective-permute-start = (bf16[1024,128]{1,0:T(8,128)(2,1)S(1)}, bf16[1024,128]{1,0:T(8,128)(2,1)S(1)}, u32[]{:S(2)}, u32[]{:S(2)}) collective-permute-start(bf16[1024,128]{1,0:T(8,128)(2,1)S(1)} %shard_map.109.refs_0_), channel_id=1, source_target_pairs={{0,2},{2,4},{4,6},{6,0},{1,3},{3,5},{5,7},{7,1},{8,10},{10,12},{12... | collective-permute-start | bytes 786440 | tf_op jit(solution)/shard_map/ppermute | solution.py:231
  88.7 12.5 %collective-permute-start.1 = (bf16[1024,128]{1,0:T(8,128)(2,1)S(1)}, bf16[1024,128]{1,0:T(8,128)(2,1)S(1)}, u32[]{:S(2)}, u32[]{:S(2)}) collective-permute-start(bf16[1024,128]{1,0:T(8,128)(2,1)S(1)} %shard_map.109.refs_0_), channel_id=1, source_target_pairs={{0,6},{2,0},{4,2},{6,4},{1,7},{3,1},{5,3},{7,5},{8,14},{10,8},{12,... | collective-permute-start | bytes 786440 | tf_op jit(solution)/shard_map/ppermute | solution.py:231
  90.2 11.1 %collective-permute-start.2 = (bf16[1024,128]{1,0:T(8,128)(2,1)S(1)}, bf16[1024,128]{1,0:T(8,128)(2,1)S(1)}, u32[]{:S(2)}, u32[]{:S(2)}) collective-permute-start(bf16[1024,128]{1,0:T(8,128)(2,1)S(1)} %shard_map.109.refs_0_), channel_id=1, source_target_pairs={{0,4},{2,6},{4,0},{6,2},{1,5},{3,7},{5,1},{7,3},{8,12},{10,14},{12... | collective-permute-start | bytes 786440 | tf_op jit(solution)/shard_map/ppermute | solution.py:231
  91.8 12.3 %collective-permute-start.3 = (bf16[1024,128]{1,0:T(8,128)(2,1)S(1)}, bf16[1024,128]{1,0:T(8,128)(2,1)S(1)}, u32[]{:S(2)}, u32[]{:S(2)}) collective-permute-start(bf16[1024,128]{1,0:T(8,128)(2,1)S(1)} %shard_map.109.refs_0_), channel_id=1, source_target_pairs={{0,1},{1,0},{2,3},{3,2},{4,5},{5,4},{6,7},{7,6},{8,9},{9,8},{10,11... | collective-permute-start | bytes 786440 | tf_op jit(solution)/shard_map/ppermute | solution.py:231
  96.6 7.5 %collective-permute-start.4 = (bf16[1024,128]{1,0:T(8,128)(2,1)S(1)}, bf16[1024,128]{1,0:T(8,128)(2,1)S(1)}, u32[]{:S(2)}, u32[]{:S(2)}) collective-permute-start(bf16[1024,128]{1,0:T(8,128)(2,1)S(1)} %collective-permute-done.refs_1_), channel_id=1, source_target_pairs={{0,1},{1,0},{2,3},{3,2},{4,5},{5,4},{6,7},{7,6},{8,9},{9,8},{10,11... | collective-permute-start | bytes 786440 | tf_op jit(solution)/shard_map/ppermute | solution.py:231
  101.2 2.9 %collective-permute-start.5 = (bf16[1024,128]{1,0:T(8,128)(2,1)S(1)}, bf16[1024,128]{1,0:T(8,128)(2,1)S(1)}, u32[]{:S(2)}, u32[]{:S(2)}) collective-permute-start(bf16[1024,128]{1,0:T(8,128)(2,1)S(1)} %collective-permute-done.1.refs_2_), channel_id=1, source_target_pairs={{0,1},{1,0},{2,3},{3,2},{4,5},{5,4},{6,7},{7,6},{8,9},{9,8},{10,11... | collective-permute-start | bytes 786440 | tf_op jit(solution)/shard_map/ppermute | solution.py:231
  101.2 4.0 %collective-permute-start.6 = (bf16[1024,128]{1,0:T(8,128)(2,1)S(1)}, bf16[1024,128]{1,0:T(8,128)(2,1)S(1)}, u32[]{:S(2)}, u32[]{:S(2)}) collective-permute-start(bf16[1024,128]{1,0:T(8,128)(2,1)S(1)} %collective-permute-done.2.refs_3_), channel_id=1, source_target_pairs={{0,1},{1,0},{2,3},{3,2},{4,5},{5,4},{6,7},{7,6},{8,9},{9,8},{10,11... | collective-permute-start | bytes 786440 | tf_op jit(solution)/shard_map/ppermute | solution.py:231
  105.2 1.2 copy-start.3
  117.1 2.8 %collective-permute-start.7 = (bf16[4,1024,128]{2,1,0:T(8,128)(2,1)S(1)}, bf16[4,1024,128]{2,1,0:T(8,128)(2,1)S(1)}, u32[]{:S(2)}, u32[]{:S(2)}) collective-permute-start(bf16[4,1024,128]{2,1,0:T(8,128)(2,1)S(1)} %get-tuple-element.19), channel_id=1, source_target_pairs={{0,1},{1,0},{2,3},{3,2},{4,5},{5,4},{6,7},{7,6},{8,9},{9,8},{10,11... | collective-permute-start | bytes 3145736 | tf_op jit(solution)/shard_map/ppermute | solution.py:231
  119.8 3.8 %copy-start.7 = (bf16[1024,1,128]{2,0,1:T(8,128)(2,1)S(1)}, bf16[1024,1,128]{2,0,1:T(8,128)(2,1)}, u32[]{:S(2)}) copy-start(bf16[1024,1,128]{2,0,1:T(8,128)(2,1)} %get-tuple-element.31) | copy-start | bytes 786436
  119.8 3.8 %copy-start.8 = (bf16[1024,1,128]{2,0,1:T(8,128)(2,1)S(1)}, bf16[1024,1,128]{2,0,1:T(8,128)(2,1)}, u32[]{:S(2)}) copy-start(bf16[1024,1,128]{2,0,1:T(8,128)(2,1)} %get-tuple-element.32) | copy-start | bytes 786436
  120.2 9.2 %collective-permute-start.10 = (bf16[1024,128]{1,0:T(8,128)(2,1)S(1)}, bf16[1024,128]{1,0:T(8,128)(2,1)S(1)}, u32[]{:S(2)}, u32[]{:S(2)}) collective-permute-start(bf16[1024,128]{1,0:T(8,128)(2,1)S(1)} %get-tuple-element.29), channel_id=1, source_target_pairs={{0,4},{2,6},{4,0},{6,2},{1,5},{3,7},{5,1},{7,3},{8,12},{10,14},{12... | collective-permute-start | bytes 786440 | tf_op jit(solution)/shard_map/ppermute | solution.py:231
  121.0 14.6 %collective-permute-start.9 = (bf16[1024,128]{1,0:T(8,128)(2,1)S(1)}, bf16[1024,128]{1,0:T(8,128)(2,1)S(1)}, u32[]{:S(2)}, u32[]{:S(2)}) collective-permute-start(bf16[1024,128]{1,0:T(8,128)(2,1)S(1)} %get-tuple-element.30), channel_id=1, source_target_pairs={{0,2},{2,4},{4,6},{6,0},{1,3},{3,5},{5,7},{7,1},{8,10},{10,12},{12... | collective-permute-start | bytes 786440 | tf_op jit(solution)/shard_map/ppermute | solution.py:231
  122.9 12.7 %collective-permute-start.8 = (bf16[1024,128]{1,0:T(8,128)(2,1)S(1)}, bf16[1024,128]{1,0:T(8,128)(2,1)S(1)}, u32[]{:S(2)}, u32[]{:S(2)}) collective-permute-start(bf16[1024,128]{1,0:T(8,128)(2,1)S(1)} %get-tuple-element.28), channel_id=1, source_target_pairs={{0,6},{2,0},{4,2},{6,4},{1,7},{3,1},{5,3},{7,5},{8,14},{10,8},{12,... | collective-permute-start | bytes 786440 | tf_op jit(solution)/shard_map/ppermute | solution.py:231
Sparse Core Ops, SparseCore 0:
  24.9 29.6 all-gather.1

commit v2 on v1

--- a/solution.py
+++ b/solution.py
@@ -15,7 +15,6 @@
 MSG = 64
 SAMPLE = ("z", "y")
 HEAD = ("x", "core")
-VLIM = 48 * 1024 * 1024
 F32 = jnp.float32
 BF = jnp.bfloat16
 NT = (((1,), (1,)), ((), ()))
@@ -26,14 +25,18 @@
     return lax.broadcasted_iota(jnp.int32, shape, dim)
 
 
-def call(kernel, out, cost, **kw):
+def call(kernel, out, cost, vmem=24, **kw):
     return pl.pallas_call(
         kernel,
         out_shape=out,
-        compiler_params=pltpu.CompilerParams(vmem_limit_bytes=VLIM),
+        compiler_params=pltpu.CompilerParams(vmem_limit_bytes=vmem * 2**20),
         cost_estimate=pl.CostEstimate(flops=cost[0], bytes_accessed=cost[1], transcendentals=0),
         **kw,
     )
+
+
+def keep(x, space=pltpu.VMEM):
+    return pltpu.with_memory_space_constraint(x, space)
 
 
 def sds(shape, dtype):
@@ -87,6 +90,32 @@
     par_ref[...] = jnp.concatenate([pars, fill], axis=1)
 
 
+def pack_kernel(up_ref, down_ref, wo_ref, right_ref, left_ref, stage, sems):
+    writes = []
+    for n in range(2):
+        half = pl.ds(n * 256, 256)
+        pairs = [(down_ref.at[half], stage.at[n, pl.ds(256, 256)])]
+        pairs.append((wo_ref, stage.at[n, pl.ds(512, 128)]))
+        for k in range(4):
+            block = pl.ds(k * 256, 256)
+            pairs.append((up_ref.at[block, half], stage.at[n, pl.ds(0, 256), block]))
+        copies = [
+            pltpu.make_async_copy(a, b, sems.at[n * 7 + i]) for i, (a, b) in enumerate(pairs)
+        ]
+        for copy in copies:
+            copy.start()
+        writes.append((copies, (right_ref, left_ref)[n]))
+    ends = []
+    for n, (copies, target) in enumerate(writes):
+        for copy in copies:
+            copy.wait()
+        end = pltpu.make_async_copy(stage.at[n], target, sems.at[n * 7 + 6])
+        end.start()
+        ends.append(end)
+    for end in ends:
+        end.wait()
+
+
 def column(lists, count, depth):
     shape = (count, depth, 128)
     picked = jnp.where(
@@ -110,7 +139,7 @@
     out_ref[...] = jnp.dot(hot, q_ref[...], preferred_element_type=F32).astype(BF)
 
 
-def place_kernel(recv_ref, q_ref, k_ref, back_ref, src_ref, mask_ref, own_ref):
+def place_kernel(recv_ref, q_ref, k_ref, out_ref):
     slot = recv_ref[...]
     high = jnp.where(slot >= 0, slot // 32, -1)
     low = slot % 32
@@ -124,17 +153,13 @@
     wide = jnp.concatenate([acc, jnp.zeros((64, 96), F32)], axis=1)
     src = column(wide[:32], 32, 32)
     place = column(wide[32:], 32, 32)
-    pos = src * float(CAP) + place
-    lane = iota((ROWS, 128), 1).astype(F32)
-    src_ref[...] = (lane == src).astype(F32).astype(BF)
-    mask_ref[...] = (lane == place).astype(F32)
-    for t in range(ITEMS // 256):
-        items = (iota((ROWS, 256), 1) + t * 256).astype(F32)
-        back_ref[:, t * 256 : (t + 1) * 256] = (items == pos).astype(F32).astype(BF)
     prod = q_ref[...].astype(F32) * k_ref[...].astype(F32) * (1.0 / HD**0.5)
     s0 = jnp.sum(prod[:, :HD], axis=1, keepdims=True)
     s1 = jnp.sum(prod[:, HD:], axis=1, keepdims=True)
-    own_ref[...] = jnp.where(iota((ROWS, 128), 1) < HD, s0, s1)
+    lane = iota((ROWS, 128), 1)
+    out_ref[...] = jnp.where(
+        lane == 0, src, jnp.where(lane == 1, place, jnp.where(lane == 2, s0, s1))
+    )
 
 
 def attend_kernel(q_ref, kv_ref, out_ref):
@@ -182,49 +207,105 @@
         out_ref[o, CAP:, :] = piece.astype(BF)
 
 
-def merge_kernel(msg_ref, back_ref, src_ref, mask_ref, own_ref, v_ref, out_ref):
-    rows = back_ref.shape[0]
-    ctx = msg_ref[:, :CAP, :].reshape(ITEMS, 128)
-    ctx = jnp.dot(back_ref[...], ctx, preferred_element_type=F32)
-    cols = []
-    src = src_ref[:, :PEERS]
+def merge_kernel(info_ref, msg_ref, place_ref, v_ref, mine_ref, theirs_ref):
+    rows = 256
+    outs = [r.at[pl.ds(n * rows, rows)] for r in (mine_ref, theirs_ref) for n in range(2)]
+    ctx_all = msg_ref[:, :CAP, :].reshape(ITEMS, 128)
+    parts = []
     for h in range(2):
-        lse = jnp.zeros((rows, 128), F32)
         for j in range(3):
-            part = msg_ref[:, CAP + h * 3 + j, :].reshape(PEERS, 128)
-            lse = lse + jnp.dot(src, part, preferred_element_type=F32)
-        cols.append(jnp.sum(lse * mask_ref[...], axis=1, keepdims=True))
-    lse = jnp.where(iota((rows, 128), 1) < HD, cols[0], cols[1])
-    own = own_ref[...]
-    top = jnp.maximum(lse, own)
-    a = jnp.exp(lse - top)
-    b = jnp.exp(own - top)
-    out_ref[...] = ((a * ctx + b * v_ref[...].astype(F32)) / (a + b)).astype(BF)
-
-
-def ffn_kernel(head_ref, *refs):
-    pieces = refs[:8]
-    x_ref, wo_ref, wu_ref, wd_ref = refs[8:12]
-    same_ref, other_ref, part_ref = refs[12:15]
-    att, hid, down = refs[15:18]
-    for i in range(8):
-        at = pl.multiple_of(head_ref[i] * 128, 128)
-        att[:, pl.ds(at, 128)] = pieces[i][...]
-    x = x_ref[...].astype(F32)
-    hidden = (x + jnp.dot(att[...], wo_ref[...], preferred_element_type=F32)).astype(BF)
-    hid[...] = hidden
-    hf = hidden.astype(F32)
-    scale = lax.rsqrt(jnp.mean(hf * hf, axis=-1, keepdims=True) + 1e-05)
-    normed = (hf * scale).astype(BF)
-    up = jnp.dot(normed, wu_ref[...], preferred_element_type=F32)
-    act = jax.nn.gelu(up).astype(BF)
-    down[...] = jnp.dot(act, wd_ref[...], preferred_element_type=F32).astype(BF)
-    part_ref[...] = hid[:, pl.ds(pl.multiple_of(head_ref[0] * 128, 128), 128)]
-    for i in range(4):
-        at = pl.multiple_of(head_ref[i] * 128, 128)
-        same_ref[i] = down[:, pl.ds(at, 128)]
-        at = pl.multiple_of(head_ref[4 + i] * 128, 128)
-        other_ref[i] = down[:, pl.ds(at, 128)]
+            parts.append(msg_ref[:, CAP + h * 3 + j, :].reshape(PEERS, 128))
+    parts = jnp.concatenate(parts, axis=1)
+    for i, out in enumerate(outs):
+        block = (info_ref[1] if i < 2 else 1 - info_ref[1]) + 2 * (i % 2)
+        at = pl.ds(pl.multiple_of(block * rows, rows), rows)
+        known = place_ref[at, :]
+        src, place = known[:, 0:1], known[:, 1:2]
+        lane = iota((rows, 128), 1)
+        lanes = lane.astype(F32)
+        pos = src * float(CAP) + place
+        hot = (iota((rows, ITEMS), 1).astype(F32) == pos).astype(F32).astype(BF)
+        ctx = jnp.dot(hot, ctx_all, preferred_element_type=F32)
+        from_src = (iota((rows, PEERS), 1).astype(F32) == src).astype(F32).astype(BF)
+        lists = jnp.dot(from_src, parts, preferred_element_type=F32)
+        cols = []
+        for h in range(2):
+            base = h * 384
+            lse = lists[:, base : base + 128] + lists[:, base + 128 : base + 256]
+            lse = lse + lists[:, base + 256 : base + 384]
+            lse = jnp.where(lanes == place, lse, 0.0)
+            cols.append(jnp.sum(lse, axis=1, keepdims=True))
+        lse = jnp.where(lane < HD, cols[0], cols[1])
+        own = jnp.where(lane < HD, known[:, 2:3], known[:, 3:4])
+        top = jnp.maximum(lse, own)
+        a = jnp.exp(lse - top)
+        b = jnp.exp(own - top)
+        out[...] = ((a * ctx + b * v_ref[at, :].astype(F32)) / (a + b)).astype(BF)
+
+
+def project_kernel(info_ref, *refs):
+    rows = jnp.concatenate([r[...] for r in refs[:4]], axis=1)
+    weight = jnp.concatenate([r[...] for r in refs[4:8]], axis=0)
+    refs[8][...] = jnp.dot(rows, weight, preferred_element_type=F32).astype(BF)
+
+
+def ffn_kernel(
+    info_ref, x0_ref, x1_ref, p_ref, r_ref, up_ref, down_ref, right_ref, left_ref, *refs
+):
+    same_ref, other_ref, ups, downs, hid, acc, sems = refs
+    pairs = [(up_ref, ups.at[0]), (down_ref, downs.at[0])]
+    for n, src in enumerate((right_ref, left_ref)):
+        for k in range(4):
+            block = pl.ds(k * 256, 256)
+            pairs.append((src.at[pl.ds(0, 256), block], ups.at[1, block, pl.ds(n * 256, 256)]))
+        pairs.append((src.at[pl.ds(256, 256)], downs.at[1, pl.ds(n * 256, 256)]))
+    copies = [pltpu.make_async_copy(a, b, sems.at[i]) for i, (a, b) in enumerate(pairs)]
+    for copy in copies:
+        copy.start()
+    normed = []
+    for n, x_ref in enumerate((x0_ref, x1_ref)):
+        at = pl.ds(n * 256, 256)
+        attn = p_ref[at].astype(F32) + r_ref[at].astype(F32)
+        hidden = (x_ref[...].astype(F32) + attn).astype(BF).astype(F32)
+        scale = lax.rsqrt(jnp.mean(hidden * hidden, axis=-1, keepdims=True) + 1e-05)
+        normed.append((hidden * scale).astype(BF))
+        hid[at] = jnp.where(info_ref[0] // 2 == n, hidden, 0.0)
+    for unit in range(2):
+        for n in range(2):
+            at = pl.ds(n * 256, 256)
+            if n == 0:
+                for copy in (copies[:1], copies[2:6] + copies[7:11])[unit]:
+                    copy.wait()
+            up = jnp.dot(normed[n], ups[unit], preferred_element_type=F32)
+            act = jax.nn.gelu(up).astype(BF)
+            if n == 0:
+                for copy in (copies[1:2], [copies[6], copies[11]])[unit]:
+                    copy.wait()
+            down = jnp.dot(act, downs[unit], preferred_element_type=F32)
+            if unit == 0:
+                acc[at] = down
+            else:
+                acc[at] += down
+    core = info_ref[2]
+    for d in range(4):
+        head = ((info_ref[0] + d) % 4) * 2
+        at = pl.ds(pl.multiple_of((head + core) * 128, 128), 128)
+        same_ref[d] = hid[:, at] + acc[:, at]
+        at = pl.ds(pl.multiple_of((head + 1 - core) * 128, 128), 128)
+        other_ref[d] = acc[:, at].astype(BF)
+
+
+def final_kernel(same_ref, other_ref, o0, o1, o2, o3):
+    for i, out in enumerate((o0, o1, o2, o3)):
+        out[...] = (same_ref[i] + other_ref[i].astype(F32)).astype(BF)
+
+
+def place_rows_kernel(info_ref, p0, p1, p2, p3, out_ref):
+    for n in range(2):
+        at = pl.ds(n * 256, 256)
+        for parity, a, b in ((info_ref[1], p0, p2), (1 - info_ref[1], p1, p3)):
+            to = pl.multiple_of((parity + 2 * n) * 256, 256)
+            out_ref[pl.ds(to, 256), :] = (a[at].astype(F32) + b[at].astype(F32)).astype(BF)
 
 
 def shift(x, axis, by, size):
@@ -236,12 +317,28 @@
 
 
 def body(stream_in, keys, values, counts, slots, w_qkv, w_out, w_up, w_down):
-    wo_full = lax.all_gather(w_out, HEAD, axis=0, tiled=True)
+    vmem = pl.BlockSpec(memory_space=pltpu.VMEM)
+    hbm = pl.BlockSpec(memory_space=pltpu.HBM)
+    x = lax.axis_index("x")
+    core = lax.axis_index("core")
+    info = jnp.stack([x, x % 2, core]).astype(jnp.int32)
+
     send, par = call(
         plan_kernel,
-        (sds((PEERS, 128), jnp.int32), sds((PEERS, 128), jnp.int32)),
+        (pltpu.HBM((PEERS, 128), jnp.int32), pltpu.VMEM((PEERS, 128), jnp.int32)),
         (4 * 10**8, 10**6),
-    )(counts.reshape(1, ROWS), slots.T)
+    )(keep(counts.reshape(1, ROWS), pltpu.HBM), keep(slots.T, pltpu.HBM))
+    for_right, for_left = call(
+        pack_kernel,
+        (pltpu.HBM((640, ROWS), BF), pltpu.HBM((640, ROWS), BF)),
+        (0, 5 * 10**6),
+        in_specs=[hbm, hbm, hbm],
+        out_specs=(hbm, hbm),
+        scratch_shapes=[pltpu.VMEM((2, 640, ROWS), BF), pltpu.SemaphoreType.DMA((14,))],
+    )(*(keep(w, pltpu.HBM) for w in (w_up, w_down, w_out)))
+    left = shift(for_right, "x", 1, 4)
+    right = shift(for_left, "x", 3, 4)
+    wo_two = shift(w_out, "x", 2, 4)
     recv = lax.all_to_all(
         send.reshape(PEERS, 1, 128), SAMPLE, split_axis=0, concat_axis=0, tiled=True
     ).reshape(PEERS, 128)
@@ -252,9 +349,10 @@
     query, own_key, own_value = projected[0], projected[1], projected[2]
     new_kv = jnp.stack([own_key, own_value], axis=1)
 
+    flat_keys, flat_values = keys.reshape(ROWS, ROWS), values.reshape(ROWS, ROWS)
     kv = call(
         expand_kernel,
-        sds((ITEMS, 2 * ROWS), BF),
+        pltpu.HBM((ITEMS, 2 * ROWS), BF),
         (2 * ITEMS * ROWS * ROWS * 2, 12 * 10**6),
         grid=(4,),
         in_specs=[
@@ -263,11 +361,11 @@
             pl.BlockSpec((ROWS, ROWS), lambda i: (0, 0)),
         ],
         out_specs=pl.BlockSpec((8 * CAP, 2 * ROWS), lambda i: (i, 0)),
-    )(par, keys.reshape(ROWS, ROWS), values.reshape(ROWS, ROWS))
+    )(keep(par), flat_keys, flat_values)
 
     q_send = call(
         query_kernel,
-        sds((ITEMS, 128), BF),
+        pltpu.HBM((ITEMS, 128), BF),
         (2 * ITEMS * ROWS * 128, 10**6),
         grid=(4,),
         in_specs=[
@@ -278,20 +376,11 @@
     )(recv, query)
     q_recv = lax.all_to_all(q_send, SAMPLE, split_axis=0, concat_axis=0, tiled=True)
 
-    back, src, mask, own = call(
-        place_kernel,
-        (
-            sds((ROWS, ITEMS), BF),
-            sds((ROWS, 128), BF),
-            sds((ROWS, 128), F32),
-            sds((ROWS, 128), F32),
-        ),
-        (10**9, 6 * 10**6),
-    )(recv, query, own_key)
+    places = call(place_kernel, pltpu.HBM((ROWS, 128), F32), (10**9, 2 * 10**6))(recv, query, own_key)
 
     msg = call(
         attend_kernel,
-        sds((PEERS, MSG, 128), BF),
+        pltpu.HBM((PEERS, MSG, 128), BF),
         (2 * ITEMS * ROWS * 128, 8 * 10**6),
         grid=(4,),
         in_specs=[
@@ -299,60 +388,73 @@
             pl.BlockSpec((8 * CAP, 2 * ROWS), lambda i: (i, 0)),
         ],
         out_specs=pl.BlockSpec((8, MSG, 128), lambda i: (i, 0, 0)),
-    )(q_recv, kv)
+    )(q_recv, keep(kv, pltpu.HBM))
     answer = lax.all_to_all(msg, SAMPLE, split_axis=0, concat_axis=0, tiled=True)
-
-    whole = lambda *shape: pl.BlockSpec(shape, lambda i: (0,) * len(shape))
-    attended = call(
+    fixed = lambda *shape: pl.BlockSpec(shape, lambda i, h: (0,) * len(shape))
+    block = lambda n: pl.BlockSpec((256, ROWS), lambda i, h: (h[1] + 2 * n, 0))
+    pair = sds((512, 128), BF)
+    smem = pl.BlockSpec(memory_space=pltpu.SMEM)
+    mine, theirs = call(
         merge_kernel,
-        sds((ROWS, 128), BF),
+        (pair, pair),
         (2 * ITEMS * ROWS * 128, 5 * 10**6),
-        grid=(4,),
-        in_specs=[
-            whole(PEERS, MSG, 128),
-            pl.BlockSpec((256, ITEMS), lambda i: (i, 0)),
-            pl.BlockSpec((256, 128), lambda i: (i, 0)),
-            pl.BlockSpec((256, 128), lambda i: (i, 0)),
-            pl.BlockSpec((256, 128), lambda i: (i, 0)),
-            pl.BlockSpec((256, 128), lambda i: (i, 0)),
-        ],
-        out_specs=pl.BlockSpec((256, 128), lambda i: (i, 0)),
-    )(answer, back, src, mask, own, own_value)
-
-    near = [attended] + [shift(attended, "x", d, 4) for d in (1, 3, 2)]
-    far = [shift(piece, "core", 1, 2) for piece in near]
-    x = lax.axis_index("x")
-    core = lax.axis_index("core")
-    xs = jnp.stack([x, (x + 3) % 4, (x + 1) % 4, (x + 2) % 4])
-    heads = jnp.concatenate([xs * 2 + core, xs * 2 + 1 - core]).astype(jnp.int32)
-
-    rows = lambda *shape: pl.BlockSpec(shape, lambda i, h: (i,) + (0,) * (len(shape) - 1))
-    fixed = lambda *shape: pl.BlockSpec(shape, lambda i, h: (0,) * len(shape))
-    blocks = lambda: pl.BlockSpec((4, 256, 128), lambda i, h: (0, i, 0))
-    same, other, hidden_part = call(
-        ffn_kernel,
-        (sds((4, ROWS, 128), BF), sds((4, ROWS, 128), BF), sds((ROWS, 128), BF)),
-        (4 * 10**9, 12 * 10**6),
+        in_specs=[smem] + [vmem] * 3,
+        out_specs=(vmem, vmem),
+    )(info, answer, keep(places, pltpu.HBM), own_value)
+
+    from_left = shift(theirs, "x", 1, 4)
+    from_right = shift(theirs, "x", 3, 4)
+    from_two = shift(mine, "x", 2, 4)
+    last = lambda at: pl.BlockSpec((128, ROWS), lambda i, h: (at, 0))
+    partial = call(
+        project_kernel,
+        sds((512, ROWS), BF),
+        (6 * 10**8, 3 * 10**6),
         grid_spec=pltpu.PrefetchScalarGridSpec(
             num_scalar_prefetch=1,
-            grid=(4,),
-            in_specs=[rows(256, 128)] * 8
-            + [rows(256, ROWS), fixed(ROWS, ROWS), fixed(ROWS, 512), fixed(512, ROWS)],
-            out_specs=(blocks(), blocks(), rows(256, 128)),
+            grid=(1,),
+            in_specs=[fixed(512, 128)] * 4 + [last(0), last(4), last(4), last(0)],
+            out_specs=fixed(512, ROWS),
+        ),
+    )(info, mine, from_left, from_right, from_two, w_out, left, right, wo_two)
+    partner = shift(partial, "core", 1, 2)
+
+    same, other = call(
+        ffn_kernel,
+        (sds((4, 512, 128), F32), sds((4, 512, 128), BF)),
+        (2 * 10**9, 10 * 10**6),
+        grid_spec=pltpu.PrefetchScalarGridSpec(
+            num_scalar_prefetch=1,
+            grid=(1,),
+            in_specs=[block(0), block(1), fixed(512, ROWS), fixed(512, ROWS)] + [hbm] * 4,
+            out_specs=(fixed(4, 512, 128), fixed(4, 512, 128)),
             scratch_shapes=[
-                pltpu.VMEM((256, ROWS), BF),
-                pltpu.VMEM((256, ROWS), BF),
-                pltpu.VMEM((256, ROWS), BF),
+                pltpu.VMEM((2, ROWS, 512), BF),
+                pltpu.VMEM((2, 512, ROWS), BF),
+                pltpu.VMEM((512, ROWS), F32),
+                pltpu.VMEM((512, ROWS), F32),
+                pltpu.SemaphoreType.DMA((12,)),
             ],
         ),
-    )(heads, *near, *far, stream_in, wo_full, w_up, w_down)
+    )(
+        info,
+        stream_in,
+        stream_in,
+        partial,
+        partner,
+        *(keep(w, pltpu.HBM) for w in (w_up, w_down, right, left)),
+    )
 
     swapped = shift(other, "core", 1, 2)
-    pair = same.astype(F32) + swapped.astype(F32)
-    sums = pair.astype(BF)
-    got = [shift(sums[1], "x", 3, 4), shift(sums[2], "x", 1, 4), shift(sums[3], "x", 2, 4)]
-    total = pair[0] + got[0].astype(F32) + got[1].astype(F32) + got[2].astype(F32)
-    layer_out = (hidden_part.astype(F32) + total).astype(BF)
+    done = call(final_kernel, (pair,) * 4, (10**6, 10**6))(same, swapped)
+    parts = [done[0]] + [shift(done[d], "x", d, 4) for d in (1, 2, 3)]
+    layer_out = call(
+        place_rows_kernel,
+        sds((ROWS, 128), BF),
+        (10**6, 5 * 10**5),
+        in_specs=[smem] + [vmem] * 4,
+        out_specs=vmem,
+    )(info, *parts)
     return (layer_out, new_kv)
 
 

time: 144 us -> 123 us (0.85)
  between operations: 14.2 us -> 0.8 us
  waiting for transfers between devices: 30.6 us -> 22.7 us
  Pallas kernels: 34.8 us -> 39.8 us
  local copies, waits for them, and re-layouts: 12.1 us -> 9.5 us
  other arithmetic: 3.42 us -> 1.19 us
    pallas_call x7 -> x11, Pallas kernels: 34.8 us -> 39.8 us  [the longest x1 8.75 us: body(): call(expand_kernel, pltpu.HBM((ITEMS, 2 * ROWS), BF), (2 * ITEMS * ROWS *...]
    all_to_all x1, waiting for transfers between devices: 11.8 us -> 7.96 us  [body(): lax.all_to_all(msg, SAMPLE, split_axis=0, concat_axis=0, tiled=True)]
    ppermute x11, starting transfers between devices: 20.4 us -> 16.8 us  [shift(): return lax.ppermute(x, axis, [(i, (i + by) % size) for i in range(size)])]
    all_to_all x1, waiting for transfers between devices: 3.41 us -> 0.01 us  [body(): lax.all_to_all(send.reshape(PEERS, 1, 128), SAMPLE, split_axis=0, concat_...]
    all_to_all x1, starting transfers between devices: 5.81 us -> 9.21 us  [body(): lax.all_to_all(q_send, SAMPLE, split_axis=0, concat_axis=0, tiled=True)]
    unnamed x19 -> x23, local copies, waits for them, and re-layouts: 7.56 us -> 4.89 us
    reduce_sum x1, other arithmetic: 2.07 us -> 0.48 us  [rms_rows(): jnp.mean(stream * stream, axis=-1, keepdims=True) + 1e-05]
  transfers between devices with their start and end apart: 15 -> 14, of which waited for: 7 -> 9; matrix products, arithmetic and copies ran while one was open for 7% -> 7% of each run, Pallas kernels for 16% -> 23%
where the time goes in v2:
time: 123 us
  starting transfers between devices  47.3 us (38%)
  Pallas kernels  39.8 us (32%)
  waiting for transfers between devices  22.7 us (18%)
  local copies, waits for them, and re-layouts  9.5 us (8%)
  matrix products  1.3 us (1%)
    ppermute x11, starting transfers between devices, shift(): return lax.ppermute(x, axis, [(i, (i + by) % size) for i in range(size)])  16.8 us
    ppermute x11, waiting for transfers between devices, shift(): return lax.ppermute(x, axis, [(i, (i + by) % size) for i in range(size)])  14.6 us
    all_to_all x1, starting transfers between devices, body(): lax.all_to_all(send.reshape(PEERS, 1, 128), SAMPLE, split_axis=0, concat_...  12 us
    all_to_all x1, starting transfers between devices, body(): lax.all_to_all(q_send, SAMPLE, split_axis=0, concat_axis=0, tiled=True)  9.21 us
    all_to_all x1, starting transfers between devices, body(): lax.all_to_all(msg, SAMPLE, split_axis=0, concat_axis=0, tiled=True)  9.18 us
    pallas_call x1, Pallas kernels, body(): call(expand_kernel, pltpu.HBM((ITEMS, 2 * ROWS), BF), (2 * ITEMS * ROWS *...  8.75 us
    all_to_all x1, waiting for transfers between devices, body(): lax.all_to_all(msg, SAMPLE, split_axis=0, concat_axis=0, tiled=True)  7.96 us
    pallas_call x1, Pallas kernels, body(): call(attend_kernel, pltpu.HBM((PEERS, MSG, 128), BF), (2 * ITEMS * ROWS *...  7.39 us
  transfers between devices with their start and end apart: 14, of which 9 were waited for; matrix products, arithmetic and copies ran while one was open for 7% of the time, Pallas kernels for 23%

profile of v2, /device:TPU:1, one launch (start us, length us, event | category | flops | bytes accessed | tf_op | source)
XLA Modules:
  0.0 122.6 jit_solution(17802865283418291792)
XLA Ops:
  0.6 0.0 copy-start
  0.7 2.4 %shard_map.104 = (s32[32,128]{1,0:T(8,128)}, s32[32,128]{1,0:T(8,128)S(1)}) custom-call(s32[1,1024]{1,0:T(1,128)} %bitcast.45, s32[4,1024]{1,0:T(4,128)} %bitcast.44), custom_call_target="tpu_custom_call" | custom-call | flops 400000000 | bytes 1000000 | tf_op jit(solution)/shard_map/pallas_call | solution.py:326
  3.0 12.0 %all-to-all-start = ((s32[32,1,128]{2,1,0:T(1,128)}), s32[32,1,128]{2,1,0:T(1,128)S(1)}, u32[]{:S(2)}, u32[]{:S(2)}) async-start(s32[32,1,128]{2,1,0:T(1,128)} %bitcast.43), calls=%async_computation | async-start | bytes 32768 | tf_op jit(solution)/shard_map/all_to_all | solution.py:342
  15.1 3.3 %shard_map.110 = (bf16[640,1024]{1,0:T(8,128)(2,1)}, bf16[640,1024]{1,0:T(8,128)(2,1)}) custom-call(bf16[1024,512]{1,0:T(8,128)(2,1)} %up_ref.3, bf16[512,1024]{1,0:T(8,128)(2,1)} %down_ref.3, bf16[128,1024]{1,0:T(8,128)(2,1)} %refs_4_.1), custom_call_target="tpu_custom_call" | custom-call | bytes 5000000 | tf_op jit(solution)/shard_map/pallas_call | solution.py:331
  18.4 1.3 %collective-permute-start.3 = (bf16[640,1024]{1,0:T(8,128)(2,1)}, bf16[640,1024]{1,0:T(8,128)(2,1)}, u32[]{:S(2)}, u32[]{:S(2)}) collective-permute-start(bf16[640,1024]{1,0:T(8,128)(2,1)} %get-tuple-element.18), channel_id=1, source_target_pairs={{0,2},{2,4},{4,6},{6,0},{1,3},{3,5},{5,7},{7,1},{8,10},{10,12},{12... | collective-permute-start | bytes 3932168 | tf_op jit(solution)/shard_map/ppermute | solution.py:312
  19.7 1.5 %collective-permute-start.4 = (bf16[640,1024]{1,0:T(8,128)(2,1)}, bf16[640,1024]{1,0:T(8,128)(2,1)}, u32[]{:S(2)}, u32[]{:S(2)}) collective-permute-start(bf16[640,1024]{1,0:T(8,128)(2,1)} %get-tuple-element.19), channel_id=1, source_target_pairs={{0,6},{2,0},{4,2},{6,4},{1,7},{3,1},{5,3},{7,5},{8,14},{10,8},{12,... | collective-permute-start | bytes 3932168 | tf_op jit(solution)/shard_map/ppermute | solution.py:312
  21.1 0.5 fusion
  21.6 1.3 %fusion.9 = bf16[3,1024,128]{2,1,0:T(8,128)(2,1)S(1)} fusion(bf16[3,1024,128]{2,1,0:T(8,128)(2,1)S(1)} %copy-done, bf16[1024,1024]{1,0:T(8,128)(2,1)S(1)} %copy-done.1, f32[1024]{0:T(1024)S(1)} %add_rsqrt_fusion), kind=kOutput, calls=%fused_computation.10 | convolution fusion | flops 808845312 | bytes 3674112 | tf_op jit(solution)/shard_map/rd,tdc->trc/dot_general | solution.py:348
  22.9 1.0 slice_bitcast_fusion.3
  24.0 0.0 all-to-all-done
  24.0 2.6 %shard_map.105 = bf16[1536,128]{1,0:T(8,128)(2,1)} custom-call(s32[32,128]{1,0:T(8,128)S(1)} %bitcast.38, bf16[1024,128]{1,0:T(8,128)(2,1)S(1)} %get-tuple-element.34.q_ref), custom_call_target="tpu_custom_call" | custom-call | flops 402653184 | bytes 1000000 | tf_op jit(solution)/shard_map/pallas_call | solution.py:366
  26.6 9.2 %all-to-all-start.1 = ((bf16[32,48,128]{2,1,0:T(8,128)(2,1)}), bf16[32,48,128]{2,1,0:T(8,128)(2,1)S(1)}, u32[]{:S(2)}, u32[]{:S(2)}) async-start(bf16[32,48,128]{2,1,0:T(8,128)(2,1)} %bitcast.42), calls=%async_computation.1 | async-start | bytes 786432 | tf_op jit(solution)/shard_map/all_to_all | solution.py:377
  35.8 3.6 %copy_bitcast_fusion = (bf16[1024,1024]{1,0:T(8,128)(2,1)S(1)}, bf16[1024,1024]{1,0:T(8,128)(2,1)S(1)}) fusion(bf16[128,8,8,128]{3,2,1,0:T(8,128)(2,1)} %bitcast.40, bf16[128,8,8,128]{3,2,1,0:T(8,128)(2,1)} %bitcast.41), kind=kLoop, calls=%fused_computation.6 | loop fusion | bytes 8388608 | tf_op jit(solution)/shard_map/reshape | solution.py:352
  39.4 8.7 %shard_map.106.kv_ref = bf16[1536,2048]{1,0:T(8,128)(2,1)} custom-call(s32[32,128]{1,0:T(8,128)S(1)} %get-tuple-element.15.par_ref, bf16[1024,1024]{1,0:T(8,128)(2,1)S(1)} %get-tuple-element.36.k_ref, bf16[1024,1024]{1,0:T(8,128)(2,1)S(1)} %get-tuple-element.35.v_ref), custom_call_target="tpu_custom_call" | custom-call | flops 6442450944 | bytes 12000000 | tf_op jit(solution)/shard_map/pallas_call | solution.py:353
  48.2 0.2 all-to-all-done.1
  48.3 7.4 %shard_map.107 = bf16[32,64,128]{2,1,0:T(8,128)(2,1)} custom-call(bf16[1536,128]{1,0:T(8,128)(2,1)S(1)} %bitcast.37, bf16[1536,2048]{1,0:T(8,128)(2,1)} %shard_map.106.kv_ref), custom_call_target="tpu_custom_call" | custom-call | flops 402653184 | bytes 8000000 | tf_op jit(solution)/shard_map/pallas_call | solution.py:381
  55.7 9.2 %all-to-all-start.2 = ((bf16[32,64,128]{2,1,0:T(8,128)(2,1)}), bf16[32,64,128]{2,1,0:T(8,128)(2,1)}, u32[]{:S(2)}, u32[]{:S(2)}) async-start(bf16[32,64,128]{2,1,0:T(8,128)(2,1)} %shard_map.107), calls=%async_computation.2 | async-start | bytes 1048576 | tf_op jit(solution)/shard_map/all_to_all | solution.py:392
  64.9 1.8 %collective-permute-start.5 = (bf16[128,1024]{1,0:T(8,128)(2,1)S(1)}, bf16[128,1024]{1,0:T(8,128)(2,1)S(1)}, u32[]{:S(2)}, u32[]{:S(2)}) collective-permute-start(bf16[128,1024]{1,0:T(8,128)(2,1)S(1)} %copy-done.2), channel_id=1, source_target_pairs={{0,4},{2,6},{4,0},{6,2},{1,5},{3,7},{5,1},{7,3},{8,12},{10,14},{12... | collective-permute-start | bytes 786440 | tf_op jit(solution)/shard_map/ppermute | solution.py:312
  66.7 0.7 pad_add_fusion.info_ref
  67.4 0.9 copy-done.4
  68.3 0.9 copy-done.6
  69.3 1.9 %shard_map.108.place_ref = f32[1024,128]{1,0:T(8,128)} custom-call(s32[32,128]{1,0:T(8,128)S(1)} %bitcast.39, bf16[1024,128]{1,0:T(8,128)(2,1)S(1)} %copy-done.6, bf16[1024,128]{1,0:T(8,128)(2,1)S(1)} %copy-done.4), custom_call_target="tpu_custom_call" | custom-call | flops 1000000000 | bytes 2000000 | tf_op jit(solution)/shard_map/pallas_call | solution.py:379
  71.2 8.0 %all-to-all-done.2.msg_ref = bf16[32,64,128]{2,1,0:T(8,128)(2,1)} async-done(((bf16[32,64,128]{2,1,0:T(8,128)(2,1)}), bf16[32,64,128]{2,1,0:T(8,128)(2,1)}, u32[]{:S(2)}, u32[]{:S(2)}) %all-to-all-start.2) | async-done | bytes 524320 | tf_op jit(solution)/shard_map/all_to_all | solution.py:392
  79.1 0.9 copy-done.3
  80.1 0.7 copy-done.7
  80.8 3.6 %shard_map.109 = (bf16[512,128]{1,0:T(8,128)(2,1)S(1)}, bf16[512,128]{1,0:T(8,128)(2,1)S(1)}) custom-call(s32[3]{0:T(128)S(1)} %copy-done.7, bf16[32,64,128]{2,1,0:T(8,128)(2,1)} %all-to-all-done.2.msg_ref, f32[1024,128]{1,0:T(8,128)} %shard_map.108.place_ref, bf16[1024,128]{1,0:T(8,128)(2,1)S(1)} %copy-done.3), custom_call_target="tpu_custom_call" | custom-call | flops 402653184 | bytes 5000000 | tf_op jit(solution)/shard_map/pallas_call | solution.py:397
  84.4 0.1 collective-permute-start
  84.5 2.6 %collective-permute-start.1 = (bf16[512,128]{1,0:T(8,128)(2,1)S(1)}, bf16[512,128]{1,0:T(8,128)(2,1)S(1)}, u32[]{:S(2)}, u32[]{:S(2)}) collective-permute-start(bf16[512,128]{1,0:T(8,128)(2,1)S(1)} %get-tuple-element.17), channel_id=1, source_target_pairs={{0,6},{2,0},{4,2},{6,4},{1,7},{3,1},{5,3},{7,5},{8,14},{10,8},{12,... | collective-permute-start | bytes 393224 | tf_op jit(solution)/shard_map/ppermute | solution.py:312
  87.2 0.3 collective-permute-start.2
  87.5 2.0 %collective-permute-done.refs_1_ = bf16[512,128]{1,0:T(8,128)(2,1)S(1)} collective-permute-done((bf16[512,128]{1,0:T(8,128)(2,1)S(1)}, bf16[512,128]{1,0:T(8,128)(2,1)S(1)}, u32[]{:S(2)}, u32[]{:S(2)}) %collective-permute-start) | collective-permute-done | bytes 131104 | tf_op jit(solution)/shard_map/ppermute | solution.py:312
  89.5 1.0 collective-permute-done.1.refs_2_
  90.5 2.0 %collective-permute-done.2.refs_3_ = bf16[512,128]{1,0:T(8,128)(2,1)S(1)} collective-permute-done((bf16[512,128]{1,0:T(8,128)(2,1)S(1)}, bf16[512,128]{1,0:T(8,128)(2,1)S(1)}, u32[]{:S(2)}, u32[]{:S(2)}) %collective-permute-start.2) | collective-permute-done | bytes 131104 | tf_op jit(solution)/shard_map/ppermute | solution.py:312
  92.5 2.3 %shard_map.111.p_ref = bf16[512,1024]{1,0:T(8,128)(2,1)S(1)} custom-call(s32[3]{0:T(128)S(1)} %copy-done.7, bf16[512,128]{1,0:T(8,128)(2,1)S(1)} %get-tuple-element.16.refs_0_, bf16[512,128]{1,0:T(8,128)(2,1)S(1)} %collective-permute-done.refs_1_, bf16[512,128]{1,0:T(8,128)(2,1)S(1)} %collective-permute-done.1.refs_2_, ...), custom_call_target="tpu_custom_call" | custom-call | flops 600000000 | bytes 3000000 | tf_op jit(solution)/shard_map/pallas_call | solution.py:409
  94.8 0.0 copy-start.9
  94.8 6.5 %collective-permute-start.6 = (bf16[512,1024]{1,0:T(8,128)(2,1)S(1)}, bf16[512,1024]{1,0:T(8,128)(2,1)S(1)}, u32[]{:S(2)}, u32[]{:S(2)}) collective-permute-start(bf16[512,1024]{1,0:T(8,128)(2,1)S(1)} %shard_map.111.p_ref), channel_id=1, source_target_pairs={{0,1},{1,0},{2,3},{3,2},{4,5},{5,4},{6,7},{7,6},{8,9},{9,8},{10,11... | collective-permute-start | bytes 3145736 | tf_op jit(solution)/shard_map/ppermute | solution.py:312
  101.3 2.3 %collective-permute-done.6.r_ref = bf16[512,1024]{1,0:T(8,128)(2,1)S(1)} collective-permute-done((bf16[512,1024]{1,0:T(8,128)(2,1)S(1)}, bf16[512,1024]{1,0:T(8,128)(2,1)S(1)}, u32[]{:S(2)}, u32[]{:S(2)}) %collective-permute-start.6) | collective-permute-done | bytes 1048608 | tf_op jit(solution)/shard_map/ppermute | solution.py:312
  103.6 6.2 %shard_map.112 = (f32[4,512,128]{2,1,0:T(8,128)S(1)}, bf16[4,512,128]{2,1,0:T(8,128)(2,1)S(1)}) custom-call(s32[3]{0:T(128)S(1)} %copy-done.7, bf16[1024,1024]{1,0:T(8,128)(2,1)S(1)} %copy-done.1, bf16[1024,1024]{1,0:T(8,128)(2,1)S(1)} %copy-done.1, bf16[512,1024]{1,0:T(8,128)(2,1)S(1)} %shard_map.111.p_ref, ...), custom_call_target="tpu_custom_call" | custom-call | flops 2000000000 | bytes 10000000 | tf_op jit(solution)/shard_map/pallas_call | solution.py:422
  109.8 0.5 collective-permute-start.7
  110.3 1.5 %collective-permute-done.7.other_ref = bf16[4,512,128]{2,1,0:T(8,128)(2,1)S(1)} collective-permute-done((bf16[4,512,128]{2,1,0:T(8,128)(2,1)S(1)}, bf16[4,512,128]{2,1,0:T(8,128)(2,1)S(1)}, u32[]{:S(2)}, u32[]{:S(2)}) %collective-permute-start.7) | collective-permute-done | bytes 524320 | tf_op jit(solution)/shard_map/ppermute | solution.py:312
  111.8 0.1 shard_map.113
  111.9 0.9 collective-permute-start.10
  112.8 0.6 collective-permute-start.8
  113.5 0.6 collective-permute-start.9
  114.1 0.1 pad_maximum_fusion
  114.2 1.3 %copy.13 = bf16[1024,2,128]{2,1,0:T(2,128)(2,1)} copy(bf16[1024,2,128]{2,0,1:T(8,128)(2,1)S(1)} %pad_maximum_fusion) | data formatting | bytes 1048576
  115.5 1.2 collective-permute-done.10.p3
  116.7 4.6 %collective-permute-done.8.p1 = bf16[512,128]{1,0:T(8,128)(2,1)S(1)} collective-permute-done((bf16[512,128]{1,0:T(8,128)(2,1)S(1)}, bf16[512,128]{1,0:T(8,128)(2,1)S(1)}, u32[]{:S(2)}, u32[]{:S(2)}) %collective-permute-start.8) | collective-permute-done | bytes 131104 | tf_op jit(solution)/shard_map/ppermute | solution.py:312
  121.3 1.3 %shard_map.114 = bf16[1024,128]{1,0:T(8,128)(2,1)} custom-call(s32[3]{0:T(128)S(1)} %copy-done.8, bf16[512,128]{1,0:T(8,128)(2,1)S(1)} %get-tuple-element.22.p0, bf16[512,128]{1,0:T(8,128)(2,1)S(1)} %collective-permute-done.8.p1, bf16[512,128]{1,0:T(8,128)(2,1)S(1)} %collective-permute-done.9.p2, bf16[512,128]{1,0:T(8,128)(2,1)S(1)} %collective-permute-done.10.p3), custom_call_target="tpu_custom_call" | custom-call | flops 1000000 | bytes 500000 | tf_op jit(solution)/shard_map/pallas_call | solution.py:451
  (21 shorter events, 0.0 us)
Async XLA Ops:
  0.6 21.0 %copy-start = (bf16[3,1024,128]{2,1,0:T(8,128)(2,1)S(1)}, bf16[3,1024,128]{2,1,0:T(8,128)(2,1)}, u32[]{:S(2)}) copy-start(bf16[3,1024,128]{2,1,0:T(8,128)(2,1)} %param.14) | copy-start | bytes 2359300
  0.6 20.5 %copy-start.1 = (bf16[1024,1024]{1,0:T(8,128)(2,1)S(1)}, bf16[1024,1024]{1,0:T(8,128)(2,1)}, u32[]{:S(2)}) copy-start(bf16[1024,1024]{1,0:T(8,128)(2,1)} %x1_ref.1) | copy-start | bytes 6291460
  3.0 21.0 %all-to-all-start = ((s32[32,1,128]{2,1,0:T(1,128)}), s32[32,1,128]{2,1,0:T(1,128)S(1)}, u32[]{:S(2)}, u32[]{:S(2)}) async-start(s32[32,1,128]{2,1,0:T(1,128)} %bitcast.43), calls=%async_computation | async-start | bytes 32768 | tf_op jit(solution)/shard_map/all_to_all | solution.py:342
  18.4 69.1 %collective-permute-start.3 = (bf16[640,1024]{1,0:T(8,128)(2,1)}, bf16[640,1024]{1,0:T(8,128)(2,1)}, u32[]{:S(2)}, u32[]{:S(2)}) collective-permute-start(bf16[640,1024]{1,0:T(8,128)(2,1)} %get-tuple-element.18), channel_id=1, source_target_pairs={{0,2},{2,4},{4,6},{6,0},{1,3},{3,5},{5,7},{7,1},{8,10},{10,12},{12... | collective-permute-start | bytes 3932168 | tf_op jit(solution)/shard_map/ppermute | solution.py:312
  19.7 67.9 %collective-permute-start.4 = (bf16[640,1024]{1,0:T(8,128)(2,1)}, bf16[640,1024]{1,0:T(8,128)(2,1)}, u32[]{:S(2)}, u32[]{:S(2)}) collective-permute-start(bf16[640,1024]{1,0:T(8,128)(2,1)} %get-tuple-element.19), channel_id=1, source_target_pairs={{0,6},{2,0},{4,2},{6,4},{1,7},{3,1},{5,3},{7,5},{8,14},{10,8},{12,... | collective-permute-start | bytes 3932168 | tf_op jit(solution)/shard_map/ppermute | solution.py:312
  24.0 2.7 %copy-start.5 = (bf16[1024,128]{1,0:T(8,128)(2,1)}, bf16[1024,128]{1,0:T(8,128)(2,1)S(1)}, u32[]{:S(2)}) copy-start(bf16[1024,128]{1,0:T(8,128)(2,1)S(1)} %get-tuple-element.34.q_ref) | copy-start | bytes 786436
  26.6 21.7 %all-to-all-start.1 = ((bf16[32,48,128]{2,1,0:T(8,128)(2,1)}), bf16[32,48,128]{2,1,0:T(8,128)(2,1)S(1)}, u32[]{:S(2)}, u32[]{:S(2)}) async-start(bf16[32,48,128]{2,1,0:T(8,128)(2,1)} %bitcast.42), calls=%async_computation.1 | async-start | bytes 786432 | tf_op jit(solution)/shard_map/all_to_all | solution.py:377
  48.3 16.6 %copy-start.2 = (bf16[128,1024]{1,0:T(8,128)(2,1)S(1)}, bf16[128,1024]{1,0:T(8,128)(2,1)}, u32[]{:S(2)}) copy-start(bf16[128,1024]{1,0:T(8,128)(2,1)} %refs_4_.1) | copy-start | bytes 786436
  55.7 23.4 %all-to-all-start.2 = ((bf16[32,64,128]{2,1,0:T(8,128)(2,1)}), bf16[32,64,128]{2,1,0:T(8,128)(2,1)}, u32[]{:S(2)}, u32[]{:S(2)}) async-start(bf16[32,64,128]{2,1,0:T(8,128)(2,1)} %shard_map.107), calls=%async_computation.2 | async-start | bytes 1048576 | tf_op jit(solution)/shard_map/all_to_all | solution.py:392
  64.9 22.2 %collective-permute-start.5 = (bf16[128,1024]{1,0:T(8,128)(2,1)S(1)}, bf16[128,1024]{1,0:T(8,128)(2,1)S(1)}, u32[]{:S(2)}, u32[]{:S(2)}) collective-permute-start(bf16[128,1024]{1,0:T(8,128)(2,1)S(1)} %copy-done.2), channel_id=1, source_target_pairs={{0,4},{2,6},{4,0},{6,2},{1,5},{3,7},{5,1},{7,3},{8,12},{10,14},{12... | collective-permute-start | bytes 786440 | tf_op jit(solution)/shard_map/ppermute | solution.py:312
  67.4 0.9 copy-start.4
  68.3 0.9 copy-start.6
  79.1 1.0 copy-start.3
  80.1 0.7 copy-start.7
  84.4 5.1 %collective-permute-start = (bf16[512,128]{1,0:T(8,128)(2,1)S(1)}, bf16[512,128]{1,0:T(8,128)(2,1)S(1)}, u32[]{:S(2)}, u32[]{:S(2)}) collective-permute-start(bf16[512,128]{1,0:T(8,128)(2,1)S(1)} %get-tuple-element.17), channel_id=1, source_target_pairs={{0,2},{2,4},{4,6},{6,0},{1,3},{3,5},{5,7},{7,1},{8,10},{10,12},{12... | collective-permute-start | bytes 393224 | tf_op jit(solution)/shard_map/ppermute | solution.py:312
  84.5 6.0 %collective-permute-start.1 = (bf16[512,128]{1,0:T(8,128)(2,1)S(1)}, bf16[512,128]{1,0:T(8,128)(2,1)S(1)}, u32[]{:S(2)}, u32[]{:S(2)}) collective-permute-start(bf16[512,128]{1,0:T(8,128)(2,1)S(1)} %get-tuple-element.17), channel_id=1, source_target_pairs={{0,6},{2,0},{4,2},{6,4},{1,7},{3,1},{5,3},{7,5},{8,14},{10,8},{12,... | collective-permute-start | bytes 393224 | tf_op jit(solution)/shard_map/ppermute | solution.py:312
  87.2 5.3 %collective-permute-start.2 = (bf16[512,128]{1,0:T(8,128)(2,1)S(1)}, bf16[512,128]{1,0:T(8,128)(2,1)S(1)}, u32[]{:S(2)}, u32[]{:S(2)}) collective-permute-start(bf16[512,128]{1,0:T(8,128)(2,1)S(1)} %get-tuple-element.16.refs_0_), channel_id=1, source_target_pairs={{0,4},{2,6},{4,0},{6,2},{1,5},{3,7},{5,1},{7,3},{8,12},{10,14},{12... | collective-permute-start | bytes 393224 | tf_op jit(solution)/shard_map/ppermute | solution.py:312
  94.8 19.3 %copy-start.9 = (bf16[1024,1,128]{2,0,1:T(8,128)(2,1)S(1)}, bf16[1024,1,128]{2,0,1:T(8,128)(2,1)}, u32[]{:S(2)}) copy-start(bf16[1024,1,128]{2,0,1:T(8,128)(2,1)} %get-tuple-element.30) | copy-start | bytes 786436
  94.8 19.3 %copy-start.10 = (bf16[1024,1,128]{2,0,1:T(8,128)(2,1)S(1)}, bf16[1024,1,128]{2,0,1:T(8,128)(2,1)}, u32[]{:S(2)}) copy-start(bf16[1024,1,128]{2,0,1:T(8,128)(2,1)} %get-tuple-element.31) | copy-start | bytes 786436
  94.8 8.8 %collective-permute-start.6 = (bf16[512,1024]{1,0:T(8,128)(2,1)S(1)}, bf16[512,1024]{1,0:T(8,128)(2,1)S(1)}, u32[]{:S(2)}, u32[]{:S(2)}) collective-permute-start(bf16[512,1024]{1,0:T(8,128)(2,1)S(1)} %shard_map.111.p_ref), channel_id=1, source_target_pairs={{0,1},{1,0},{2,3},{3,2},{4,5},{5,4},{6,7},{7,6},{8,9},{9,8},{10,11... | collective-permute-start | bytes 3145736 | tf_op jit(solution)/shard_map/ppermute | solution.py:312
  109.8 11.5 %copy-start.8 = (s32[3]{0:T(128)S(1)}, s32[3]{0:T(128)}, u32[]{:S(2)}) copy-start(s32[3]{0:T(128)} %pad_add_fusion.info_ref) | copy-start | bytes 40
  109.8 2.0 %collective-permute-start.7 = (bf16[4,512,128]{2,1,0:T(8,128)(2,1)S(1)}, bf16[4,512,128]{2,1,0:T(8,128)(2,1)S(1)}, u32[]{:S(2)}, u32[]{:S(2)}) collective-permute-start(bf16[4,512,128]{2,1,0:T(8,128)(2,1)S(1)} %get-tuple-element.21), channel_id=1, source_target_pairs={{0,1},{1,0},{2,3},{3,2},{4,5},{5,4},{6,7},{7,6},{8,9},{9,8},{10,11... | collective-permute-start | bytes 1572872 | tf_op jit(solution)/shard_map/ppermute | solution.py:312
  111.9 4.8 %collective-permute-start.10 = (bf16[512,128]{1,0:T(8,128)(2,1)S(1)}, bf16[512,128]{1,0:T(8,128)(2,1)S(1)}, u32[]{:S(2)}, u32[]{:S(2)}) collective-permute-start(bf16[512,128]{1,0:T(8,128)(2,1)S(1)} %get-tuple-element.25), channel_id=1, source_target_pairs={{0,6},{2,0},{4,2},{6,4},{1,7},{3,1},{5,3},{7,5},{8,14},{10,8},{12,... | collective-permute-start | bytes 393224 | tf_op jit(solution)/shard_map/ppermute | solution.py:312
  112.8 8.5 %collective-permute-start.8 = (bf16[512,128]{1,0:T(8,128)(2,1)S(1)}, bf16[512,128]{1,0:T(8,128)(2,1)S(1)}, u32[]{:S(2)}, u32[]{:S(2)}) collective-permute-start(bf16[512,128]{1,0:T(8,128)(2,1)S(1)} %get-tuple-element.23), channel_id=1, source_target_pairs={{0,2},{2,4},{4,6},{6,0},{1,3},{3,5},{5,7},{7,1},{8,10},{10,12},{12... | collective-permute-start | bytes 393224 | tf_op jit(solution)/shard_map/ppermute | solution.py:312
  113.5 7.8 %collective-permute-start.9 = (bf16[512,128]{1,0:T(8,128)(2,1)S(1)}, bf16[512,128]{1,0:T(8,128)(2,1)S(1)}, u32[]{:S(2)}, u32[]{:S(2)}) collective-permute-start(bf16[512,128]{1,0:T(8,128)(2,1)S(1)} %get-tuple-element.24), channel_id=1, source_target_pairs={{0,4},{2,6},{4,0},{6,2},{1,5},{3,7},{5,1},{7,3},{8,12},{10,14},{12... | collective-permute-start | bytes 393224 | tf_op jit(solution)/shard_map/ppermute | solution.py:312

commit v3 on v2

--- a/solution.py
+++ b/solution.py
@@ -13,6 +13,9 @@
 ROWS = 1024
 ITEMS = PEERS * CAP
 MSG = 64
+LOW = 16
+FULL = PEERS // 2
+REST = CAP - LOW
 SAMPLE = ("z", "y")
 HEAD = ("x", "core")
 F32 = jnp.float32
@@ -43,7 +46,20 @@
     return jax.ShapeDtypeStruct(shape, dtype)
 
 
-def plan_kernel(cnt_ref, slot_ref, send_ref, par_ref):
+def full_peers(last):
+    rows, cols = iota((PEERS, PEERS), 0), iota((PEERS, PEERS), 1)
+    order = jnp.sum(jnp.where(rows < cols, last, 0.0), axis=0, keepdims=True)
+    flag = jnp.sum(jnp.where(rows == cols, last, 0.0), axis=0, keepdims=True)
+    hit = iota((FULL, PEERS), 0).astype(F32) == order
+    return jnp.where(hit, flag, 0.0).astype(BF)
+
+
+def peer_numbers(chosen):
+    numbers = iota((PEERS, 128), 0).astype(F32).astype(BF)
+    return jnp.dot(chosen, numbers, preferred_element_type=F32).astype(jnp.int32)
+
+
+def plan_kernel(cnt_ref, slot_ref, send_ref, par_ref, full_ref):
     width = 256
     blocks = ROWS // width
     cnt = cnt_ref[...]
@@ -84,10 +100,17 @@
     whole = total.astype(jnp.int32)
     have = whole[2 * PEERS : 3 * PEERS] > 0
     send = jnp.where(have, whole[:PEERS] * 32 + whole[PEERS : 2 * PEERS], -1)
-    pars = jnp.where(have, whole[3 * PEERS : 4 * PEERS] * 32 + whole[4 * PEERS :], -1)
     fill = jnp.full((PEERS, 128 - CAP), -1, jnp.int32)
     send_ref[...] = jnp.concatenate([send, fill], axis=1)
-    par_ref[...] = jnp.concatenate([pars, fill], axis=1)
+    chosen = full_peers(jnp.where(have[:, CAP - 1 :], 1.0, 0.0))
+    full_ref[...] = peer_numbers(chosen)
+    high, low = total[3 * PEERS : 4 * PEERS], total[4 * PEERS :]
+    rest = 32.0 * jnp.dot(chosen, high.astype(BF), preferred_element_type=F32)
+    rest = rest + jnp.dot(chosen, low.astype(BF), preferred_element_type=F32)
+    par_ref[:PEERS, :LOW] = high[:, :LOW] * 32.0 + low[:, :LOW]
+    par_ref[:PEERS, LOW:] = jnp.zeros((PEERS, 128 - LOW), F32)
+    par_ref[PEERS:, :REST] = rest[:, LOW:]
+    par_ref[PEERS:, REST:] = jnp.zeros((FULL, 128 - REST), F32)
 
 
 def pack_kernel(up_ref, down_ref, wo_ref, right_ref, left_ref, stage, sems):
@@ -124,10 +147,20 @@
     return jnp.sum(picked, axis=2, keepdims=True).reshape(count * depth, 1)
 
 
-def expand_kernel(par_ref, k_ref, v_ref, out_ref):
-    peers = par_ref.shape[0]
-    col = column(par_ref[...].astype(F32), peers, CAP)
-    hot = (col == iota((peers * CAP, ROWS), 1).astype(F32)).astype(F32).astype(BF)
+def expand_kernel(par_ref, k_ref, v_ref, out_ref, col_ref):
+    step = pl.program_id(0)
+
+    @pl.when(step < 2)
+    def _():
+        lists = par_ref[pl.ds(pl.multiple_of(step * 16, 16), 16), :]
+        col_ref[...] = jnp.broadcast_to(column(lists, 16, LOW), (256, 128))
+
+    @pl.when(step >= 2)
+    def _():
+        lists = par_ref[pl.ds(pl.multiple_of(PEERS + (step - 2) * 8, 8), 8), :]
+        col_ref[...] = jnp.broadcast_to(column(lists, 8, REST), (256, 128))
+
+    hot = (col_ref[:, 0:1] == iota((256, ROWS), 1).astype(F32)).astype(F32).astype(BF)
     out_ref[:, :ROWS] = jnp.dot(hot, k_ref[...], preferred_element_type=F32).astype(BF)
     out_ref[:, ROWS:] = jnp.dot(hot, v_ref[...], preferred_element_type=F32).astype(BF)
 
@@ -139,36 +172,56 @@
     out_ref[...] = jnp.dot(hot, q_ref[...], preferred_element_type=F32).astype(BF)
 
 
-def place_kernel(recv_ref, q_ref, k_ref, out_ref):
+def place_kernel(recv_ref, q_ref, k_ref, out_ref, full_ref):
     slot = recv_ref[...]
+    last = jnp.where(slot[:, CAP - 1 : CAP] >= 0, 1.0, 0.0)
+    full_ref[...] = peer_numbers(full_peers(last))
+    below = iota((PEERS, PEERS), 1) < iota((PEERS, PEERS), 0)
+    order = jnp.dot(
+        below.astype(F32).astype(BF),
+        jnp.broadcast_to(last, (PEERS, 128)).astype(BF),
+        preferred_element_type=F32,
+    )
     high = jnp.where(slot >= 0, slot // 32, -1)
     low = slot % 32
-    acc = jnp.zeros((64, 32), F32)
+    acc = jnp.zeros((96, 32), F32)
     where_c = iota((32, 128), 1).astype(F32)
     for s in range(PEERS):
         a = (iota((32, 128), 0) == high[s : s + 1, :]).astype(F32)
         b = (iota((32, 128), 0) == low[s : s + 1, :]).astype(F32).astype(BF)
-        left = jnp.concatenate([a * float(s), a * where_c], axis=0).astype(BF)
-        acc = acc + lax.dot_general(left, b, NT, preferred_element_type=F32)
-    wide = jnp.concatenate([acc, jnp.zeros((64, 96), F32)], axis=1)
-    src = column(wide[:32], 32, 32)
-    place = column(wide[32:], 32, 32)
+        left = jnp.concatenate([a * float(s), a * where_c, a * order[s : s + 1]], axis=0)
+        acc = acc + lax.dot_general(left.astype(BF), b, NT, preferred_element_type=F32)
+    wide = jnp.concatenate([acc, jnp.zeros((96, 96), F32)], axis=1)
+    src, place, rank = (column(wide[n * 32 : n * 32 + 32], 32, 32) for n in range(3))
+    rest = float(PEERS * LOW - LOW) + rank * float(REST) + place
+    pos = jnp.where(place < float(LOW), src * float(LOW) + place, rest)
     prod = q_ref[...].astype(F32) * k_ref[...].astype(F32) * (1.0 / HD**0.5)
     s0 = jnp.sum(prod[:, :HD], axis=1, keepdims=True)
     s1 = jnp.sum(prod[:, HD:], axis=1, keepdims=True)
     lane = iota((ROWS, 128), 1)
-    out_ref[...] = jnp.where(
-        lane == 0, src, jnp.where(lane == 1, place, jnp.where(lane == 2, s0, s1))
-    )
-
-
-def attend_kernel(q_ref, kv_ref, out_ref):
-    n = q_ref.shape[0]
-    peers = n // CAP
+    known = jnp.where(lane == 0, src, jnp.where(lane == 1, place, pos))
+    out_ref[...] = jnp.where(lane == 3, s0, jnp.where(lane == 4, s1, known))
+
+
+def attend_kernel(full_ref, q_ref, kv_ref, out_ref, rows_ref):
+    n = 256
+    step = pl.program_id(0)
+
+    @pl.when(step < 2)
+    def _():
+        rows_ref[...] = q_ref[pl.ds(step * 16, 16), :LOW, :].reshape(n, 128)
+
+    @pl.when(step >= 2)
+    def _():
+        for k in range(8):
+            peer = full_ref[(step - 2) * 8 + k, 0]
+            rows = q_ref[pl.ds(peer, 1), LOW:, :].reshape(REST, 128)
+            rows_ref[k * REST : (k + 1) * REST, :] = rows
+
     sel_p = iota((16, ROWS), 1) // 128
     sel_h = (iota((16, ROWS), 1) % 128) // HD
     sel = (iota((16, ROWS), 0) == sel_h * 8 + sel_p).astype(F32).astype(BF)
-    q = q_ref[...].astype(F32)
+    q = rows_ref[...].astype(F32)
     highs, lows = [], []
     for p in range(8):
         prod = q * kv_ref[:, p * 128 : (p + 1) * 128].astype(F32)
@@ -180,7 +233,7 @@
         sel, jnp.concatenate(lows, axis=1), NT, preferred_element_type=F32
     )
     score = score * (1.0 / HD**0.5)
-    weights, rows = [], []
+    weights, parts = [], []
     for h in range(2):
         part = score[h * 8 : (h + 1) * 8]
         top = jnp.max(part, axis=0, keepdims=True)
@@ -190,7 +243,7 @@
         lse = top + jnp.log(norm)
         for _ in range(3):
             piece = lse.astype(BF).astype(F32)
-            rows.append(piece)
+            parts.append(piece)
             lse = lse - piece
     weight = jnp.concatenate(weights, axis=0).astype(BF)
     wide = lax.dot_general(weight, sel, TN, preferred_element_type=F32)
@@ -199,18 +252,41 @@
         ctx = ctx + wide[:, p * 128 : (p + 1) * 128] * kv_ref[
             :, ROWS + p * 128 : ROWS + (p + 1) * 128
         ].astype(F32)
-    out_ref[:, :CAP, :] = ctx.astype(BF).reshape(peers, CAP, 128)
-    tail = jnp.concatenate(rows + [jnp.zeros((10, n), F32)], axis=0)
-    for o in range(peers):
-        piece = tail[:, o * CAP : (o + 1) * CAP]
-        piece = jnp.concatenate([piece, jnp.zeros((16, 128 - CAP), F32)], axis=1)
-        out_ref[o, CAP:, :] = piece.astype(BF)
-
-
-def merge_kernel(info_ref, msg_ref, place_ref, v_ref, mine_ref, theirs_ref):
+    ctx = ctx.astype(BF)
+    tail = jnp.concatenate(parts + [jnp.zeros((10, n), F32)], axis=0)
+
+    @pl.when(step < 2)
+    def _():
+        peers = pl.ds(step * 16, 16)
+        out_ref[peers, :LOW, :] = ctx.reshape(16, LOW, 128)
+        out_ref[peers, LOW:CAP, :] = jnp.zeros((16, REST, 128), BF)
+        for k in range(16):
+            piece = tail[:, k * LOW : (k + 1) * LOW]
+            piece = jnp.concatenate([piece, jnp.zeros((16, 128 - LOW), F32)], axis=1)
+            out_ref[pl.ds(step * 16 + k, 1), CAP:, :] = piece.astype(BF).reshape(1, 16, 128)
+
+    @pl.when(step >= 2)
+    def _():
+        for k in range(8):
+            peer = pl.ds(full_ref[(step - 2) * 8 + k, 0], 1)
+            rows = ctx[k * REST : (k + 1) * REST].reshape(1, REST, 128)
+            out_ref[peer, LOW:CAP, :] = rows
+            piece = tail[:, k * REST : (k + 1) * REST]
+            before, after = jnp.zeros((16, LOW), F32), jnp.zeros((16, 128 - CAP), F32)
+            piece = jnp.concatenate([before, piece, after], axis=1).astype(BF)
+            out_ref[peer, CAP:, :] = out_ref[peer, CAP:, :] + piece.reshape(1, 16, 128)
+
+
+def merge_kernel(
+    info_ref, full_ref, msg_ref, place_ref, v_ref, mine_ref, theirs_ref, ctx_ref
+):
     rows = 256
+    low = PEERS * LOW
+    ctx_ref[:low, :] = msg_ref[:, :LOW, :].reshape(low, 128)
+    for k in range(FULL):
+        got = msg_ref[pl.ds(full_ref[k, 0], 1), LOW:CAP, :].reshape(REST, 128)
+        ctx_ref[low + k * REST : low + (k + 1) * REST, :] = got
     outs = [r.at[pl.ds(n * rows, rows)] for r in (mine_ref, theirs_ref) for n in range(2)]
-    ctx_all = msg_ref[:, :CAP, :].reshape(ITEMS, 128)
     parts = []
     for h in range(2):
         for j in range(3):
@@ -223,9 +299,8 @@
         src, place = known[:, 0:1], known[:, 1:2]
         lane = iota((rows, 128), 1)
         lanes = lane.astype(F32)
-        pos = src * float(CAP) + place
-        hot = (iota((rows, ITEMS), 1).astype(F32) == pos).astype(F32).astype(BF)
-        ctx = jnp.dot(hot, ctx_all, preferred_element_type=F32)
+        hot = (iota((rows, ROWS), 1).astype(F32) == known[:, 2:3]).astype(F32).astype(BF)
+        ctx = jnp.dot(hot, ctx_ref[...], preferred_element_type=F32)
         from_src = (iota((rows, PEERS), 1).astype(F32) == src).astype(F32).astype(BF)
         lists = jnp.dot(from_src, parts, preferred_element_type=F32)
         cols = []
@@ -236,7 +311,7 @@
             lse = jnp.where(lanes == place, lse, 0.0)
             cols.append(jnp.sum(lse, axis=1, keepdims=True))
         lse = jnp.where(lane < HD, cols[0], cols[1])
-        own = jnp.where(lane < HD, known[:, 2:3], known[:, 3:4])
+        own = jnp.where(lane < HD, known[:, 3:4], known[:, 4:5])
         top = jnp.maximum(lse, own)
         a = jnp.exp(lse - top)
         b = jnp.exp(own - top)
@@ -321,11 +396,15 @@
     hbm = pl.BlockSpec(memory_space=pltpu.HBM)
     x = lax.axis_index("x")
     core = lax.axis_index("core")
-    info = jnp.stack([x, x % 2, core]).astype(jnp.int32)
-
-    send, par = call(
+    info = keep(jnp.stack([x, x % 2, core]).astype(jnp.int32), pltpu.HBM)
+
+    send, par, my_full = call(
         plan_kernel,
-        (pltpu.HBM((PEERS, 128), jnp.int32), pltpu.VMEM((PEERS, 128), jnp.int32)),
+        (
+            pltpu.HBM((PEERS, 128), jnp.int32),
+            pltpu.HBM((PEERS + FULL, 128), F32),
+            pltpu.HBM((FULL, 128), jnp.int32),
+        ),
         (4 * 10**8, 10**6),
     )(keep(counts.reshape(1, ROWS), pltpu.HBM), keep(slots.T, pltpu.HBM))
     for_right, for_left = call(
@@ -352,16 +431,17 @@
     flat_keys, flat_values = keys.reshape(ROWS, ROWS), values.reshape(ROWS, ROWS)
     kv = call(
         expand_kernel,
-        pltpu.HBM((ITEMS, 2 * ROWS), BF),
-        (2 * ITEMS * ROWS * ROWS * 2, 12 * 10**6),
+        pltpu.HBM((ROWS, 2 * ROWS), BF),
+        (2 * ROWS * ROWS * ROWS * 2, 12 * 10**6),
         grid=(4,),
         in_specs=[
-            pl.BlockSpec((8, 128), lambda i: (i, 0)),
+            pl.BlockSpec((PEERS + FULL, 128), lambda i: (0, 0)),
             pl.BlockSpec((ROWS, ROWS), lambda i: (0, 0)),
             pl.BlockSpec((ROWS, ROWS), lambda i: (0, 0)),
         ],
-        out_specs=pl.BlockSpec((8 * CAP, 2 * ROWS), lambda i: (i, 0)),
-    )(keep(par), flat_keys, flat_values)
+        out_specs=pl.BlockSpec((256, 2 * ROWS), lambda i: (i, 0)),
+        scratch_shapes=[pltpu.VMEM((256, 128), F32)],
+    )(keep(par, pltpu.HBM), flat_keys, flat_values)
 
     q_send = call(
         query_kernel,
@@ -376,31 +456,38 @@
     )(recv, query)
     q_recv = lax.all_to_all(q_send, SAMPLE, split_axis=0, concat_axis=0, tiled=True)
 
-    places = call(place_kernel, pltpu.HBM((ROWS, 128), F32), (10**9, 2 * 10**6))(recv, query, own_key)
+    smem = pl.BlockSpec(memory_space=pltpu.SMEM)
+    places, your_full = call(
+        place_kernel,
+        (pltpu.HBM((ROWS, 128), F32), pltpu.HBM((FULL, 128), jnp.int32)),
+        (10**9, 2 * 10**6),
+    )(recv, keep(query, pltpu.HBM), keep(own_key, pltpu.HBM))
 
     msg = call(
         attend_kernel,
         pltpu.HBM((PEERS, MSG, 128), BF),
-        (2 * ITEMS * ROWS * 128, 8 * 10**6),
+        (2 * ROWS * ROWS * 128, 8 * 10**6),
         grid=(4,),
         in_specs=[
-            pl.BlockSpec((8 * CAP, 128), lambda i: (i, 0)),
-            pl.BlockSpec((8 * CAP, 2 * ROWS), lambda i: (i, 0)),
+            smem,
+            pl.BlockSpec((PEERS, CAP, 128), lambda i: (0, 0, 0)),
+            pl.BlockSpec((256, 2 * ROWS), lambda i: (i, 0)),
         ],
-        out_specs=pl.BlockSpec((8, MSG, 128), lambda i: (i, 0, 0)),
-    )(q_recv, keep(kv, pltpu.HBM))
+        out_specs=pl.BlockSpec((PEERS, MSG, 128), lambda i: (0, 0, 0)),
+        scratch_shapes=[pltpu.VMEM((256, 128), BF)],
+    )(keep(my_full, pltpu.HBM), q_recv.reshape(PEERS, CAP, 128), keep(kv, pltpu.HBM))
     answer = lax.all_to_all(msg, SAMPLE, split_axis=0, concat_axis=0, tiled=True)
     fixed = lambda *shape: pl.BlockSpec(shape, lambda i, h: (0,) * len(shape))
     block = lambda n: pl.BlockSpec((256, ROWS), lambda i, h: (h[1] + 2 * n, 0))
     pair = sds((512, 128), BF)
-    smem = pl.BlockSpec(memory_space=pltpu.SMEM)
     mine, theirs = call(
         merge_kernel,
         (pair, pair),
         (2 * ITEMS * ROWS * 128, 5 * 10**6),
-        in_specs=[smem] + [vmem] * 3,
+        in_specs=[smem, smem] + [vmem] * 3,
         out_specs=(vmem, vmem),
-    )(info, answer, keep(places, pltpu.HBM), own_value)
+        scratch_shapes=[pltpu.VMEM((ROWS, 128), BF)],
+    )(info, *(keep(a, pltpu.HBM) for a in (your_full, answer, places, own_value)))
 
     from_left = shift(theirs, "x", 1, 4)
     from_right = shift(theirs, "x", 3, 4)

time: 123 us -> 120 us (0.976)
  local copies, waits for them, and re-layouts: 9.5 us -> 5.98 us
    unnamed x23 -> x13, local copies, waits for them, and re-layouts: 4.89 us -> 1.36 us
    all_to_all x1, waiting for transfers between devices: 0.17 us -> 1.41 us  [body(): lax.all_to_all(q_send, SAMPLE, split_axis=0, concat_axis=0, tiled=True)]
    all_to_all x1, starting transfers between devices: 9.18 us -> 7.94 us  [body(): lax.all_to_all(msg, SAMPLE, split_axis=0, concat_axis=0, tiled=True)]
  transfers between devices with their start and end apart: 14 -> 14, of which waited for: 9 -> 10; matrix products, arithmetic and copies ran while one was open for 7% -> 7% of each run, Pallas kernels for 23% -> 23%
where the time goes in v3:
time: 120 us
  starting transfers between devices  46.6 us (39%)
  Pallas kernels  40 us (33%)
  waiting for transfers between devices  23.8 us (20%)
  local copies, waits for them, and re-layouts  5.98 us (5%)
  matrix products  1.29 us (1%)
    ppermute x11, starting transfers between devices, shift(): return lax.ppermute(x, axis, [(i, (i + by) % size) for i in range(size)])  17.4 us
    ppermute x11, waiting for transfers between devices, shift(): return lax.ppermute(x, axis, [(i, (i + by) % size) for i in range(size)])  13.8 us
    all_to_all x1, starting transfers between devices, body(): lax.all_to_all(send.reshape(PEERS, 1, 128), SAMPLE, split_axis=0, concat_...  12 us
    all_to_all x1, starting transfers between devices, body(): lax.all_to_all(q_send, SAMPLE, split_axis=0, concat_axis=0, tiled=True)  9.22 us
    all_to_all x1, waiting for transfers between devices, body(): lax.all_to_all(msg, SAMPLE, split_axis=0, concat_axis=0, tiled=True)  8.6 us
    all_to_all x1, starting transfers between devices, body(): lax.all_to_all(msg, SAMPLE, split_axis=0, concat_axis=0, tiled=True)  7.94 us
    pallas_call x1, Pallas kernels, body(): call(expand_kernel, pltpu.HBM((ROWS, 2 * ROWS), BF), (2 * ROWS * ROWS * R...  7.51 us
    pallas_call x1, Pallas kernels, body(): call(attend_kernel, pltpu.HBM((PEERS, MSG, 128), BF), (2 * ROWS * ROWS *...  6.68 us
  transfers between devices with their start and end apart: 14, of which 10 were waited for; matrix products, arithmetic and copies ran while one was open for 7% of the time, Pallas kernels for 23%

profile of v3, /device:TPU:1, one launch (start us, length us, event | category | flops | bytes accessed | tf_op | source)
XLA Modules:
  0.0 119.6 jit_solution(13369115865090628281)
XLA Ops:
  0.6 0.0 copy-start
  0.7 2.6 %shard_map.104 = (s32[32,128]{1,0:T(8,128)}, f32[48,128]{1,0:T(8,128)}, s32[16,128]{1,0:T(8,128)}) custom-call(s32[1,1024]{1,0:T(1,128)} %bitcast.43, s32[4,1024]{1,0:T(4,128)} %bitcast.42), custom_call_target="tpu_custom_call" | custom-call | flops 400000000 | bytes 1000000 | tf_op jit(solution)/shard_map/pallas_call | solution.py:401
  3.3 12.0 %all-to-all-start = ((s32[32,1,128]{2,1,0:T(1,128)}), s32[32,1,128]{2,1,0:T(1,128)S(1)}, u32[]{:S(2)}, u32[]{:S(2)}) async-start(s32[32,1,128]{2,1,0:T(1,128)} %bitcast.41), calls=%async_computation | async-start | bytes 32768 | tf_op jit(solution)/shard_map/all_to_all | solution.py:421
  15.3 3.1 %shard_map.110 = (bf16[640,1024]{1,0:T(8,128)(2,1)}, bf16[640,1024]{1,0:T(8,128)(2,1)}) custom-call(bf16[1024,512]{1,0:T(8,128)(2,1)} %up_ref.3, bf16[512,1024]{1,0:T(8,128)(2,1)} %down_ref.3, bf16[128,1024]{1,0:T(8,128)(2,1)} %refs_4_.1), custom_call_target="tpu_custom_call" | custom-call | bytes 5000000 | tf_op jit(solution)/shard_map/pallas_call | solution.py:410
  18.5 1.3 %collective-permute-start.3 = (bf16[640,1024]{1,0:T(8,128)(2,1)}, bf16[640,1024]{1,0:T(8,128)(2,1)}, u32[]{:S(2)}, u32[]{:S(2)}) collective-permute-start(bf16[640,1024]{1,0:T(8,128)(2,1)} %get-tuple-element.24), channel_id=1, source_target_pairs={{0,2},{2,4},{4,6},{6,0},{1,3},{3,5},{5,7},{7,1},{8,10},{10,12},{12... | collective-permute-start | bytes 3932168 | tf_op jit(solution)/shard_map/ppermute | solution.py:387
  19.8 1.5 %collective-permute-start.4 = (bf16[640,1024]{1,0:T(8,128)(2,1)}, bf16[640,1024]{1,0:T(8,128)(2,1)}, u32[]{:S(2)}, u32[]{:S(2)}) collective-permute-start(bf16[640,1024]{1,0:T(8,128)(2,1)} %get-tuple-element.25), channel_id=1, source_target_pairs={{0,6},{2,0},{4,2},{6,4},{1,7},{3,1},{5,3},{7,5},{8,14},{10,8},{12,... | collective-permute-start | bytes 3932168 | tf_op jit(solution)/shard_map/ppermute | solution.py:387
  21.2 0.5 fusion
  21.7 1.3 %fusion.9 = bf16[3,1024,128]{2,1,0:T(8,128)(2,1)S(1)} fusion(bf16[3,1024,128]{2,1,0:T(8,128)(2,1)S(1)} %copy-done, bf16[1024,1024]{1,0:T(8,128)(2,1)S(1)} %copy-done.1, f32[1024]{0:T(1024)S(1)} %add_rsqrt_fusion), kind=kOutput, calls=%fused_computation.10 | convolution fusion | flops 808845312 | bytes 3674112 | tf_op jit(solution)/shard_map/rd,tdc->trc/dot_general | solution.py:427
  23.0 1.0 slice_bitcast_fusion.3
  24.1 0.0 all-to-all-done
  24.1 2.6 %shard_map.106 = bf16[1536,128]{1,0:T(8,128)(2,1)} custom-call(s32[32,128]{1,0:T(8,128)S(1)} %bitcast.36, bf16[1024,128]{1,0:T(8,128)(2,1)S(1)} %get-tuple-element.40.q_ref), custom_call_target="tpu_custom_call" | custom-call | flops 402653184 | bytes 1000000 | tf_op jit(solution)/shard_map/pallas_call | solution.py:446
  26.7 9.2 %all-to-all-start.1 = ((bf16[32,48,128]{2,1,0:T(8,128)(2,1)}), bf16[32,48,128]{2,1,0:T(8,128)(2,1)S(1)}, u32[]{:S(2)}, u32[]{:S(2)}) async-start(bf16[32,48,128]{2,1,0:T(8,128)(2,1)} %bitcast.40), calls=%async_computation.1 | async-start | bytes 786432 | tf_op jit(solution)/shard_map/all_to_all | solution.py:457
  35.9 3.6 %copy_bitcast_fusion = (bf16[1024,1024]{1,0:T(8,128)(2,1)S(1)}, bf16[1024,1024]{1,0:T(8,128)(2,1)S(1)}) fusion(bf16[128,8,8,128]{3,2,1,0:T(8,128)(2,1)} %bitcast.38, bf16[128,8,8,128]{3,2,1,0:T(8,128)(2,1)} %bitcast.39), kind=kLoop, calls=%fused_computation.6 | loop fusion | bytes 8388608 | tf_op jit(solution)/shard_map/reshape | solution.py:431
  39.5 7.5 %shard_map.107.kv_ref = bf16[1024,2048]{1,0:T(8,128)(2,1)} custom-call(f32[48,128]{1,0:T(8,128)} %get-tuple-element.20.par_ref, bf16[1024,1024]{1,0:T(8,128)(2,1)S(1)} %get-tuple-element.42.k_ref, bf16[1024,1024]{1,0:T(8,128)(2,1)S(1)} %get-tuple-element.41.v_ref), custom_call_target="tpu_custom_call" | custom-call | flops 4294967296 | bytes 12000000 | tf_op jit(solution)/shard_map/pallas_call | solution.py:432
  47.0 1.4 %all-to-all-done.1.q_ref = bf16[32,48,128]{2,1,0:T(8,128)(2,1)S(1)} async-done(((bf16[32,48,128]{2,1,0:T(8,128)(2,1)}), bf16[32,48,128]{2,1,0:T(8,128)(2,1)S(1)}, u32[]{:S(2)}, u32[]{:S(2)}) %all-to-all-start.1) | async-done | bytes 393248 | tf_op jit(solution)/shard_map/all_to_all | solution.py:457
  48.5 6.7 %shard_map.108 = bf16[32,64,128]{2,1,0:T(8,128)(2,1)} custom-call(s32[16,128]{1,0:T(8,128)} %get-tuple-element.19.full_ref, bf16[32,48,128]{2,1,0:T(8,128)(2,1)S(1)} %all-to-all-done.1.q_ref, bf16[1024,2048]{1,0:T(8,128)(2,1)} %shard_map.107.kv_ref), custom_call_target="tpu_custom_call" | custom-call | flops 268435456 | bytes 8000000 | tf_op jit(solution)/shard_map/pallas_call | solution.py:466
  55.1 7.9 %all-to-all-start.2 = ((bf16[32,64,128]{2,1,0:T(8,128)(2,1)}), bf16[32,64,128]{2,1,0:T(8,128)(2,1)}, u32[]{:S(2)}, u32[]{:S(2)}) async-start(bf16[32,64,128]{2,1,0:T(8,128)(2,1)} %shard_map.108), calls=%async_computation.2 | async-start | bytes 1048576 | tf_op jit(solution)/shard_map/all_to_all | solution.py:479
  63.1 1.8 %collective-permute-start.5 = (bf16[128,1024]{1,0:T(8,128)(2,1)S(1)}, bf16[128,1024]{1,0:T(8,128)(2,1)S(1)}, u32[]{:S(2)}, u32[]{:S(2)}) collective-permute-start(bf16[128,1024]{1,0:T(8,128)(2,1)S(1)} %copy-done.2), channel_id=1, source_target_pairs={{0,4},{2,6},{4,0},{6,2},{1,5},{3,7},{5,1},{7,3},{8,12},{10,14},{12... | collective-permute-start | bytes 786440 | tf_op jit(solution)/shard_map/ppermute | solution.py:387
  64.9 0.6 pad_add_fusion.info_ref
  65.5 3.2 %shard_map.105 = (f32[1024,128]{1,0:T(8,128)}, s32[16,128]{1,0:T(8,128)}) custom-call(s32[32,128]{1,0:T(8,128)S(1)} %bitcast.37, bf16[1024,128]{1,0:T(8,128)(2,1)} %copy-done.3, bf16[1024,128]{1,0:T(8,128)(2,1)} %get-tuple-element.39.k_ref), custom_call_target="tpu_custom_call" | custom-call | flops 1000000000 | bytes 2000000 | tf_op jit(solution)/shard_map/pallas_call | solution.py:460
  68.7 8.6 %all-to-all-done.2.msg_ref = bf16[32,64,128]{2,1,0:T(8,128)(2,1)} async-done(((bf16[32,64,128]{2,1,0:T(8,128)(2,1)}), bf16[32,64,128]{2,1,0:T(8,128)(2,1)}, u32[]{:S(2)}, u32[]{:S(2)}) %all-to-all-start.2) | async-done | bytes 524320 | tf_op jit(solution)/shard_map/all_to_all | solution.py:479
  77.3 4.0 %shard_map.109 = (bf16[512,128]{1,0:T(8,128)(2,1)S(1)}, bf16[512,128]{1,0:T(8,128)(2,1)S(1)}) custom-call(s32[3]{0:T(128)} %pad_add_fusion.info_ref, s32[16,128]{1,0:T(8,128)} %get-tuple-element.18.full_ref, bf16[32,64,128]{2,1,0:T(8,128)(2,1)} %all-to-all-done.2.msg_ref, f32[1024,128]{1,0:T(8,128)} %get-tuple-element.21.place_ref, ...), custom_call_target="tpu_custom_call" | custom-call | flops 402653184 | bytes 5000000 | tf_op jit(solution)/shard_map/pallas_call | solution.py:483
  81.3 0.1 collective-permute-start
  81.4 2.7 %collective-permute-start.1 = (bf16[512,128]{1,0:T(8,128)(2,1)S(1)}, bf16[512,128]{1,0:T(8,128)(2,1)S(1)}, u32[]{:S(2)}, u32[]{:S(2)}) collective-permute-start(bf16[512,128]{1,0:T(8,128)(2,1)S(1)} %get-tuple-element.23), channel_id=1, source_target_pairs={{0,6},{2,0},{4,2},{6,4},{1,7},{3,1},{5,3},{7,5},{8,14},{10,8},{12,... | collective-permute-start | bytes 393224 | tf_op jit(solution)/shard_map/ppermute | solution.py:387
  84.0 0.0 collective-permute-done.5.refs_7_
  84.0 0.3 collective-permute-start.2
  84.4 0.0 collective-permute-done.3.refs_5_.left_ref
  84.4 0.0 collective-permute-done.4.refs_6_.right_ref
  84.4 2.0 %collective-permute-done.refs_1_ = bf16[512,128]{1,0:T(8,128)(2,1)S(1)} collective-permute-done((bf16[512,128]{1,0:T(8,128)(2,1)S(1)}, bf16[512,128]{1,0:T(8,128)(2,1)S(1)}, u32[]{:S(2)}, u32[]{:S(2)}) %collective-permute-start) | collective-permute-done | bytes 131104 | tf_op jit(solution)/shard_map/ppermute | solution.py:387
  86.4 1.0 collective-permute-done.1.refs_2_
  87.4 2.0 %collective-permute-done.2.refs_3_ = bf16[512,128]{1,0:T(8,128)(2,1)S(1)} collective-permute-done((bf16[512,128]{1,0:T(8,128)(2,1)S(1)}, bf16[512,128]{1,0:T(8,128)(2,1)S(1)}, u32[]{:S(2)}, u32[]{:S(2)}) %collective-permute-start.2) | collective-permute-done | bytes 131104 | tf_op jit(solution)/shard_map/ppermute | solution.py:387
  89.4 2.4 %shard_map.111.p_ref = bf16[512,1024]{1,0:T(8,128)(2,1)S(1)} custom-call(s32[3]{0:T(128)} %pad_add_fusion.info_ref, bf16[512,128]{1,0:T(8,128)(2,1)S(1)} %get-tuple-element.22.refs_0_, bf16[512,128]{1,0:T(8,128)(2,1)S(1)} %collective-permute-done.refs_1_, bf16[512,128]{1,0:T(8,128)(2,1)S(1)} %collective-permute-done.1.refs_2_, ...), custom_call_target="tpu_custom_call" | custom-call | flops 600000000 | bytes 3000000 | tf_op jit(solution)/shard_map/pallas_call | solution.py:496
  91.8 0.0 copy-start.4
  91.8 6.5 %collective-permute-start.6 = (bf16[512,1024]{1,0:T(8,128)(2,1)S(1)}, bf16[512,1024]{1,0:T(8,128)(2,1)S(1)}, u32[]{:S(2)}, u32[]{:S(2)}) collective-permute-start(bf16[512,1024]{1,0:T(8,128)(2,1)S(1)} %shard_map.111.p_ref), channel_id=1, source_target_pairs={{0,1},{1,0},{2,3},{3,2},{4,5},{5,4},{6,7},{7,6},{8,9},{9,8},{10,11... | collective-permute-start | bytes 3145736 | tf_op jit(solution)/shard_map/ppermute | solution.py:387
  98.3 2.3 %collective-permute-done.6.r_ref = bf16[512,1024]{1,0:T(8,128)(2,1)S(1)} collective-permute-done((bf16[512,1024]{1,0:T(8,128)(2,1)S(1)}, bf16[512,1024]{1,0:T(8,128)(2,1)S(1)}, u32[]{:S(2)}, u32[]{:S(2)}) %collective-permute-start.6) | collective-permute-done | bytes 1048608 | tf_op jit(solution)/shard_map/ppermute | solution.py:387
  100.6 6.3 %shard_map.112 = (f32[4,512,128]{2,1,0:T(8,128)S(1)}, bf16[4,512,128]{2,1,0:T(8,128)(2,1)S(1)}) custom-call(s32[3]{0:T(128)} %pad_add_fusion.info_ref, bf16[1024,1024]{1,0:T(8,128)(2,1)S(1)} %copy-done.1, bf16[1024,1024]{1,0:T(8,128)(2,1)S(1)} %copy-done.1, bf16[512,1024]{1,0:T(8,128)(2,1)S(1)} %shard_map.111.p_ref, ...), custom_call_target="tpu_custom_call" | custom-call | flops 2000000000 | bytes 10000000 | tf_op jit(solution)/shard_map/pallas_call | solution.py:509
  106.9 0.5 collective-permute-start.7
  107.4 1.5 %collective-permute-done.7.other_ref = bf16[4,512,128]{2,1,0:T(8,128)(2,1)S(1)} collective-permute-done((bf16[4,512,128]{2,1,0:T(8,128)(2,1)S(1)}, bf16[4,512,128]{2,1,0:T(8,128)(2,1)S(1)}, u32[]{:S(2)}, u32[]{:S(2)}) %collective-permute-start.7) | collective-permute-done | bytes 524320 | tf_op jit(solution)/shard_map/ppermute | solution.py:387
  108.9 0.1 shard_map.113
  109.0 0.1 collective-permute-start.8
  109.1 2.0 %collective-permute-start.9 = (bf16[512,128]{1,0:T(8,128)(2,1)S(1)}, bf16[512,128]{1,0:T(8,128)(2,1)S(1)}, u32[]{:S(2)}, u32[]{:S(2)}) collective-permute-start(bf16[512,128]{1,0:T(8,128)(2,1)S(1)} %get-tuple-element.30), channel_id=1, source_target_pairs={{0,4},{2,6},{4,0},{6,2},{1,5},{3,7},{5,1},{7,3},{8,12},{10,14},{12... | collective-permute-start | bytes 393224 | tf_op jit(solution)/shard_map/ppermute | solution.py:387
  111.1 0.7 collective-permute-start.10
  111.8 0.1 pad_maximum_fusion
  111.8 1.3 %copy.13 = bf16[1024,2,128]{2,1,0:T(2,128)(2,1)} copy(bf16[1024,2,128]{2,0,1:T(8,128)(2,1)S(1)} %pad_maximum_fusion) | data formatting | bytes 1048576
  113.2 2.5 %collective-permute-done.8.p1 = bf16[512,128]{1,0:T(8,128)(2,1)S(1)} collective-permute-done((bf16[512,128]{1,0:T(8,128)(2,1)S(1)}, bf16[512,128]{1,0:T(8,128)(2,1)S(1)}, u32[]{:S(2)}, u32[]{:S(2)}) %collective-permute-start.8) | collective-permute-done | bytes 131104 | tf_op jit(solution)/shard_map/ppermute | solution.py:387
  115.7 1.5 %collective-permute-done.9.p2 = bf16[512,128]{1,0:T(8,128)(2,1)S(1)} collective-permute-done((bf16[512,128]{1,0:T(8,128)(2,1)S(1)}, bf16[512,128]{1,0:T(8,128)(2,1)S(1)}, u32[]{:S(2)}, u32[]{:S(2)}) %collective-permute-start.9) | collective-permute-done | bytes 131104 | tf_op jit(solution)/shard_map/ppermute | solution.py:387
  117.2 1.0 collective-permute-done.10.p3
  118.2 1.4 %shard_map.114 = bf16[1024,128]{1,0:T(8,128)(2,1)} custom-call(s32[3]{0:T(128)} %pad_add_fusion.info_ref, bf16[512,128]{1,0:T(8,128)(2,1)S(1)} %get-tuple-element.28.p0, bf16[512,128]{1,0:T(8,128)(2,1)S(1)} %collective-permute-done.8.p1, bf16[512,128]{1,0:T(8,128)(2,1)S(1)} %collective-permute-done.9.p2, bf16[512,128]{1,0:T(8,128)(2,1)S(1)} %collective-permute-done.10.p3), custom_call_target="tpu_custom_call" | custom-call | flops 1000000 | bytes 500000 | tf_op jit(solution)/shard_map/pallas_call | solution.py:538
  (11 shorter events, 0.0 us)
Async XLA Ops:
  0.6 21.1 %copy-start = (bf16[3,1024,128]{2,1,0:T(8,128)(2,1)S(1)}, bf16[3,1024,128]{2,1,0:T(8,128)(2,1)}, u32[]{:S(2)}) copy-start(bf16[3,1024,128]{2,1,0:T(8,128)(2,1)} %param.14) | copy-start | bytes 2359300
  0.6 20.6 %copy-start.1 = (bf16[1024,1024]{1,0:T(8,128)(2,1)S(1)}, bf16[1024,1024]{1,0:T(8,128)(2,1)}, u32[]{:S(2)}) copy-start(bf16[1024,1024]{1,0:T(8,128)(2,1)} %x1_ref.1) | copy-start | bytes 6291460
  3.3 20.8 %all-to-all-start = ((s32[32,1,128]{2,1,0:T(1,128)}), s32[32,1,128]{2,1,0:T(1,128)S(1)}, u32[]{:S(2)}, u32[]{:S(2)}) async-start(s32[32,1,128]{2,1,0:T(1,128)} %bitcast.41), calls=%async_computation | async-start | bytes 32768 | tf_op jit(solution)/shard_map/all_to_all | solution.py:421
  18.5 65.9 %collective-permute-start.3 = (bf16[640,1024]{1,0:T(8,128)(2,1)}, bf16[640,1024]{1,0:T(8,128)(2,1)}, u32[]{:S(2)}, u32[]{:S(2)}) collective-permute-start(bf16[640,1024]{1,0:T(8,128)(2,1)} %get-tuple-element.24), channel_id=1, source_target_pairs={{0,2},{2,4},{4,6},{6,0},{1,3},{3,5},{5,7},{7,1},{8,10},{10,12},{12... | collective-permute-start | bytes 3932168 | tf_op jit(solution)/shard_map/ppermute | solution.py:387
  19.8 64.6 %collective-permute-start.4 = (bf16[640,1024]{1,0:T(8,128)(2,1)}, bf16[640,1024]{1,0:T(8,128)(2,1)}, u32[]{:S(2)}, u32[]{:S(2)}) collective-permute-start(bf16[640,1024]{1,0:T(8,128)(2,1)} %get-tuple-element.25), channel_id=1, source_target_pairs={{0,6},{2,0},{4,2},{6,4},{1,7},{3,1},{5,3},{7,5},{8,14},{10,8},{12,... | collective-permute-start | bytes 3932168 | tf_op jit(solution)/shard_map/ppermute | solution.py:387
  24.1 2.7 %copy-start.3 = (bf16[1024,128]{1,0:T(8,128)(2,1)}, bf16[1024,128]{1,0:T(8,128)(2,1)S(1)}, u32[]{:S(2)}) copy-start(bf16[1024,128]{1,0:T(8,128)(2,1)S(1)} %get-tuple-element.40.q_ref) | copy-start | bytes 786436
  26.7 21.7 %all-to-all-start.1 = ((bf16[32,48,128]{2,1,0:T(8,128)(2,1)}), bf16[32,48,128]{2,1,0:T(8,128)(2,1)S(1)}, u32[]{:S(2)}, u32[]{:S(2)}) async-start(bf16[32,48,128]{2,1,0:T(8,128)(2,1)} %bitcast.40), calls=%async_computation.1 | async-start | bytes 786432 | tf_op jit(solution)/shard_map/all_to_all | solution.py:457
  48.5 14.6 %copy-start.2 = (bf16[128,1024]{1,0:T(8,128)(2,1)S(1)}, bf16[128,1024]{1,0:T(8,128)(2,1)}, u32[]{:S(2)}) copy-start(bf16[128,1024]{1,0:T(8,128)(2,1)} %refs_4_.1) | copy-start | bytes 786436
  55.1 22.2 %all-to-all-start.2 = ((bf16[32,64,128]{2,1,0:T(8,128)(2,1)}), bf16[32,64,128]{2,1,0:T(8,128)(2,1)}, u32[]{:S(2)}, u32[]{:S(2)}) async-start(bf16[32,64,128]{2,1,0:T(8,128)(2,1)} %shard_map.108), calls=%async_computation.2 | async-start | bytes 1048576 | tf_op jit(solution)/shard_map/all_to_all | solution.py:479
  63.1 20.9 %collective-permute-start.5 = (bf16[128,1024]{1,0:T(8,128)(2,1)S(1)}, bf16[128,1024]{1,0:T(8,128)(2,1)S(1)}, u32[]{:S(2)}, u32[]{:S(2)}) collective-permute-start(bf16[128,1024]{1,0:T(8,128)(2,1)S(1)} %copy-done.2), channel_id=1, source_target_pairs={{0,4},{2,6},{4,0},{6,2},{1,5},{3,7},{5,1},{7,3},{8,12},{10,14},{12... | collective-permute-start | bytes 786440 | tf_op jit(solution)/shard_map/ppermute | solution.py:387
  81.3 5.1 %collective-permute-start = (bf16[512,128]{1,0:T(8,128)(2,1)S(1)}, bf16[512,128]{1,0:T(8,128)(2,1)S(1)}, u32[]{:S(2)}, u32[]{:S(2)}) collective-permute-start(bf16[512,128]{1,0:T(8,128)(2,1)S(1)} %get-tuple-element.23), channel_id=1, source_target_pairs={{0,2},{2,4},{4,6},{6,0},{1,3},{3,5},{5,7},{7,1},{8,10},{10,12},{12... | collective-permute-start | bytes 393224 | tf_op jit(solution)/shard_map/ppermute | solution.py:387
  81.4 6.0 %collective-permute-start.1 = (bf16[512,128]{1,0:T(8,128)(2,1)S(1)}, bf16[512,128]{1,0:T(8,128)(2,1)S(1)}, u32[]{:S(2)}, u32[]{:S(2)}) collective-permute-start(bf16[512,128]{1,0:T(8,128)(2,1)S(1)} %get-tuple-element.23), channel_id=1, source_target_pairs={{0,6},{2,0},{4,2},{6,4},{1,7},{3,1},{5,3},{7,5},{8,14},{10,8},{12,... | collective-permute-start | bytes 393224 | tf_op jit(solution)/shard_map/ppermute | solution.py:387
  84.0 5.3 %collective-permute-start.2 = (bf16[512,128]{1,0:T(8,128)(2,1)S(1)}, bf16[512,128]{1,0:T(8,128)(2,1)S(1)}, u32[]{:S(2)}, u32[]{:S(2)}) collective-permute-start(bf16[512,128]{1,0:T(8,128)(2,1)S(1)} %get-tuple-element.22.refs_0_), channel_id=1, source_target_pairs={{0,4},{2,6},{4,0},{6,2},{1,5},{3,7},{5,1},{7,3},{8,12},{10,14},{12... | collective-permute-start | bytes 393224 | tf_op jit(solution)/shard_map/ppermute | solution.py:387
  91.8 20.0 %copy-start.4 = (bf16[1024,1,128]{2,0,1:T(8,128)(2,1)S(1)}, bf16[1024,1,128]{2,0,1:T(8,128)(2,1)}, u32[]{:S(2)}) copy-start(bf16[1024,1,128]{2,0,1:T(8,128)(2,1)} %get-tuple-element.36) | copy-start | bytes 786436
  91.8 20.0 %copy-start.5 = (bf16[1024,1,128]{2,0,1:T(8,128)(2,1)S(1)}, bf16[1024,1,128]{2,0,1:T(8,128)(2,1)}, u32[]{:S(2)}) copy-start(bf16[1024,1,128]{2,0,1:T(8,128)(2,1)} %get-tuple-element.37) | copy-start | bytes 786436
  91.8 8.8 %collective-permute-start.6 = (bf16[512,1024]{1,0:T(8,128)(2,1)S(1)}, bf16[512,1024]{1,0:T(8,128)(2,1)S(1)}, u32[]{:S(2)}, u32[]{:S(2)}) collective-permute-start(bf16[512,1024]{1,0:T(8,128)(2,1)S(1)} %shard_map.111.p_ref), channel_id=1, source_target_pairs={{0,1},{1,0},{2,3},{3,2},{4,5},{5,4},{6,7},{7,6},{8,9},{9,8},{10,11... | collective-permute-start | bytes 3145736 | tf_op jit(solution)/shard_map/ppermute | solution.py:387
  106.9 2.0 %collective-permute-start.7 = (bf16[4,512,128]{2,1,0:T(8,128)(2,1)S(1)}, bf16[4,512,128]{2,1,0:T(8,128)(2,1)S(1)}, u32[]{:S(2)}, u32[]{:S(2)}) collective-permute-start(bf16[4,512,128]{2,1,0:T(8,128)(2,1)S(1)} %get-tuple-element.27), channel_id=1, source_target_pairs={{0,1},{1,0},{2,3},{3,2},{4,5},{5,4},{6,7},{7,6},{8,9},{9,8},{10,11... | collective-permute-start | bytes 1572872 | tf_op jit(solution)/shard_map/ppermute | solution.py:387
  109.0 6.7 %collective-permute-start.8 = (bf16[512,128]{1,0:T(8,128)(2,1)S(1)}, bf16[512,128]{1,0:T(8,128)(2,1)S(1)}, u32[]{:S(2)}, u32[]{:S(2)}) collective-permute-start(bf16[512,128]{1,0:T(8,128)(2,1)S(1)} %get-tuple-element.29), channel_id=1, source_target_pairs={{0,2},{2,4},{4,6},{6,0},{1,3},{3,5},{5,7},{7,1},{8,10},{10,12},{12... | collective-permute-start | bytes 393224 | tf_op jit(solution)/shard_map/ppermute | solution.py:387
  109.1 8.1 %collective-permute-start.9 = (bf16[512,128]{1,0:T(8,128)(2,1)S(1)}, bf16[512,128]{1,0:T(8,128)(2,1)S(1)}, u32[]{:S(2)}, u32[]{:S(2)}) collective-permute-start(bf16[512,128]{1,0:T(8,128)(2,1)S(1)} %get-tuple-element.30), channel_id=1, source_target_pairs={{0,4},{2,6},{4,0},{6,2},{1,5},{3,7},{5,1},{7,3},{8,12},{10,14},{12... | collective-permute-start | bytes 393224 | tf_op jit(solution)/shard_map/ppermute | solution.py:387
  111.1 7.1 %collective-permute-start.10 = (bf16[512,128]{1,0:T(8,128)(2,1)S(1)}, bf16[512,128]{1,0:T(8,128)(2,1)S(1)}, u32[]{:S(2)}, u32[]{:S(2)}) collective-permute-start(bf16[512,128]{1,0:T(8,128)(2,1)S(1)} %get-tuple-element.31), channel_id=1, source_target_pairs={{0,6},{2,0},{4,2},{6,4},{1,7},{3,1},{5,3},{7,5},{8,14},{10,8},{12,... | collective-permute-start | bytes 393224 | tf_op jit(solution)/shard_map/ppermute | solution.py:387

commit v4 on v3

--- a/solution.py
+++ b/solution.py
@@ -165,11 +165,20 @@
     out_ref[:, ROWS:] = jnp.dot(hot, v_ref[...], preferred_element_type=F32).astype(BF)
 
 
-def query_kernel(recv_ref, q_ref, out_ref):
-    peers = recv_ref.shape[0]
-    col = column(recv_ref[...].astype(F32), peers, CAP)
-    hot = (col == iota((peers * CAP, ROWS), 1).astype(F32)).astype(F32).astype(BF)
-    out_ref[...] = jnp.dot(hot, q_ref[...], preferred_element_type=F32).astype(BF)
+def query_kernel(recv_ref, q_ref, out_ref, stage, sems):
+    lists = recv_ref[...].astype(F32)
+    slots = iota((8 * CAP, ROWS), 1).astype(F32)
+    copies = []
+    for n in range(4):
+        at = pl.ds(n * 8 * CAP, 8 * CAP)
+        col = column(lists[n * 8 : n * 8 + 8], 8, CAP)
+        hot = (col == slots).astype(F32).astype(BF)
+        stage[at] = jnp.dot(hot, q_ref[...], preferred_element_type=F32).astype(BF)
+        copy = pltpu.make_async_copy(stage.at[at], out_ref.at[at], sems.at[n])
+        copy.start()
+        copies.append(copy)
+    for copy in copies:
+        copy.wait()
 
 
 def place_kernel(recv_ref, q_ref, k_ref, out_ref, full_ref):
@@ -198,41 +207,63 @@
     prod = q_ref[...].astype(F32) * k_ref[...].astype(F32) * (1.0 / HD**0.5)
     s0 = jnp.sum(prod[:, :HD], axis=1, keepdims=True)
     s1 = jnp.sum(prod[:, HD:], axis=1, keepdims=True)
+    high = jnp.floor(pos * (1.0 / 32.0))
+    pieces = [high, pos - high * 32.0, place, src]
+    for value in (s0, s1):
+        for _ in range(3):
+            piece = value.astype(BF).astype(F32)
+            pieces.append(piece)
+            value = value - piece
     lane = iota((ROWS, 128), 1)
-    known = jnp.where(lane == 0, src, jnp.where(lane == 1, place, pos))
-    out_ref[...] = jnp.where(lane == 3, s0, jnp.where(lane == 4, s1, known))
-
-
-def attend_kernel(full_ref, q_ref, kv_ref, out_ref, rows_ref):
+    known = jnp.zeros((ROWS, 128), F32)
+    for n, piece in enumerate(pieces):
+        known = jnp.where(lane == n, piece, known)
+    out_ref[...] = known.astype(BF)
+
+
+def attend_kernel(full_hbm, q_ref, kv_ref, out_ref, kv, rows_ref, stage, full_ref, sems):
     n = 256
-    step = pl.program_id(0)
-
-    @pl.when(step < 2)
-    def _():
-        rows_ref[...] = q_ref[pl.ds(step * 16, 16), :LOW, :].reshape(n, 128)
-
-    @pl.when(step >= 2)
-    def _():
-        for k in range(8):
-            peer = full_ref[(step - 2) * 8 + k, 0]
-            rows = q_ref[pl.ds(peer, 1), LOW:, :].reshape(REST, 128)
-            rows_ref[k * REST : (k + 1) * REST, :] = rows
-
+    listing = pltpu.make_async_copy(full_hbm, full_ref, sems.at[9])
+    listing.start()
+    copies = []
+    for part in range(2):
+        for i in range(4):
+            src = kv_ref.at[pl.ds(i * n, n), pl.ds(part * ROWS, ROWS)]
+            dst = kv.at[i, :, pl.ds(part * ROWS, ROWS)]
+            copies.append(pltpu.make_async_copy(src, dst, sems.at[part * 4 + i]))
+    for copy in copies:
+        copy.start()
+    split = PEERS * LOW
+    rows_ref[:split, :] = q_ref[:, :LOW, :].reshape(split, 128)
+    listing.wait()
+    peers = [pl.ds(full_ref[k, 0], 1) for k in range(FULL)]
+    for k, peer in enumerate(peers):
+        at = split + k * REST
+        rows_ref[at : at + REST, :] = q_ref[peer, LOW:, :].reshape(REST, 128)
     sel_p = iota((16, ROWS), 1) // 128
     sel_h = (iota((16, ROWS), 1) % 128) // HD
     sel = (iota((16, ROWS), 0) == sel_h * 8 + sel_p).astype(F32).astype(BF)
-    q = rows_ref[...].astype(F32)
-    highs, lows = [], []
-    for p in range(8):
-        prod = q * kv_ref[:, p * 128 : (p + 1) * 128].astype(F32)
-        high = prod.astype(BF)
-        highs.append(high)
-        lows.append((prod - high.astype(F32)).astype(BF))
-    score = lax.dot_general(sel, jnp.concatenate(highs, axis=1), NT, preferred_element_type=F32)
-    score = score + lax.dot_general(
-        sel, jnp.concatenate(lows, axis=1), NT, preferred_element_type=F32
-    )
-    score = score * (1.0 / HD**0.5)
+    sum_p = iota((ROWS, 128), 0) // 128
+    sum_h = (iota((ROWS, 128), 0) % 128) // HD
+    sums = (iota((ROWS, 128), 1) == sum_h * 8 + sum_p).astype(F32).astype(BF)
+    scores = []
+    for i in range(4):
+        q = rows_ref[i * n : (i + 1) * n, :].astype(F32)
+        copies[i].wait()
+        score = jnp.zeros((n, 128), F32)
+        for p in range(0, 8, 2):
+            highs, lows = [], []
+            for t in (p, p + 1):
+                prod = q * kv[i, :, t * 128 : (t + 1) * 128].astype(F32)
+                high = prod.astype(BF)
+                highs.append(high)
+                lows.append((prod - high.astype(F32)).astype(BF))
+            part = sums[p * 128 : (p + 2) * 128]
+            highs, lows = jnp.concatenate(highs, axis=1), jnp.concatenate(lows, axis=1)
+            score = score + jnp.dot(highs, part, preferred_element_type=F32)
+            score = score + jnp.dot(lows, part, preferred_element_type=F32)
+        scores.append(score.T[:16])
+    score = jnp.concatenate(scores, axis=1) * (1.0 / HD**0.5)
     weights, parts = [], []
     for h in range(2):
         part = score[h * 8 : (h + 1) * 8]
@@ -246,124 +277,144 @@
             parts.append(piece)
             lse = lse - piece
     weight = jnp.concatenate(weights, axis=0).astype(BF)
-    wide = lax.dot_general(weight, sel, TN, preferred_element_type=F32)
-    ctx = wide[:, :128] * kv_ref[:, ROWS : ROWS + 128].astype(F32)
-    for p in range(1, 8):
-        ctx = ctx + wide[:, p * 128 : (p + 1) * 128] * kv_ref[
-            :, ROWS + p * 128 : ROWS + (p + 1) * 128
-        ].astype(F32)
-    ctx = ctx.astype(BF)
-    tail = jnp.concatenate(parts + [jnp.zeros((10, n), F32)], axis=0)
-
-    @pl.when(step < 2)
-    def _():
-        peers = pl.ds(step * 16, 16)
-        out_ref[peers, :LOW, :] = ctx.reshape(16, LOW, 128)
-        out_ref[peers, LOW:CAP, :] = jnp.zeros((16, REST, 128), BF)
-        for k in range(16):
-            piece = tail[:, k * LOW : (k + 1) * LOW]
-            piece = jnp.concatenate([piece, jnp.zeros((16, 128 - LOW), F32)], axis=1)
-            out_ref[pl.ds(step * 16 + k, 1), CAP:, :] = piece.astype(BF).reshape(1, 16, 128)
-
-    @pl.when(step >= 2)
-    def _():
-        for k in range(8):
-            peer = pl.ds(full_ref[(step - 2) * 8 + k, 0], 1)
-            rows = ctx[k * REST : (k + 1) * REST].reshape(1, REST, 128)
-            out_ref[peer, LOW:CAP, :] = rows
-            piece = tail[:, k * REST : (k + 1) * REST]
-            before, after = jnp.zeros((16, LOW), F32), jnp.zeros((16, 128 - CAP), F32)
-            piece = jnp.concatenate([before, piece, after], axis=1).astype(BF)
-            out_ref[peer, CAP:, :] = out_ref[peer, CAP:, :] + piece.reshape(1, 16, 128)
+    tail = jnp.concatenate(parts + [jnp.zeros((10, ROWS), F32)], axis=0)
+    stage[:, LOW:CAP, :] = jnp.zeros((PEERS, REST, 128), BF)
+    for k in range(PEERS):
+        piece = tail[:, k * LOW : (k + 1) * LOW]
+        piece = jnp.concatenate([piece, jnp.zeros((16, 128 - LOW), F32)], axis=1)
+        stage[k, CAP:, :] = piece.astype(BF)
+    for i in range(4):
+        wide = lax.dot_general(
+            weight[:, i * n : (i + 1) * n], sel, TN, preferred_element_type=F32
+        )
+        copies[4 + i].wait()
+        ctx = jnp.zeros((n, 128), F32)
+        for p in range(8):
+            value = kv[i, :, ROWS + p * 128 : ROWS + (p + 1) * 128].astype(F32)
+            ctx = ctx + wide[:, p * 128 : (p + 1) * 128] * value
+        ctx = ctx.astype(BF)
+        if i < 2:
+            stage[i * 16 : (i + 1) * 16, :LOW, :] = ctx.reshape(16, LOW, 128)
+        else:
+            for k in range(8):
+                peer = peers[(i - 2) * 8 + k]
+                stage[peer, LOW:CAP, :] = ctx[k * REST : (k + 1) * REST].reshape(1, REST, 128)
+    for k, peer in enumerate(peers):
+        at = split + k * REST
+        before, after = jnp.zeros((16, LOW), F32), jnp.zeros((16, 128 - CAP), F32)
+        piece = jnp.concatenate([before, tail[:, at : at + REST], after], axis=1).astype(BF)
+        stage[peer, CAP:, :] = stage[peer, CAP:, :] + piece.reshape(1, 16, 128)
+    end = pltpu.make_async_copy(stage, out_ref, sems.at[8])
+    end.start()
+    end.wait()
 
 
 def merge_kernel(
-    info_ref, full_ref, msg_ref, place_ref, v_ref, mine_ref, theirs_ref, ctx_ref
+    full_hbm, msg_hbm, place_hbm, v_hbm, mine_ref, theirs_ref, msg_ref, place_ref, v_ref, ctx_ref,
+    full_ref, sems
 ):
     rows = 256
+    outs = [r.at[pl.ds(n * rows, rows)] for r in (mine_ref, theirs_ref) for n in range(2)]
+    pairs = [(full_hbm, full_ref), (msg_hbm, msg_ref), (place_hbm, place_ref), (v_hbm, v_ref)]
+    fetch = [pltpu.make_async_copy(a, b, sems.at[i]) for i, (a, b) in enumerate(pairs)]
+    for copy in fetch:
+        copy.start()
+    piece, lane = iota((128, 512), 0), iota((128, 512), 1)
+    use = jnp.where(lane < 128, jnp.where(piece == 0, 32.0, jnp.where(piece == 1, 1.0, 0.0)), 0.0)
+    use = use + jnp.where((lane // 128 == 1) & (piece == 2), 1.0, 0.0)
+    use = use + jnp.where((lane // 128 == 2) & (piece == 3), 1.0, 0.0)
+    scores = (lane >= 384) & (piece >= 4) & (piece < 10)
+    head = (lane - 384) // HD
+    use = use + jnp.where(scores & ((piece - 4) // 3 == head), 1.0, 0.0)
+    use = use.astype(BF)
+    lanes = iota((rows, 128), 1).astype(F32)
+    entry = iota((rows, PEERS * 16), 1)
+    of_source = (entry // 16).astype(F32)
+    of_head = entry % 16 // 3
+    for copy in fetch:
+        copy.wait()
     low = PEERS * LOW
     ctx_ref[:low, :] = msg_ref[:, :LOW, :].reshape(low, 128)
     for k in range(FULL):
         got = msg_ref[pl.ds(full_ref[k, 0], 1), LOW:CAP, :].reshape(REST, 128)
         ctx_ref[low + k * REST : low + (k + 1) * REST, :] = got
-    outs = [r.at[pl.ds(n * rows, rows)] for r in (mine_ref, theirs_ref) for n in range(2)]
-    parts = []
-    for h in range(2):
-        for j in range(3):
-            parts.append(msg_ref[:, CAP + h * 3 + j, :].reshape(PEERS, 128))
-    parts = jnp.concatenate(parts, axis=1)
+    parts = msg_ref[:, CAP:, :].reshape(PEERS * 16, 128)
+    parity = lax.axis_index("x") % 2
     for i, out in enumerate(outs):
-        block = (info_ref[1] if i < 2 else 1 - info_ref[1]) + 2 * (i % 2)
+        block = (parity if i < 2 else 1 - parity) + 2 * (i % 2)
         at = pl.ds(pl.multiple_of(block * rows, rows), rows)
-        known = place_ref[at, :]
-        src, place = known[:, 0:1], known[:, 1:2]
-        lane = iota((rows, 128), 1)
-        lanes = lane.astype(F32)
-        hot = (iota((rows, ROWS), 1).astype(F32) == known[:, 2:3]).astype(F32).astype(BF)
+        known = jnp.dot(place_ref[at, :], use, preferred_element_type=F32)
+        pos, own = known[:, :128], known[:, 384:]
+        hot = [(lanes + float(t * 128) == pos).astype(F32).astype(BF) for t in range(8)]
+        hot = jnp.concatenate(hot, axis=1)
         ctx = jnp.dot(hot, ctx_ref[...], preferred_element_type=F32)
-        from_src = (iota((rows, PEERS), 1).astype(F32) == src).astype(F32).astype(BF)
-        lists = jnp.dot(from_src, parts, preferred_element_type=F32)
+        hit = of_source == jnp.concatenate([known[:, 256:384]] * 4, axis=1)
+        here = lanes == known[:, 128:256]
         cols = []
         for h in range(2):
-            base = h * 384
-            lse = lists[:, base : base + 128] + lists[:, base + 128 : base + 256]
-            lse = lse + lists[:, base + 256 : base + 384]
-            lse = jnp.where(lanes == place, lse, 0.0)
-            cols.append(jnp.sum(lse, axis=1, keepdims=True))
-        lse = jnp.where(lane < HD, cols[0], cols[1])
-        own = jnp.where(lane < HD, known[:, 3:4], known[:, 4:5])
+            pick = jnp.where(hit & (of_head == h), 1.0, 0.0).astype(BF)
+            lists = jnp.dot(pick, parts, preferred_element_type=F32)
+            cols.append(jnp.sum(jnp.where(here, lists, 0.0), axis=1, keepdims=True))
+        lse = jnp.where(lanes < HD, cols[0], cols[1])
         top = jnp.maximum(lse, own)
         a = jnp.exp(lse - top)
         b = jnp.exp(own - top)
         out[...] = ((a * ctx + b * v_ref[at, :].astype(F32)) / (a + b)).astype(BF)
 
 
-def project_kernel(info_ref, *refs):
-    rows = jnp.concatenate([r[...] for r in refs[:4]], axis=1)
-    weight = jnp.concatenate([r[...] for r in refs[4:8]], axis=0)
-    refs[8][...] = jnp.dot(rows, weight, preferred_element_type=F32).astype(BF)
+def project_kernel(a0, a1, a2, a3, own_ref, two_ref, left_ref, right_ref, out_ref, near, sems):
+    copies = [
+        pltpu.make_async_copy(r.at[pl.ds(512, 128)], near.at[pl.ds(n * 128, 128)], sems.at[n])
+        for n, r in enumerate((left_ref, right_ref))
+    ]
+    for copy in copies:
+        copy.start()
+    rows = jnp.concatenate([a0[...], a3[...]], axis=1)
+    weight = jnp.concatenate([own_ref[...], two_ref[...]], axis=0)
+    total = jnp.dot(rows, weight, preferred_element_type=F32)
+    rows = jnp.concatenate([a1[...], a2[...]], axis=1)
+    for copy in copies:
+        copy.wait()
+    total = total + jnp.dot(rows, near[...], preferred_element_type=F32)
+    out_ref[...] = total.astype(BF)
 
 
 def ffn_kernel(
-    info_ref, x0_ref, x1_ref, p_ref, r_ref, up_ref, down_ref, right_ref, left_ref, *refs
+    x_ref, p_ref, r_ref, up_ref, down_ref, right_ref, left_ref, same_ref, other_ref, ups, downs,
+    hid, acc, sems
 ):
-    same_ref, other_ref, ups, downs, hid, acc, sems = refs
-    pairs = [(up_ref, ups.at[0]), (down_ref, downs.at[0])]
+    pairs = []
     for n, src in enumerate((right_ref, left_ref)):
         for k in range(4):
             block = pl.ds(k * 256, 256)
-            pairs.append((src.at[pl.ds(0, 256), block], ups.at[1, block, pl.ds(n * 256, 256)]))
-        pairs.append((src.at[pl.ds(256, 256)], downs.at[1, pl.ds(n * 256, 256)]))
+            pairs.append((src.at[pl.ds(0, 256), block], ups.at[block, pl.ds(n * 256, 256)]))
+    for n, src in enumerate((right_ref, left_ref)):
+        pairs.append((src.at[pl.ds(256, 256)], downs.at[pl.ds(n * 256, 256)]))
     copies = [pltpu.make_async_copy(a, b, sems.at[i]) for i, (a, b) in enumerate(pairs)]
     for copy in copies:
         copy.start()
+    x = lax.axis_index("x")
+    core = lax.axis_index("core")
     normed = []
-    for n, x_ref in enumerate((x0_ref, x1_ref)):
+    for n in range(2):
         at = pl.ds(n * 256, 256)
         attn = p_ref[at].astype(F32) + r_ref[at].astype(F32)
-        hidden = (x_ref[...].astype(F32) + attn).astype(BF).astype(F32)
+        rows = pl.ds(pl.multiple_of((x % 2 + 2 * n) * 256, 256), 256)
+        hidden = (x_ref[rows, :].astype(F32) + attn).astype(BF).astype(F32)
         scale = lax.rsqrt(jnp.mean(hidden * hidden, axis=-1, keepdims=True) + 1e-05)
         normed.append((hidden * scale).astype(BF))
-        hid[at] = jnp.where(info_ref[0] // 2 == n, hidden, 0.0)
-    for unit in range(2):
-        for n in range(2):
-            at = pl.ds(n * 256, 256)
-            if n == 0:
-                for copy in (copies[:1], copies[2:6] + copies[7:11])[unit]:
-                    copy.wait()
-            up = jnp.dot(normed[n], ups[unit], preferred_element_type=F32)
-            act = jax.nn.gelu(up).astype(BF)
-            if n == 0:
-                for copy in (copies[1:2], [copies[6], copies[11]])[unit]:
-                    copy.wait()
-            down = jnp.dot(act, downs[unit], preferred_element_type=F32)
-            if unit == 0:
-                acc[at] = down
-            else:
-                acc[at] += down
-    core = info_ref[2]
+        hid[at] = jnp.where(x // 2 == n, hidden, 0.0)
+    normed = jnp.concatenate(normed, axis=0)
+    act = jax.nn.gelu(jnp.dot(normed, up_ref[...], preferred_element_type=F32)).astype(BF)
+    total = jnp.dot(act, down_ref[...], preferred_element_type=F32)
+    for copy in copies[:8]:
+        copy.wait()
+    act = jax.nn.gelu(jnp.dot(normed, ups[...], preferred_element_type=F32)).astype(BF)
+    for copy in copies[8:]:
+        copy.wait()
+    acc[...] = total + jnp.dot(act, downs[...], preferred_element_type=F32)
     for d in range(4):
-        head = ((info_ref[0] + d) % 4) * 2
+        head = ((x + d) % 4) * 2
         at = pl.ds(pl.multiple_of((head + core) * 128, 128), 128)
         same_ref[d] = hid[:, at] + acc[:, at]
         at = pl.ds(pl.multiple_of((head + 1 - core) * 128, 128), 128)
@@ -375,10 +426,11 @@
         out[...] = (same_ref[i] + other_ref[i].astype(F32)).astype(BF)
 
 
-def place_rows_kernel(info_ref, p0, p1, p2, p3, out_ref):
+def place_rows_kernel(p0, p1, p2, p3, out_ref):
+    mine = lax.axis_index("x") % 2
     for n in range(2):
         at = pl.ds(n * 256, 256)
-        for parity, a, b in ((info_ref[1], p0, p2), (1 - info_ref[1], p1, p3)):
+        for parity, a, b in ((mine, p0, p2), (1 - mine, p1, p3)):
             to = pl.multiple_of((parity + 2 * n) * 256, 256)
             out_ref[pl.ds(to, 256), :] = (a[at].astype(F32) + b[at].astype(F32)).astype(BF)
 
@@ -394,10 +446,6 @@
 def body(stream_in, keys, values, counts, slots, w_qkv, w_out, w_up, w_down):
     vmem = pl.BlockSpec(memory_space=pltpu.VMEM)
     hbm = pl.BlockSpec(memory_space=pltpu.HBM)
-    x = lax.axis_index("x")
-    core = lax.axis_index("core")
-    info = keep(jnp.stack([x, x % 2, core]).astype(jnp.int32), pltpu.HBM)
-
     send, par, my_full = call(
         plan_kernel,
         (
@@ -447,19 +495,15 @@
         query_kernel,
         pltpu.HBM((ITEMS, 128), BF),
         (2 * ITEMS * ROWS * 128, 10**6),
-        grid=(4,),
-        in_specs=[
-            pl.BlockSpec((8, 128), lambda i: (i, 0)),
-            pl.BlockSpec((ROWS, 128), lambda i: (0, 0)),
-        ],
-        out_specs=pl.BlockSpec((8 * CAP, 128), lambda i: (i, 0)),
+        in_specs=[vmem, vmem],
+        out_specs=hbm,
+        scratch_shapes=[pltpu.VMEM((ITEMS, 128), BF), pltpu.SemaphoreType.DMA((4,))],
     )(recv, query)
     q_recv = lax.all_to_all(q_send, SAMPLE, split_axis=0, concat_axis=0, tiled=True)
 
-    smem = pl.BlockSpec(memory_space=pltpu.SMEM)
     places, your_full = call(
         place_kernel,
-        (pltpu.HBM((ROWS, 128), F32), pltpu.HBM((FULL, 128), jnp.int32)),
+        (pltpu.HBM((ROWS, 128), BF), pltpu.HBM((FULL, 128), jnp.int32)),
         (10**9, 2 * 10**6),
     )(recv, keep(query, pltpu.HBM), keep(own_key, pltpu.HBM))
 
@@ -467,69 +511,77 @@
         attend_kernel,
         pltpu.HBM((PEERS, MSG, 128), BF),
         (2 * ROWS * ROWS * 128, 8 * 10**6),
-        grid=(4,),
-        in_specs=[
-            smem,
-            pl.BlockSpec((PEERS, CAP, 128), lambda i: (0, 0, 0)),
-            pl.BlockSpec((256, 2 * ROWS), lambda i: (i, 0)),
+        in_specs=[hbm, vmem, hbm],
+        out_specs=hbm,
+        scratch_shapes=[
+            pltpu.VMEM((4, 256, 2 * ROWS), BF),
+            pltpu.VMEM((ROWS, 128), BF),
+            pltpu.VMEM((PEERS, MSG, 128), BF),
+            pltpu.SMEM((FULL, 128), jnp.int32),
+            pltpu.SemaphoreType.DMA((10,)),
         ],
-        out_specs=pl.BlockSpec((PEERS, MSG, 128), lambda i: (0, 0, 0)),
-        scratch_shapes=[pltpu.VMEM((256, 128), BF)],
     )(keep(my_full, pltpu.HBM), q_recv.reshape(PEERS, CAP, 128), keep(kv, pltpu.HBM))
     answer = lax.all_to_all(msg, SAMPLE, split_axis=0, concat_axis=0, tiled=True)
-    fixed = lambda *shape: pl.BlockSpec(shape, lambda i, h: (0,) * len(shape))
-    block = lambda n: pl.BlockSpec((256, ROWS), lambda i, h: (h[1] + 2 * n, 0))
     pair = sds((512, 128), BF)
     mine, theirs = call(
         merge_kernel,
         (pair, pair),
         (2 * ITEMS * ROWS * 128, 5 * 10**6),
-        in_specs=[smem, smem] + [vmem] * 3,
+        in_specs=[hbm] * 4,
         out_specs=(vmem, vmem),
-        scratch_shapes=[pltpu.VMEM((ROWS, 128), BF)],
-    )(info, *(keep(a, pltpu.HBM) for a in (your_full, answer, places, own_value)))
+        scratch_shapes=[
+            pltpu.VMEM((PEERS, MSG, 128), BF),
+            pltpu.VMEM((ROWS, 128), BF),
+            pltpu.VMEM((ROWS, 128), BF),
+            pltpu.VMEM((ROWS, 128), BF),
+            pltpu.SMEM((FULL, 128), jnp.int32),
+            pltpu.SemaphoreType.DMA((4,)),
+        ],
+    )(*(keep(a, pltpu.HBM) for a in (your_full, answer, places, own_value)))
 
     from_left = shift(theirs, "x", 1, 4)
     from_right = shift(theirs, "x", 3, 4)
     from_two = shift(mine, "x", 2, 4)
-    last = lambda at: pl.BlockSpec((128, ROWS), lambda i, h: (at, 0))
     partial = call(
         project_kernel,
         sds((512, ROWS), BF),
         (6 * 10**8, 3 * 10**6),
-        grid_spec=pltpu.PrefetchScalarGridSpec(
-            num_scalar_prefetch=1,
-            grid=(1,),
-            in_specs=[fixed(512, 128)] * 4 + [last(0), last(4), last(4), last(0)],
-            out_specs=fixed(512, ROWS),
-        ),
-    )(info, mine, from_left, from_right, from_two, w_out, left, right, wo_two)
+        in_specs=[vmem] * 6 + [hbm] * 2,
+        out_specs=vmem,
+        scratch_shapes=[pltpu.VMEM((256, ROWS), BF), pltpu.SemaphoreType.DMA((2,))],
+    )(
+        mine,
+        from_left,
+        from_right,
+        from_two,
+        keep(w_out),
+        keep(wo_two),
+        keep(left, pltpu.HBM),
+        keep(right, pltpu.HBM),
+    )
     partner = shift(partial, "core", 1, 2)
 
     same, other = call(
         ffn_kernel,
         (sds((4, 512, 128), F32), sds((4, 512, 128), BF)),
         (2 * 10**9, 10 * 10**6),
-        grid_spec=pltpu.PrefetchScalarGridSpec(
-            num_scalar_prefetch=1,
-            grid=(1,),
-            in_specs=[block(0), block(1), fixed(512, ROWS), fixed(512, ROWS)] + [hbm] * 4,
-            out_specs=(fixed(4, 512, 128), fixed(4, 512, 128)),
-            scratch_shapes=[
-                pltpu.VMEM((2, ROWS, 512), BF),
-                pltpu.VMEM((2, 512, ROWS), BF),
-                pltpu.VMEM((512, ROWS), F32),
-                pltpu.VMEM((512, ROWS), F32),
-                pltpu.SemaphoreType.DMA((12,)),
-            ],
-        ),
+        in_specs=[vmem] * 5 + [hbm] * 2,
+        out_specs=(vmem, vmem),
+        scratch_shapes=[
+            pltpu.VMEM((ROWS, 512), BF),
+            pltpu.VMEM((512, ROWS), BF),
+            pltpu.VMEM((512, ROWS), F32),
+            pltpu.VMEM((512, ROWS), F32),
+            pltpu.SemaphoreType.DMA((10,)),
+        ],
     )(
-        info,
-        stream_in,
         stream_in,
         partial,
         partner,
-        *(keep(w, pltpu.HBM) for w in (w_up, w_down, right, left)),
+        keep(w_up),
+        keep(w_down),
+        keep(right, pltpu.HBM),
+        keep(left, pltpu.HBM),
     )
 
     swapped = shift(other, "core", 1, 2)
@@ -539,9 +591,9 @@
         place_rows_kernel,
         sds((ROWS, 128), BF),
         (10**6, 5 * 10**5),
-        in_specs=[smem] + [vmem] * 4,
+        in_specs=[vmem] * 4,
         out_specs=vmem,
-    )(info, *parts)
+    )(*parts)
     return (layer_out, new_kv)
 
 

time: 120 us -> 115 us (0.958)
  Pallas kernels: 40 us -> 34.5 us
    pallas_call x1, Pallas kernels: 6.28 us -> 4.76 us  [body(): call(ffn_kernel, (sds((4, 512, 128), F32), sds((4, 512, 128), BF)), (2 *...]
    pallas_call x1, Pallas kernels: 6.68 us -> 5.48 us  [body(): call(attend_kernel, pltpu.HBM((PEERS, MSG, 128), BF), (2 * ROWS * ROWS *...]
  transfers between devices with their start and end apart: 14 -> 14, of which waited for: 10 -> 10; matrix products, arithmetic and copies ran while one was open for 7% -> 7% of each run, Pallas kernels for 23% -> 21%
where the time goes in v4:
time: 115 us; the launch traced here: 114 us
  starting transfers between devices  46.6 us (41%)
  Pallas kernels  34.5 us (30%)
  waiting for transfers between devices  24.3 us (21%)
  local copies, waits for them, and re-layouts  5.99 us (5%)
  matrix products  1.29 us (1%)
    ppermute x11, starting transfers between devices, shift(): return lax.ppermute(x, axis, [(i, (i + by) % size) for i in range(size)])  17.4 us
    ppermute x11, waiting for transfers between devices, shift(): return lax.ppermute(x, axis, [(i, (i + by) % size) for i in range(size)])  13.8 us
    all_to_all x1, starting transfers between devices, body(): lax.all_to_all(send.reshape(PEERS, 1, 128), SAMPLE, split_axis=0, concat_...  12 us
    all_to_all x1, starting transfers between devices, body(): lax.all_to_all(q_send, SAMPLE, split_axis=0, concat_axis=0, tiled=True)  9.23 us
    all_to_all x1, waiting for transfers between devices, body(): lax.all_to_all(msg, SAMPLE, split_axis=0, concat_axis=0, tiled=True)  9.08 us
    all_to_all x1, starting transfers between devices, body(): lax.all_to_all(msg, SAMPLE, split_axis=0, concat_axis=0, tiled=True)  7.95 us
    pallas_call x1, Pallas kernels, body(): call(expand_kernel, pltpu.HBM((ROWS, 2 * ROWS), BF), (2 * ROWS * ROWS * R...  7.52 us
    pallas_call x1, Pallas kernels, body(): call(attend_kernel, pltpu.HBM((PEERS, MSG, 128), BF), (2 * ROWS * ROWS *...  5.48 us
  transfers between devices with their start and end apart: 14, of which 10 were waited for; matrix products, arithmetic and copies ran while one was open for 7% of the time, Pallas kernels for 21%

profile of v4, /device:TPU:1, one launch (start us, length us, event | category | flops | bytes accessed | tf_op | source)
XLA Modules:
  0.0 114.1 jit_solution(8806207147072444746)
XLA Ops:
  0.6 0.0 copy-start
  0.7 2.6 %shard_map.104 = (s32[32,128]{1,0:T(8,128)}, f32[48,128]{1,0:T(8,128)}, s32[16,128]{1,0:T(8,128)}) custom-call(s32[1,1024]{1,0:T(1,128)} %bitcast.40, s32[4,1024]{1,0:T(4,128)} %bitcast.39), custom_call_target="tpu_custom_call" | custom-call | flops 400000000 | bytes 1000000 | tf_op jit(solution)/shard_map/pallas_call | solution.py:449
  3.3 12.0 %all-to-all-start = ((s32[32,1,128]{2,1,0:T(1,128)}), s32[32,1,128]{2,1,0:T(1,128)S(1)}, u32[]{:S(2)}, u32[]{:S(2)}) async-start(s32[32,1,128]{2,1,0:T(1,128)} %bitcast.38), calls=%async_computation | async-start | bytes 32768 | tf_op jit(solution)/shard_map/all_to_all | solution.py:469
  15.3 3.1 %shard_map.110 = (bf16[640,1024]{1,0:T(8,128)(2,1)}, bf16[640,1024]{1,0:T(8,128)(2,1)}) custom-call(bf16[1024,512]{1,0:T(8,128)(2,1)} %up_ref.3, bf16[512,1024]{1,0:T(8,128)(2,1)} %down_ref.3, bf16[128,1024]{1,0:T(8,128)(2,1)} %own_ref.1), custom_call_target="tpu_custom_call" | custom-call | bytes 5000000 | tf_op jit(solution)/shard_map/pallas_call | solution.py:458
  18.5 1.3 %collective-permute-start.4 = (bf16[640,1024]{1,0:T(8,128)(2,1)}, bf16[640,1024]{1,0:T(8,128)(2,1)}, u32[]{:S(2)}, u32[]{:S(2)}) collective-permute-start(bf16[640,1024]{1,0:T(8,128)(2,1)} %get-tuple-element.24), channel_id=1, source_target_pairs={{0,2},{2,4},{4,6},{6,0},{1,3},{3,5},{5,7},{7,1},{8,10},{10,12},{12... | collective-permute-start | bytes 3932168 | tf_op jit(solution)/shard_map/ppermute | solution.py:439
  19.8 1.5 %collective-permute-start.5 = (bf16[640,1024]{1,0:T(8,128)(2,1)}, bf16[640,1024]{1,0:T(8,128)(2,1)}, u32[]{:S(2)}, u32[]{:S(2)}) collective-permute-start(bf16[640,1024]{1,0:T(8,128)(2,1)} %get-tuple-element.25), channel_id=1, source_target_pairs={{0,6},{2,0},{4,2},{6,4},{1,7},{3,1},{5,3},{7,5},{8,14},{10,8},{12,... | collective-permute-start | bytes 3932168 | tf_op jit(solution)/shard_map/ppermute | solution.py:439
  21.2 0.5 fusion
  21.7 0.0 copy-done
  21.7 1.3 %fusion.9 = bf16[3,1024,128]{2,1,0:T(8,128)(2,1)S(1)} fusion(bf16[3,1024,128]{2,1,0:T(8,128)(2,1)S(1)} %copy-done, bf16[1024,1024]{1,0:T(8,128)(2,1)S(1)} %copy-done.1, f32[1024]{0:T(1024)S(1)} %add_rsqrt_fusion), kind=kOutput, calls=%fused_computation.10 | convolution fusion | flops 808845312 | bytes 3674112 | tf_op jit(solution)/shard_map/rd,tdc->trc/dot_general | solution.py:475
  23.0 1.0 slice_bitcast_fusion.3
  24.1 0.0 all-to-all-done
  24.1 1.7 %shard_map.106 = bf16[1536,128]{1,0:T(8,128)(2,1)} custom-call(s32[32,128]{1,0:T(8,128)S(1)} %bitcast.33, bf16[1024,128]{1,0:T(8,128)(2,1)S(1)} %get-tuple-element.40.q_ref), custom_call_target="tpu_custom_call" | custom-call | flops 402653184 | bytes 1000000 | tf_op jit(solution)/shard_map/pallas_call | solution.py:494
  25.8 9.2 %all-to-all-start.1 = ((bf16[32,48,128]{2,1,0:T(8,128)(2,1)}), bf16[32,48,128]{2,1,0:T(8,128)(2,1)S(1)}, u32[]{:S(2)}, u32[]{:S(2)}) async-start(bf16[32,48,128]{2,1,0:T(8,128)(2,1)} %bitcast.37), calls=%async_computation.1 | async-start | bytes 786432 | tf_op jit(solution)/shard_map/all_to_all | solution.py:502
  35.1 3.6 %copy_bitcast_fusion = (bf16[1024,1024]{1,0:T(8,128)(2,1)S(1)}, bf16[1024,1024]{1,0:T(8,128)(2,1)S(1)}) fusion(bf16[128,8,8,128]{3,2,1,0:T(8,128)(2,1)} %bitcast.35, bf16[128,8,8,128]{3,2,1,0:T(8,128)(2,1)} %bitcast.36), kind=kLoop, calls=%fused_computation.6 | loop fusion | bytes 8388608 | tf_op jit(solution)/shard_map/reshape | solution.py:479
  38.7 7.5 %shard_map.107.kv_ref = bf16[1024,2048]{1,0:T(8,128)(2,1)} custom-call(f32[48,128]{1,0:T(8,128)} %get-tuple-element.20.par_ref, bf16[1024,1024]{1,0:T(8,128)(2,1)S(1)} %get-tuple-element.42.k_ref, bf16[1024,1024]{1,0:T(8,128)(2,1)S(1)} %get-tuple-element.41.v_ref), custom_call_target="tpu_custom_call" | custom-call | flops 4294967296 | bytes 12000000 | tf_op jit(solution)/shard_map/pallas_call | solution.py:480
  46.2 1.4 %all-to-all-done.1.q_ref = bf16[32,48,128]{2,1,0:T(8,128)(2,1)S(1)} async-done(((bf16[32,48,128]{2,1,0:T(8,128)(2,1)}), bf16[32,48,128]{2,1,0:T(8,128)(2,1)S(1)}, u32[]{:S(2)}, u32[]{:S(2)}) %all-to-all-start.1) | async-done | bytes 393248 | tf_op jit(solution)/shard_map/all_to_all | solution.py:502
  47.6 5.5 %shard_map.108 = bf16[32,64,128]{2,1,0:T(8,128)(2,1)} custom-call(s32[16,128]{1,0:T(8,128)} %get-tuple-element.19.full_hbm, bf16[32,48,128]{2,1,0:T(8,128)(2,1)S(1)} %all-to-all-done.1.q_ref, bf16[1024,2048]{1,0:T(8,128)(2,1)} %shard_map.107.kv_ref), custom_call_target="tpu_custom_call" | custom-call | flops 268435456 | bytes 8000000 | tf_op jit(solution)/shard_map/pallas_call | solution.py:510
  53.1 8.0 %all-to-all-start.2 = ((bf16[32,64,128]{2,1,0:T(8,128)(2,1)}), bf16[32,64,128]{2,1,0:T(8,128)(2,1)}, u32[]{:S(2)}, u32[]{:S(2)}) async-start(bf16[32,64,128]{2,1,0:T(8,128)(2,1)} %shard_map.108), calls=%async_computation.2 | async-start | bytes 1048576 | tf_op jit(solution)/shard_map/all_to_all | solution.py:524
  61.0 1.8 %collective-permute-start.3 = (bf16[128,1024]{1,0:T(8,128)(2,1)S(1)}, bf16[128,1024]{1,0:T(8,128)(2,1)S(1)}, u32[]{:S(2)}, u32[]{:S(2)}) collective-permute-start(bf16[128,1024]{1,0:T(8,128)(2,1)S(1)} %copy-done.4), channel_id=1, source_target_pairs={{0,4},{2,6},{4,0},{6,2},{1,5},{3,7},{5,1},{7,3},{8,12},{10,14},{12... | collective-permute-start | bytes 786440 | tf_op jit(solution)/shard_map/ppermute | solution.py:439
  62.9 3.3 %shard_map.105 = (bf16[1024,128]{1,0:T(8,128)(2,1)}, s32[16,128]{1,0:T(8,128)}) custom-call(s32[32,128]{1,0:T(8,128)S(1)} %bitcast.34, bf16[1024,128]{1,0:T(8,128)(2,1)} %copy-done.5, bf16[1024,128]{1,0:T(8,128)(2,1)} %get-tuple-element.39.k_ref), custom_call_target="tpu_custom_call" | custom-call | flops 1000000000 | bytes 2000000 | tf_op jit(solution)/shard_map/pallas_call | solution.py:504
  66.2 9.1 %all-to-all-done.2.msg_hbm = bf16[32,64,128]{2,1,0:T(8,128)(2,1)} async-done(((bf16[32,64,128]{2,1,0:T(8,128)(2,1)}), bf16[32,64,128]{2,1,0:T(8,128)(2,1)}, u32[]{:S(2)}, u32[]{:S(2)}) %all-to-all-start.2) | async-done | bytes 524320 | tf_op jit(solution)/shard_map/all_to_all | solution.py:524
  75.3 3.3 %shard_map.109 = (bf16[512,128]{1,0:T(8,128)(2,1)S(1)}, bf16[512,128]{1,0:T(8,128)(2,1)S(1)}) custom-call(s32[16,128]{1,0:T(8,128)} %get-tuple-element.18.full_hbm, bf16[32,64,128]{2,1,0:T(8,128)(2,1)} %all-to-all-done.2.msg_hbm, bf16[1024,128]{1,0:T(8,128)(2,1)} %get-tuple-element.21.place_hbm, bf16[1024,128]{1,0:T(8,128)(2,1)} %get-tuple-element.38.v_hbm), custom_call_target="tpu_custom_call" | custom-call | flops 402653184 | bytes 5000000 | tf_op jit(solution)/shard_map/pallas_call | solution.py:526
  78.6 0.1 collective-permute-start
  78.7 2.6 %collective-permute-start.1 = (bf16[512,128]{1,0:T(8,128)(2,1)S(1)}, bf16[512,128]{1,0:T(8,128)(2,1)S(1)}, u32[]{:S(2)}, u32[]{:S(2)}) collective-permute-start(bf16[512,128]{1,0:T(8,128)(2,1)S(1)} %get-tuple-element.23), channel_id=1, source_target_pairs={{0,6},{2,0},{4,2},{6,4},{1,7},{3,1},{5,3},{7,5},{8,14},{10,8},{12,... | collective-permute-start | bytes 393224 | tf_op jit(solution)/shard_map/ppermute | solution.py:439
  81.3 0.0 collective-permute-done.3.two_ref
  81.3 0.4 collective-permute-start.2
  81.7 0.0 collective-permute-done.4.left_ref
  81.7 0.0 collective-permute-done.5.right_ref
  81.7 2.0 %collective-permute-done.a1 = bf16[512,128]{1,0:T(8,128)(2,1)S(1)} collective-permute-done((bf16[512,128]{1,0:T(8,128)(2,1)S(1)}, bf16[512,128]{1,0:T(8,128)(2,1)S(1)}, u32[]{:S(2)}, u32[]{:S(2)}) %collective-permute-start) | collective-permute-done | bytes 131104 | tf_op jit(solution)/shard_map/ppermute | solution.py:439
  83.7 1.0 collective-permute-done.1.a2
  84.7 2.0 %collective-permute-done.2.a3 = bf16[512,128]{1,0:T(8,128)(2,1)S(1)} collective-permute-done((bf16[512,128]{1,0:T(8,128)(2,1)S(1)}, bf16[512,128]{1,0:T(8,128)(2,1)S(1)}, u32[]{:S(2)}, u32[]{:S(2)}) %collective-permute-start.2) | collective-permute-done | bytes 131104 | tf_op jit(solution)/shard_map/ppermute | solution.py:439
  86.7 1.8 %shard_map.111.p_ref = bf16[512,1024]{1,0:T(8,128)(2,1)S(1)} custom-call(bf16[512,128]{1,0:T(8,128)(2,1)S(1)} %get-tuple-element.22.a0, bf16[512,128]{1,0:T(8,128)(2,1)S(1)} %collective-permute-done.a1, bf16[512,128]{1,0:T(8,128)(2,1)S(1)} %collective-permute-done.1.a2, bf16[512,128]{1,0:T(8,128)(2,1)S(1)} %collective-permute-done.2.a3, ...), custom_call_target="tpu_custom_call" | custom-call | flops 600000000 | bytes 3000000 | tf_op jit(solution)/shard_map/pallas_call | solution.py:545
  88.4 0.0 copy-start.6
  88.5 6.5 %collective-permute-start.6 = (bf16[512,1024]{1,0:T(8,128)(2,1)S(1)}, bf16[512,1024]{1,0:T(8,128)(2,1)S(1)}, u32[]{:S(2)}, u32[]{:S(2)}) collective-permute-start(bf16[512,1024]{1,0:T(8,128)(2,1)S(1)} %shard_map.111.p_ref), channel_id=1, source_target_pairs={{0,1},{1,0},{2,3},{3,2},{4,5},{5,4},{6,7},{7,6},{8,9},{9,8},{10,11... | collective-permute-start | bytes 3145736 | tf_op jit(solution)/shard_map/ppermute | solution.py:439
  95.0 2.3 %collective-permute-done.6.r_ref = bf16[512,1024]{1,0:T(8,128)(2,1)S(1)} collective-permute-done((bf16[512,1024]{1,0:T(8,128)(2,1)S(1)}, bf16[512,1024]{1,0:T(8,128)(2,1)S(1)}, u32[]{:S(2)}, u32[]{:S(2)}) %collective-permute-start.6) | collective-permute-done | bytes 1048608 | tf_op jit(solution)/shard_map/ppermute | solution.py:439
  97.3 4.8 %shard_map.112 = (f32[4,512,128]{2,1,0:T(8,128)S(1)}, bf16[4,512,128]{2,1,0:T(8,128)(2,1)S(1)}) custom-call(bf16[1024,1024]{1,0:T(8,128)(2,1)S(1)} %copy-done.1, bf16[512,1024]{1,0:T(8,128)(2,1)S(1)} %shard_map.111.p_ref, bf16[512,1024]{1,0:T(8,128)(2,1)S(1)} %collective-permute-done.6.r_ref, bf16[1024,512]{1,0:T(8,128)(2,1)S(1)} %copy-done.2, ...), custom_call_target="tpu_custom_call" | custom-call | flops 2000000000 | bytes 10000000 | tf_op jit(solution)/shard_map/pallas_call | solution.py:564
  102.0 0.5 collective-permute-start.7
  102.5 1.5 %collective-permute-done.7.other_ref = bf16[4,512,128]{2,1,0:T(8,128)(2,1)S(1)} collective-permute-done((bf16[4,512,128]{2,1,0:T(8,128)(2,1)S(1)}, bf16[4,512,128]{2,1,0:T(8,128)(2,1)S(1)}, u32[]{:S(2)}, u32[]{:S(2)}) %collective-permute-start.7) | collective-permute-done | bytes 524320 | tf_op jit(solution)/shard_map/ppermute | solution.py:439
  104.1 0.1 shard_map.113
  104.1 0.1 collective-permute-start.8
  104.2 2.0 %collective-permute-start.9 = (bf16[512,128]{1,0:T(8,128)(2,1)S(1)}, bf16[512,128]{1,0:T(8,128)(2,1)S(1)}, u32[]{:S(2)}, u32[]{:S(2)}) collective-permute-start(bf16[512,128]{1,0:T(8,128)(2,1)S(1)} %get-tuple-element.30), channel_id=1, source_target_pairs={{0,4},{2,6},{4,0},{6,2},{1,5},{3,7},{5,1},{7,3},{8,12},{10,14},{12... | collective-permute-start | bytes 393224 | tf_op jit(solution)/shard_map/ppermute | solution.py:439
  106.2 0.7 collective-permute-start.10
  106.9 0.1 pad_maximum_fusion
  107.0 1.3 %copy.13 = bf16[1024,2,128]{2,1,0:T(2,128)(2,1)} copy(bf16[1024,2,128]{2,0,1:T(8,128)(2,1)S(1)} %pad_maximum_fusion) | data formatting | bytes 1048576
  108.3 2.5 %collective-permute-done.8.p1 = bf16[512,128]{1,0:T(8,128)(2,1)S(1)} collective-permute-done((bf16[512,128]{1,0:T(8,128)(2,1)S(1)}, bf16[512,128]{1,0:T(8,128)(2,1)S(1)}, u32[]{:S(2)}, u32[]{:S(2)}) %collective-permute-start.8) | collective-permute-done | bytes 131104 | tf_op jit(solution)/shard_map/ppermute | solution.py:439
  110.8 1.5 %collective-permute-done.9.p2 = bf16[512,128]{1,0:T(8,128)(2,1)S(1)} collective-permute-done((bf16[512,128]{1,0:T(8,128)(2,1)S(1)}, bf16[512,128]{1,0:T(8,128)(2,1)S(1)}, u32[]{:S(2)}, u32[]{:S(2)}) %collective-permute-start.9) | collective-permute-done | bytes 131104 | tf_op jit(solution)/shard_map/ppermute | solution.py:439
  112.3 1.0 collective-permute-done.10.p3
  113.3 0.8 shard_map.114
  (14 shorter events, 0.0 us)
Async XLA Ops:
  0.6 21.1 %copy-start = (bf16[3,1024,128]{2,1,0:T(8,128)(2,1)S(1)}, bf16[3,1024,128]{2,1,0:T(8,128)(2,1)}, u32[]{:S(2)}) copy-start(bf16[3,1024,128]{2,1,0:T(8,128)(2,1)} %param.14) | copy-start | bytes 2359300
  0.6 20.6 %copy-start.1 = (bf16[1024,1024]{1,0:T(8,128)(2,1)S(1)}, bf16[1024,1024]{1,0:T(8,128)(2,1)}, u32[]{:S(2)}) copy-start(bf16[1024,1024]{1,0:T(8,128)(2,1)} %x_ref.1) | copy-start | bytes 6291460
  3.3 20.8 %all-to-all-start = ((s32[32,1,128]{2,1,0:T(1,128)}), s32[32,1,128]{2,1,0:T(1,128)S(1)}, u32[]{:S(2)}, u32[]{:S(2)}) async-start(s32[32,1,128]{2,1,0:T(1,128)} %bitcast.38), calls=%async_computation | async-start | bytes 32768 | tf_op jit(solution)/shard_map/all_to_all | solution.py:469
  18.5 63.2 %collective-permute-start.4 = (bf16[640,1024]{1,0:T(8,128)(2,1)}, bf16[640,1024]{1,0:T(8,128)(2,1)}, u32[]{:S(2)}, u32[]{:S(2)}) collective-permute-start(bf16[640,1024]{1,0:T(8,128)(2,1)} %get-tuple-element.24), channel_id=1, source_target_pairs={{0,2},{2,4},{4,6},{6,0},{1,3},{3,5},{5,7},{7,1},{8,10},{10,12},{12... | collective-permute-start | bytes 3932168 | tf_op jit(solution)/shard_map/ppermute | solution.py:439
  19.8 62.0 %collective-permute-start.5 = (bf16[640,1024]{1,0:T(8,128)(2,1)}, bf16[640,1024]{1,0:T(8,128)(2,1)}, u32[]{:S(2)}, u32[]{:S(2)}) collective-permute-start(bf16[640,1024]{1,0:T(8,128)(2,1)} %get-tuple-element.25), channel_id=1, source_target_pairs={{0,6},{2,0},{4,2},{6,4},{1,7},{3,1},{5,3},{7,5},{8,14},{10,8},{12,... | collective-permute-start | bytes 3932168 | tf_op jit(solution)/shard_map/ppermute | solution.py:439
  24.1 1.8 %copy-start.5 = (bf16[1024,128]{1,0:T(8,128)(2,1)}, bf16[1024,128]{1,0:T(8,128)(2,1)S(1)}, u32[]{:S(2)}) copy-start(bf16[1024,128]{1,0:T(8,128)(2,1)S(1)} %get-tuple-element.40.q_ref) | copy-start | bytes 786436
  25.8 21.7 %all-to-all-start.1 = ((bf16[32,48,128]{2,1,0:T(8,128)(2,1)}), bf16[32,48,128]{2,1,0:T(8,128)(2,1)S(1)}, u32[]{:S(2)}, u32[]{:S(2)}) async-start(bf16[32,48,128]{2,1,0:T(8,128)(2,1)} %bitcast.37), calls=%async_computation.1 | async-start | bytes 786432 | tf_op jit(solution)/shard_map/all_to_all | solution.py:502
  47.6 13.5 %copy-start.4 = (bf16[128,1024]{1,0:T(8,128)(2,1)S(1)}, bf16[128,1024]{1,0:T(8,128)(2,1)}, u32[]{:S(2)}) copy-start(bf16[128,1024]{1,0:T(8,128)(2,1)} %own_ref.1) | copy-start | bytes 786436
  53.1 22.2 %all-to-all-start.2 = ((bf16[32,64,128]{2,1,0:T(8,128)(2,1)}), bf16[32,64,128]{2,1,0:T(8,128)(2,1)}, u32[]{:S(2)}, u32[]{:S(2)}) async-start(bf16[32,64,128]{2,1,0:T(8,128)(2,1)} %shard_map.108), calls=%async_computation.2 | async-start | bytes 1048576 | tf_op jit(solution)/shard_map/all_to_all | solution.py:524
  61.0 20.3 %collective-permute-start.3 = (bf16[128,1024]{1,0:T(8,128)(2,1)S(1)}, bf16[128,1024]{1,0:T(8,128)(2,1)S(1)}, u32[]{:S(2)}, u32[]{:S(2)}) collective-permute-start(bf16[128,1024]{1,0:T(8,128)(2,1)S(1)} %copy-done.4), channel_id=1, source_target_pairs={{0,4},{2,6},{4,0},{6,2},{1,5},{3,7},{5,1},{7,3},{8,12},{10,14},{12... | collective-permute-start | bytes 786440 | tf_op jit(solution)/shard_map/ppermute | solution.py:439
  78.6 5.1 %collective-permute-start = (bf16[512,128]{1,0:T(8,128)(2,1)S(1)}, bf16[512,128]{1,0:T(8,128)(2,1)S(1)}, u32[]{:S(2)}, u32[]{:S(2)}) collective-permute-start(bf16[512,128]{1,0:T(8,128)(2,1)S(1)} %get-tuple-element.23), channel_id=1, source_target_pairs={{0,2},{2,4},{4,6},{6,0},{1,3},{3,5},{5,7},{7,1},{8,10},{10,12},{12... | collective-permute-start | bytes 393224 | tf_op jit(solution)/shard_map/ppermute | solution.py:439
  78.7 5.9 %collective-permute-start.1 = (bf16[512,128]{1,0:T(8,128)(2,1)S(1)}, bf16[512,128]{1,0:T(8,128)(2,1)S(1)}, u32[]{:S(2)}, u32[]{:S(2)}) collective-permute-start(bf16[512,128]{1,0:T(8,128)(2,1)S(1)} %get-tuple-element.23), channel_id=1, source_target_pairs={{0,6},{2,0},{4,2},{6,4},{1,7},{3,1},{5,3},{7,5},{8,14},{10,8},{12,... | collective-permute-start | bytes 393224 | tf_op jit(solution)/shard_map/ppermute | solution.py:439
  81.3 15.9 %copy-start.2 = (bf16[1024,512]{1,0:T(8,128)(2,1)S(1)}, bf16[1024,512]{1,0:T(8,128)(2,1)}, u32[]{:S(2)}) copy-start(bf16[1024,512]{1,0:T(8,128)(2,1)} %up_ref.3) | copy-start | bytes 3145732
  81.3 15.9 %copy-start.3 = (bf16[512,1024]{1,0:T(8,128)(2,1)S(1)}, bf16[512,1024]{1,0:T(8,128)(2,1)}, u32[]{:S(2)}) copy-start(bf16[512,1024]{1,0:T(8,128)(2,1)} %down_ref.3) | copy-start | bytes 3145732
  81.3 5.3 %collective-permute-start.2 = (bf16[512,128]{1,0:T(8,128)(2,1)S(1)}, bf16[512,128]{1,0:T(8,128)(2,1)S(1)}, u32[]{:S(2)}, u32[]{:S(2)}) collective-permute-start(bf16[512,128]{1,0:T(8,128)(2,1)S(1)} %get-tuple-element.22.a0), channel_id=1, source_target_pairs={{0,4},{2,6},{4,0},{6,2},{1,5},{3,7},{5,1},{7,3},{8,12},{10,14},{12... | collective-permute-start | bytes 393224 | tf_op jit(solution)/shard_map/ppermute | solution.py:439
  88.4 18.5 %copy-start.6 = (bf16[1024,1,128]{2,0,1:T(8,128)(2,1)S(1)}, bf16[1024,1,128]{2,0,1:T(8,128)(2,1)}, u32[]{:S(2)}) copy-start(bf16[1024,1,128]{2,0,1:T(8,128)(2,1)} %get-tuple-element.36) | copy-start | bytes 786436
  88.4 18.5 %copy-start.7 = (bf16[1024,1,128]{2,0,1:T(8,128)(2,1)S(1)}, bf16[1024,1,128]{2,0,1:T(8,128)(2,1)}, u32[]{:S(2)}) copy-start(bf16[1024,1,128]{2,0,1:T(8,128)(2,1)} %get-tuple-element.37) | copy-start | bytes 786436
  88.5 8.8 %collective-permute-start.6 = (bf16[512,1024]{1,0:T(8,128)(2,1)S(1)}, bf16[512,1024]{1,0:T(8,128)(2,1)S(1)}, u32[]{:S(2)}, u32[]{:S(2)}) collective-permute-start(bf16[512,1024]{1,0:T(8,128)(2,1)S(1)} %shard_map.111.p_ref), channel_id=1, source_target_pairs={{0,1},{1,0},{2,3},{3,2},{4,5},{5,4},{6,7},{7,6},{8,9},{9,8},{10,11... | collective-permute-start | bytes 3145736 | tf_op jit(solution)/shard_map/ppermute | solution.py:439
  102.0 2.0 %collective-permute-start.7 = (bf16[4,512,128]{2,1,0:T(8,128)(2,1)S(1)}, bf16[4,512,128]{2,1,0:T(8,128)(2,1)S(1)}, u32[]{:S(2)}, u32[]{:S(2)}) collective-permute-start(bf16[4,512,128]{2,1,0:T(8,128)(2,1)S(1)} %get-tuple-element.27), channel_id=1, source_target_pairs={{0,1},{1,0},{2,3},{3,2},{4,5},{5,4},{6,7},{7,6},{8,9},{9,8},{10,11... | collective-permute-start | bytes 1572872 | tf_op jit(solution)/shard_map/ppermute | solution.py:439
  104.1 6.7 %collective-permute-start.8 = (bf16[512,128]{1,0:T(8,128)(2,1)S(1)}, bf16[512,128]{1,0:T(8,128)(2,1)S(1)}, u32[]{:S(2)}, u32[]{:S(2)}) collective-permute-start(bf16[512,128]{1,0:T(8,128)(2,1)S(1)} %get-tuple-element.29), channel_id=1, source_target_pairs={{0,2},{2,4},{4,6},{6,0},{1,3},{3,5},{5,7},{7,1},{8,10},{10,12},{12... | collective-permute-start | bytes 393224 | tf_op jit(solution)/shard_map/ppermute | solution.py:439
  104.2 8.1 %collective-permute-start.9 = (bf16[512,128]{1,0:T(8,128)(2,1)S(1)}, bf16[512,128]{1,0:T(8,128)(2,1)S(1)}, u32[]{:S(2)}, u32[]{:S(2)}) collective-permute-start(bf16[512,128]{1,0:T(8,128)(2,1)S(1)} %get-tuple-element.30), channel_id=1, source_target_pairs={{0,4},{2,6},{4,0},{6,2},{1,5},{3,7},{5,1},{7,3},{8,12},{10,14},{12... | collective-permute-start | bytes 393224 | tf_op jit(solution)/shard_map/ppermute | solution.py:439
  106.2 7.1 %collective-permute-start.10 = (bf16[512,128]{1,0:T(8,128)(2,1)S(1)}, bf16[512,128]{1,0:T(8,128)(2,1)S(1)}, u32[]{:S(2)}, u32[]{:S(2)}) collective-permute-start(bf16[512,128]{1,0:T(8,128)(2,1)S(1)} %get-tuple-element.31), channel_id=1, source_target_pairs={{0,6},{2,0},{4,2},{6,4},{1,7},{3,1},{5,3},{7,5},{8,14},{10,8},{12,... | collective-permute-start | bytes 393224 | tf_op jit(solution)/shard_map/ppermute | solution.py:439

commit v5 on v4

--- a/solution.py
+++ b/solution.py
@@ -114,29 +114,32 @@
 
 
 def pack_kernel(up_ref, down_ref, wo_ref, right_ref, left_ref, stage, sems):
-    writes = []
+    loads, stores = [], []
+    for n, out in enumerate((right_ref, left_ref)):
+        half = pl.ds(n * 256, 256)
+        pairs = [(up_ref.at[pl.ds(k * 256, 256), half], pl.ds(k * 256, 256)) for k in range(4)]
+        pairs = [(a, stage.at[n, pl.ds(0, 256), b]) for a, b in pairs]
+        pairs.append((down_ref.at[half], stage.at[n, pl.ds(256, 256)]))
+        pairs.append((wo_ref, stage.at[n, pl.ds(512, 128)]))
+        loads.append(
+            [pltpu.make_async_copy(a, b, sems.at[n * 9 + i]) for i, (a, b) in enumerate(pairs)]
+        )
+        parts = [pl.ds(0, 256), pl.ds(256, 256), pl.ds(512, 128)]
+        stores.append(
+            [
+                pltpu.make_async_copy(stage.at[n, p], out.at[p], sems.at[n * 9 + 6 + i])
+                for i, p in enumerate(parts)
+            ]
+        )
+    for copy in loads[0] + loads[1]:
+        copy.start()
     for n in range(2):
-        half = pl.ds(n * 256, 256)
-        pairs = [(down_ref.at[half], stage.at[n, pl.ds(256, 256)])]
-        pairs.append((wo_ref, stage.at[n, pl.ds(512, 128)]))
-        for k in range(4):
-            block = pl.ds(k * 256, 256)
-            pairs.append((up_ref.at[block, half], stage.at[n, pl.ds(0, 256), block]))
-        copies = [
-            pltpu.make_async_copy(a, b, sems.at[n * 7 + i]) for i, (a, b) in enumerate(pairs)
-        ]
-        for copy in copies:
-            copy.start()
-        writes.append((copies, (right_ref, left_ref)[n]))
-    ends = []
-    for n, (copies, target) in enumerate(writes):
-        for copy in copies:
-            copy.wait()
-        end = pltpu.make_async_copy(stage.at[n], target, sems.at[n * 7 + 6])
-        end.start()
-        ends.append(end)
-    for end in ends:
-        end.wait()
+        for i in range(3):
+            for copy in (loads[n][:4], loads[n][4:5], loads[n][5:])[i]:
+                copy.wait()
+            stores[n][i].start()
+    for copy in stores[0] + stores[1]:
+        copy.wait()
 
 
 def column(lists, count, depth):
@@ -147,25 +150,55 @@
     return jnp.sum(picked, axis=2, keepdims=True).reshape(count * depth, 1)
 
 
-def expand_kernel(par_ref, k_ref, v_ref, out_ref, col_ref):
-    step = pl.program_id(0)
-
-    @pl.when(step < 2)
-    def _():
-        lists = par_ref[pl.ds(pl.multiple_of(step * 16, 16), 16), :]
-        col_ref[...] = jnp.broadcast_to(column(lists, 16, LOW), (256, 128))
-
-    @pl.when(step >= 2)
-    def _():
-        lists = par_ref[pl.ds(pl.multiple_of(PEERS + (step - 2) * 8, 8), 8), :]
-        col_ref[...] = jnp.broadcast_to(column(lists, 8, REST), (256, 128))
-
-    hot = (col_ref[:, 0:1] == iota((256, ROWS), 1).astype(F32)).astype(F32).astype(BF)
-    out_ref[:, :ROWS] = jnp.dot(hot, k_ref[...], preferred_element_type=F32).astype(BF)
-    out_ref[:, ROWS:] = jnp.dot(hot, v_ref[...], preferred_element_type=F32).astype(BF)
-
-
-def query_kernel(recv_ref, q_ref, out_ref, stage, sems):
+def expand_kernel(par_ref, k_hbm, v_hbm, out_ref, raw, flat, hot_ref, stage, sems):
+    n = 256
+    loads = [
+        pltpu.make_async_copy(a, raw.at[t], sems.at[t]) for t, a in enumerate((k_hbm, v_hbm))
+    ]
+    for copy in loads:
+        copy.start()
+    low = column(par_ref[:PEERS, :], PEERS, LOW)
+    rest = column(par_ref[PEERS:, :], FULL, REST)
+    parents = iota((n, ROWS), 1).astype(F32)
+    for i in range(4):
+        col = low[i * n : (i + 1) * n] if i < 2 else rest[(i - 2) * n : (i - 1) * n]
+        hot_ref[i] = (col == parents).astype(F32).astype(BF)
+    copies = []
+
+    def gather(t, i):
+        got = jnp.dot(hot_ref[i], flat[t], preferred_element_type=F32)
+        stage[t, i] = got.astype(BF)
+        to = out_ref.at[pl.ds(i * n, n), pl.ds(t * ROWS, ROWS)]
+        copies.append(pltpu.make_async_copy(stage.at[t, i], to, sems.at[2 + t * 4 + i]))
+        copies[-1].start()
+
+    loads[0].wait()
+    flat[0] = raw[0].reshape(ROWS, ROWS)
+    gather(0, 0)
+    gather(0, 1)
+    loads[1].wait()
+    flat[1] = raw[1].reshape(ROWS, ROWS)
+    gather(0, 2)
+    gather(0, 3)
+    for i in range(4):
+        gather(1, i)
+    for copy in copies:
+        copy.wait()
+
+
+def row_scales(x):
+    x = x.astype(F32)
+    return lax.rsqrt(jnp.mean(x * x, axis=-1, keepdims=True) + 1e-05)
+
+
+def project_query_kernel(x_ref, w_ref, out_ref):
+    for n in range(4):
+        at = pl.ds(n * 256, 256)
+        got = jnp.dot(x_ref[at], w_ref[0], preferred_element_type=F32)
+        out_ref[at] = (got * row_scales(x_ref[at])).astype(BF)
+
+
+def query_kernel(recv_ref, q_ref, after_ref, out_ref, stage, sems):
     lists = recv_ref[...].astype(F32)
     slots = iota((8 * CAP, ROWS), 1).astype(F32)
     copies = []
@@ -181,7 +214,13 @@
         copy.wait()
 
 
-def place_kernel(recv_ref, q_ref, k_ref, out_ref, full_ref):
+def place_kernel(recv_ref, x_ref, w_ref, q_ref, out_ref, full_ref, own_k_ref, own_v_ref):
+    for n in range(4):
+        at = pl.ds(n * 256, 256)
+        scale = row_scales(x_ref[at])
+        for t, own_ref in ((1, own_k_ref), (2, own_v_ref)):
+            got = jnp.dot(x_ref[at], w_ref[t], preferred_element_type=F32)
+            own_ref[at] = (got * scale).astype(BF)
     slot = recv_ref[...]
     last = jnp.where(slot[:, CAP - 1 : CAP] >= 0, 1.0, 0.0)
     full_ref[...] = peer_numbers(full_peers(last))
@@ -204,7 +243,7 @@
     src, place, rank = (column(wide[n * 32 : n * 32 + 32], 32, 32) for n in range(3))
     rest = float(PEERS * LOW - LOW) + rank * float(REST) + place
     pos = jnp.where(place < float(LOW), src * float(LOW) + place, rest)
-    prod = q_ref[...].astype(F32) * k_ref[...].astype(F32) * (1.0 / HD**0.5)
+    prod = q_ref[...].astype(F32) * own_k_ref[...].astype(F32) * (1.0 / HD**0.5)
     s0 = jnp.sum(prod[:, :HD], axis=1, keepdims=True)
     s1 = jnp.sum(prod[:, HD:], axis=1, keepdims=True)
     high = jnp.floor(pos * (1.0 / 32.0))
@@ -439,10 +478,6 @@
     return lax.ppermute(x, axis, [(i, (i + by) % size) for i in range(size)])
 
 
-def rms_rows(stream):
-    return stream * lax.rsqrt(jnp.mean(stream * stream, axis=-1, keepdims=True) + 1e-05)
-
-
 def body(stream_in, keys, values, counts, slots, w_qkv, w_out, w_up, w_down):
     vmem = pl.BlockSpec(memory_space=pltpu.VMEM)
     hbm = pl.BlockSpec(memory_space=pltpu.HBM)
@@ -455,57 +490,64 @@
         ),
         (4 * 10**8, 10**6),
     )(keep(counts.reshape(1, ROWS), pltpu.HBM), keep(slots.T, pltpu.HBM))
+    recv = lax.all_to_all(
+        send.reshape(PEERS, 1, 128), SAMPLE, split_axis=0, concat_axis=0, tiled=True
+    ).reshape(PEERS, 128)
+
+    query = call(
+        project_query_kernel,
+        sds((ROWS, 128), BF),
+        (3 * 10**8, 3 * 10**6),
+        in_specs=[vmem, vmem],
+        out_specs=vmem,
+    )(stream_in, w_qkv)
     for_right, for_left = call(
         pack_kernel,
         (pltpu.HBM((640, ROWS), BF), pltpu.HBM((640, ROWS), BF)),
         (0, 5 * 10**6),
-        in_specs=[hbm, hbm, hbm],
+        in_specs=[hbm] * 3,
         out_specs=(hbm, hbm),
-        scratch_shapes=[pltpu.VMEM((2, 640, ROWS), BF), pltpu.SemaphoreType.DMA((14,))],
+        scratch_shapes=[pltpu.VMEM((2, 640, ROWS), BF), pltpu.SemaphoreType.DMA((18,))],
     )(*(keep(w, pltpu.HBM) for w in (w_up, w_down, w_out)))
-    left = shift(for_right, "x", 1, 4)
-    right = shift(for_left, "x", 3, 4)
-    wo_two = shift(w_out, "x", 2, 4)
-    recv = lax.all_to_all(
-        send.reshape(PEERS, 1, 128), SAMPLE, split_axis=0, concat_axis=0, tiled=True
-    ).reshape(PEERS, 128)
-
-    stream = stream_in.astype(F32)
-    normed = rms_rows(stream).astype(BF)
-    projected = jnp.einsum("rd,tdc->trc", normed, w_qkv, preferred_element_type=F32).astype(BF)
-    query, own_key, own_value = projected[0], projected[1], projected[2]
-    new_kv = jnp.stack([own_key, own_value], axis=1)
-
-    flat_keys, flat_values = keys.reshape(ROWS, ROWS), values.reshape(ROWS, ROWS)
+    q_send = call(
+        query_kernel,
+        pltpu.HBM((ITEMS, 128), BF),
+        (2 * ITEMS * ROWS * 128, 10**6),
+        in_specs=[vmem, vmem, hbm],
+        out_specs=hbm,
+        scratch_shapes=[pltpu.VMEM((ITEMS, 128), BF), pltpu.SemaphoreType.DMA((4,))],
+    )(recv, query, keep(for_left, pltpu.HBM))
     kv = call(
         expand_kernel,
         pltpu.HBM((ROWS, 2 * ROWS), BF),
         (2 * ROWS * ROWS * ROWS * 2, 12 * 10**6),
-        grid=(4,),
-        in_specs=[
-            pl.BlockSpec((PEERS + FULL, 128), lambda i: (0, 0)),
-            pl.BlockSpec((ROWS, ROWS), lambda i: (0, 0)),
-            pl.BlockSpec((ROWS, ROWS), lambda i: (0, 0)),
+        in_specs=[vmem, hbm, hbm],
+        out_specs=hbm,
+        scratch_shapes=[
+            pltpu.VMEM((2, ROWS, 8, 128), BF),
+            pltpu.VMEM((2, ROWS, ROWS), BF),
+            pltpu.VMEM((4, 256, ROWS), BF),
+            pltpu.VMEM((2, 4, 256, ROWS), BF),
+            pltpu.SemaphoreType.DMA((10,)),
         ],
-        out_specs=pl.BlockSpec((256, 2 * ROWS), lambda i: (i, 0)),
-        scratch_shapes=[pltpu.VMEM((256, 128), F32)],
-    )(keep(par, pltpu.HBM), flat_keys, flat_values)
-
-    q_send = call(
-        query_kernel,
-        pltpu.HBM((ITEMS, 128), BF),
-        (2 * ITEMS * ROWS * 128, 10**6),
-        in_specs=[vmem, vmem],
-        out_specs=hbm,
-        scratch_shapes=[pltpu.VMEM((ITEMS, 128), BF), pltpu.SemaphoreType.DMA((4,))],
-    )(recv, query)
+    )(*(keep(a, pltpu.HBM) for a in (par, keys, values)))
+    left = shift(for_right, "x", 1, 4)
+    right = shift(for_left, "x", 3, 4)
+    wo_two = shift(w_out, "x", 2, 4)
+
     q_recv = lax.all_to_all(q_send, SAMPLE, split_axis=0, concat_axis=0, tiled=True)
 
-    places, your_full = call(
+    places, your_full, own_key, own_value = call(
         place_kernel,
-        (pltpu.HBM((ROWS, 128), BF), pltpu.HBM((FULL, 128), jnp.int32)),
-        (10**9, 2 * 10**6),
-    )(recv, keep(query, pltpu.HBM), keep(own_key, pltpu.HBM))
+        (
+            pltpu.HBM((ROWS, 128), BF),
+            pltpu.HBM((FULL, 128), jnp.int32),
+            sds((ROWS, 128), BF),
+            pltpu.HBM((ROWS, 128), BF),
+        ),
+        (2 * 10**9, 4 * 10**6),
+    )(recv, stream_in, w_qkv, keep(query, pltpu.HBM))
+    new_kv = jnp.stack([own_key, own_value], axis=1)
 
     msg = call(
         attend_kernel,

time: 115 us -> 111 us (0.965)
  starting transfers between devices: 46.6 us -> 41.5 us
  local copies, waits for them, and re-layouts: 5.99 us -> 2.08 us
  waiting for transfers between devices: 24.3 us -> 27.8 us
  Pallas kernels: 34.5 us -> 37.7 us
  matrix products: 1.29 us -> 0 us
    all_to_all x1, waiting for transfers between devices: 0.01 us -> 4.79 us  [body(): lax.all_to_all(send.reshape(PEERS, 1, 128), SAMPLE, split_axis=0, concat_...]
    all_to_all x1, starting transfers between devices: 9.23 us -> 4.45 us  [body(): lax.all_to_all(q_send, SAMPLE, split_axis=0, concat_axis=0, tiled=True)]
    reshape x1 -> x0, local copies, waits for them, and re-layouts: 3.57 us -> none  [body(): values.reshape(ROWS, ROWS)]
    all_to_all x1, waiting for transfers between devices: 9.08 us -> 6.68 us  [body(): lax.all_to_all(msg, SAMPLE, split_axis=0, concat_axis=0, tiled=True)]
    pallas_call x1, Pallas kernels: 3.32 us -> 5.08 us  [body(): call(place_kernel, (pltpu.HBM((ROWS, 128), BF), pltpu.HBM((FULL, 128), jn...]
    dot_general x1 -> x0, matrix products: 1.29 us -> none  [body(): jnp.einsum('rd,tdc->trc', normed, w_qkv, preferred_element_type=F32)]
  transfers between devices with their start and end apart: 14 -> 14, of which waited for: 10 -> 9; matrix products, arithmetic and copies ran while one was open for 7% -> 1% of each run, Pallas kernels for 21% -> 24%
where the time goes in v5:
time: 111 us; the launch traced here: 110 us
  starting transfers between devices  41.5 us (37%)
  Pallas kernels  37.7 us (34%)
  waiting for transfers between devices  27.8 us (25%)
  local copies, waits for them, and re-layouts  2.08 us (2%)
    ppermute x11, starting transfers between devices, shift(): return lax.ppermute(x, axis, [(i, (i + by) % size) for i in range(size)])  17.8 us
    ppermute x11, waiting for transfers between devices, shift(): return lax.ppermute(x, axis, [(i, (i + by) % size) for i in range(size)])  14.2 us
    all_to_all x1, starting transfers between devices, body(): lax.all_to_all(send.reshape(PEERS, 1, 128), SAMPLE, split_axis=0, concat_...  12 us
    pallas_call x1, Pallas kernels, body(): call(expand_kernel, pltpu.HBM((ROWS, 2 * ROWS), BF), (2 * ROWS * ROWS * R...  8.35 us
    all_to_all x1, starting transfers between devices, body(): lax.all_to_all(msg, SAMPLE, split_axis=0, concat_axis=0, tiled=True)  7.27 us
    all_to_all x1, waiting for transfers between devices, body(): lax.all_to_all(msg, SAMPLE, split_axis=0, concat_axis=0, tiled=True)  6.68 us
    pallas_call x1, Pallas kernels, body(): call(attend_kernel, pltpu.HBM((PEERS, MSG, 128), BF), (2 * ROWS * ROWS *...  5.54 us
    pallas_call x1, Pallas kernels, body(): call(place_kernel, (pltpu.HBM((ROWS, 128), BF), pltpu.HBM((FULL, 128), jn...  5.08 us
  transfers between devices with their start and end apart: 14, of which 9 were waited for; matrix products, arithmetic and copies ran while one was open for 1% of the time, Pallas kernels for 24%

profile of v5, /device:TPU:1, one launch (start us, length us, event | category | flops | bytes accessed | tf_op | source)
XLA Modules:
  0.0 110.0 jit_solution(6645476562455372357)
XLA Ops:
  0.6 2.6 %shard_map.104 = (s32[32,128]{1,0:T(8,128)}, f32[48,128]{1,0:T(8,128)}, s32[16,128]{1,0:T(8,128)}) custom-call(s32[1,1024]{1,0:T(1,128)} %bitcast.16, s32[4,1024]{1,0:T(4,128)} %bitcast.15), custom_call_target="tpu_custom_call" | custom-call | flops 400000000 | bytes 1000000 | tf_op jit(solution)/shard_map/pallas_call | solution.py:484
  3.3 12.0 %all-to-all-start = ((s32[32,1,128]{2,1,0:T(1,128)}), s32[32,1,128]{2,1,0:T(1,128)S(1)}, u32[]{:S(2)}, u32[]{:S(2)}) async-start(s32[32,1,128]{2,1,0:T(1,128)} %bitcast.14), calls=%async_computation | async-start | bytes 32768 | tf_op jit(solution)/shard_map/all_to_all | solution.py:493
  15.3 0.0 copy-start.5
  15.3 2.9 %shard_map.107 = (bf16[640,1024]{1,0:T(8,128)(2,1)}, bf16[640,1024]{1,0:T(8,128)(2,1)}) custom-call(bf16[1024,512]{1,0:T(8,128)(2,1)} %up_ref.3, bf16[512,1024]{1,0:T(8,128)(2,1)} %down_ref.3, bf16[128,1024]{1,0:T(8,128)(2,1)} %own_ref.1), custom_call_target="tpu_custom_call" | custom-call | bytes 5000000 | tf_op jit(solution)/shard_map/pallas_call | solution.py:504
  18.2 0.8 shard_map.105.q_ref
  19.0 0.0 copy-start.4
  19.0 4.8 %all-to-all-done = s32[32,1,128]{2,1,0:T(1,128)S(1)} async-done(((s32[32,1,128]{2,1,0:T(1,128)}), s32[32,1,128]{2,1,0:T(1,128)S(1)}, u32[]{:S(2)}, u32[]{:S(2)}) %all-to-all-start) | async-done | bytes 16416 | tf_op jit(solution)/shard_map/all_to_all | solution.py:493
  23.8 1.7 %shard_map.108 = bf16[1536,128]{1,0:T(8,128)(2,1)} custom-call(s32[32,128]{1,0:T(8,128)S(1)} %bitcast.10, bf16[1024,128]{1,0:T(8,128)(2,1)S(1)} %shard_map.105.q_ref, bf16[640,1024]{1,0:T(8,128)(2,1)} %get-tuple-element.22.after_ref), custom_call_target="tpu_custom_call" | custom-call | flops 402653184 | bytes 1000000 | tf_op jit(solution)/shard_map/pallas_call | solution.py:512
  25.6 4.5 %all-to-all-start.1 = ((bf16[32,48,128]{2,1,0:T(8,128)(2,1)}), bf16[32,48,128]{2,1,0:T(8,128)(2,1)S(1)}, u32[]{:S(2)}, u32[]{:S(2)}) async-start(bf16[32,48,128]{2,1,0:T(8,128)(2,1)} %bitcast.12), calls=%async_computation.1 | async-start | bytes 786432 | tf_op jit(solution)/shard_map/all_to_all | solution.py:538
  30.0 2.6 %collective-permute-start.5 = (bf16[640,1024]{1,0:T(8,128)(2,1)}, bf16[640,1024]{1,0:T(8,128)(2,1)}, u32[]{:S(2)}, u32[]{:S(2)}) collective-permute-start(bf16[640,1024]{1,0:T(8,128)(2,1)} %get-tuple-element.22.after_ref), channel_id=1, source_target_pairs={{0,6},{2,0},{4,2},{6,4},{1,7},{3,1},{5,3},{7,5},{8,14},{10,8},{12,... | collective-permute-start | bytes 3932168 | tf_op jit(solution)/shard_map/ppermute | solution.py:478
  32.6 0.0 collective-permute-start.4
  32.6 8.3 %shard_map.109.kv_ref = bf16[1024,2048]{1,0:T(8,128)(2,1)} custom-call(f32[48,128]{1,0:T(8,128)} %get-tuple-element.23.par_ref, bf16[1024,8,128]{2,1,0:T(8,128)(2,1)} %k_hbm.1, bf16[1024,8,128]{2,1,0:T(8,128)(2,1)} %v_hbm.1), custom_call_target="tpu_custom_call" | custom-call | flops 4294967296 | bytes 12000000 | tf_op jit(solution)/shard_map/pallas_call | solution.py:520
  41.0 0.0 copy-done.4
  41.0 2.1 %all-to-all-done.1.q_ref = bf16[32,48,128]{2,1,0:T(8,128)(2,1)S(1)} async-done(((bf16[32,48,128]{2,1,0:T(8,128)(2,1)}), bf16[32,48,128]{2,1,0:T(8,128)(2,1)S(1)}, u32[]{:S(2)}, u32[]{:S(2)}) %all-to-all-start.1) | async-done | bytes 393248 | tf_op jit(solution)/shard_map/all_to_all | solution.py:538
  43.1 5.5 %shard_map.110 = bf16[32,64,128]{2,1,0:T(8,128)(2,1)} custom-call(s32[16,128]{1,0:T(8,128)} %get-tuple-element.21.full_hbm, bf16[32,48,128]{2,1,0:T(8,128)(2,1)S(1)} %all-to-all-done.1.q_ref, bf16[1024,2048]{1,0:T(8,128)(2,1)} %shard_map.109.kv_ref), custom_call_target="tpu_custom_call" | custom-call | flops 268435456 | bytes 8000000 | tf_op jit(solution)/shard_map/pallas_call | solution.py:552
  48.6 7.3 %all-to-all-start.2 = ((bf16[32,64,128]{2,1,0:T(8,128)(2,1)}), bf16[32,64,128]{2,1,0:T(8,128)(2,1)}, u32[]{:S(2)}, u32[]{:S(2)}) async-start(bf16[32,64,128]{2,1,0:T(8,128)(2,1)} %shard_map.110), calls=%async_computation.2 | async-start | bytes 1048576 | tf_op jit(solution)/shard_map/all_to_all | solution.py:566
  55.9 2.0 %collective-permute-start.3 = (bf16[128,1024]{1,0:T(8,128)(2,1)S(1)}, bf16[128,1024]{1,0:T(8,128)(2,1)S(1)}, u32[]{:S(2)}, u32[]{:S(2)}) collective-permute-start(bf16[128,1024]{1,0:T(8,128)(2,1)S(1)} %copy-done.3), channel_id=1, source_target_pairs={{0,4},{2,6},{4,0},{6,2},{1,5},{3,7},{5,1},{7,3},{8,12},{10,14},{12... | collective-permute-start | bytes 786440 | tf_op jit(solution)/shard_map/ppermute | solution.py:478
  57.9 5.1 %shard_map.106 = (bf16[1024,128]{1,0:T(8,128)(2,1)}, s32[16,128]{1,0:T(8,128)}, bf16[1024,128]{1,0:T(8,128)(2,1)S(1)}, bf16[1024,128]{1,0:T(8,128)(2,1)}) custom-call(s32[32,128]{1,0:T(8,128)S(1)} %bitcast.11, bf16[1024,1024]{1,0:T(8,128)(2,1)S(1)} %copy-done, bf16[3,1024,128]{2,1,0:T(8,128)(2,1)S(1)} %copy-done.6, bf16[1024,128]{1,0:T(8,128)(2,1)} %copy-done.4), custom_call_target="tpu_custom_call" | custom-call | flops 2000000000 | bytes 4000000 | tf_op jit(solution)/shard_map/pallas_call | solution.py:540
  63.0 0.7 copy-done.7
  63.7 6.7 %all-to-all-done.2.msg_hbm = bf16[32,64,128]{2,1,0:T(8,128)(2,1)} async-done(((bf16[32,64,128]{2,1,0:T(8,128)(2,1)}), bf16[32,64,128]{2,1,0:T(8,128)(2,1)}, u32[]{:S(2)}, u32[]{:S(2)}) %all-to-all-start.2) | async-done | bytes 524320 | tf_op jit(solution)/shard_map/all_to_all | solution.py:566
  70.4 3.3 %shard_map.111 = (bf16[512,128]{1,0:T(8,128)(2,1)S(1)}, bf16[512,128]{1,0:T(8,128)(2,1)S(1)}) custom-call(s32[16,128]{1,0:T(8,128)} %get-tuple-element.20.full_hbm, bf16[32,64,128]{2,1,0:T(8,128)(2,1)} %all-to-all-done.2.msg_hbm, bf16[1024,128]{1,0:T(8,128)(2,1)} %get-tuple-element.24.place_hbm, bf16[1024,128]{1,0:T(8,128)(2,1)} %get-tuple-element.25.v_hbm), custom_call_target="tpu_custom_call" | custom-call | flops 402653184 | bytes 5000000 | tf_op jit(solution)/shard_map/pallas_call | solution.py:568
  73.7 0.1 collective-permute-start
  73.8 2.7 %collective-permute-start.1 = (bf16[512,128]{1,0:T(8,128)(2,1)S(1)}, bf16[512,128]{1,0:T(8,128)(2,1)S(1)}, u32[]{:S(2)}, u32[]{:S(2)}) collective-permute-start(bf16[512,128]{1,0:T(8,128)(2,1)S(1)} %get-tuple-element.27), channel_id=1, source_target_pairs={{0,6},{2,0},{4,2},{6,4},{1,7},{3,1},{5,3},{7,5},{8,14},{10,8},{12,... | collective-permute-start | bytes 393224 | tf_op jit(solution)/shard_map/ppermute | solution.py:478
  76.5 0.0 collective-permute-done.3.two_ref
  76.5 0.9 collective-permute-start.2
  77.4 0.0 collective-permute-done.5.right_ref
  77.4 0.0 collective-permute-done.4.left_ref
  77.4 1.4 %collective-permute-done.a1 = bf16[512,128]{1,0:T(8,128)(2,1)S(1)} collective-permute-done((bf16[512,128]{1,0:T(8,128)(2,1)S(1)}, bf16[512,128]{1,0:T(8,128)(2,1)S(1)}, u32[]{:S(2)}, u32[]{:S(2)}) %collective-permute-start) | collective-permute-done | bytes 131104 | tf_op jit(solution)/shard_map/ppermute | solution.py:478
  78.8 0.0 collective-permute-done.1.a2
  78.8 3.0 %collective-permute-done.2.a3 = bf16[512,128]{1,0:T(8,128)(2,1)S(1)} collective-permute-done((bf16[512,128]{1,0:T(8,128)(2,1)S(1)}, bf16[512,128]{1,0:T(8,128)(2,1)S(1)}, u32[]{:S(2)}, u32[]{:S(2)}) %collective-permute-start.2) | collective-permute-done | bytes 131104 | tf_op jit(solution)/shard_map/ppermute | solution.py:478
  81.8 1.8 %shard_map.112.p_ref = bf16[512,1024]{1,0:T(8,128)(2,1)S(1)} custom-call(bf16[512,128]{1,0:T(8,128)(2,1)S(1)} %get-tuple-element.26.a0, bf16[512,128]{1,0:T(8,128)(2,1)S(1)} %collective-permute-done.a1, bf16[512,128]{1,0:T(8,128)(2,1)S(1)} %collective-permute-done.1.a2, bf16[512,128]{1,0:T(8,128)(2,1)S(1)} %collective-permute-done.2.a3, ...), custom_call_target="tpu_custom_call" | custom-call | flops 600000000 | bytes 3000000 | tf_op jit(solution)/shard_map/pallas_call | solution.py:587
  83.6 0.0 copy-start.8
  83.6 0.0 copy-start.9
  83.6 6.2 %collective-permute-start.6 = (bf16[512,1024]{1,0:T(8,128)(2,1)S(1)}, bf16[512,1024]{1,0:T(8,128)(2,1)S(1)}, u32[]{:S(2)}, u32[]{:S(2)}) collective-permute-start(bf16[512,1024]{1,0:T(8,128)(2,1)S(1)} %shard_map.112.p_ref), channel_id=1, source_target_pairs={{0,1},{1,0},{2,3},{3,2},{4,5},{5,4},{6,7},{7,6},{8,9},{9,8},{10,11... | collective-permute-start | bytes 3145736 | tf_op jit(solution)/shard_map/ppermute | solution.py:478
  89.8 2.3 %collective-permute-done.6.r_ref = bf16[512,1024]{1,0:T(8,128)(2,1)S(1)} collective-permute-done((bf16[512,1024]{1,0:T(8,128)(2,1)S(1)}, bf16[512,1024]{1,0:T(8,128)(2,1)S(1)}, u32[]{:S(2)}, u32[]{:S(2)}) %collective-permute-start.6) | collective-permute-done | bytes 1048608 | tf_op jit(solution)/shard_map/ppermute | solution.py:478
  92.1 4.8 %shard_map.113 = (f32[4,512,128]{2,1,0:T(8,128)S(1)}, bf16[4,512,128]{2,1,0:T(8,128)(2,1)S(1)}) custom-call(bf16[1024,1024]{1,0:T(8,128)(2,1)S(1)} %copy-done, bf16[512,1024]{1,0:T(8,128)(2,1)S(1)} %shard_map.112.p_ref, bf16[512,1024]{1,0:T(8,128)(2,1)S(1)} %collective-permute-done.6.r_ref, bf16[1024,512]{1,0:T(8,128)(2,1)S(1)} %copy-done.1, ...), custom_call_target="tpu_custom_call" | custom-call | flops 2000000000 | bytes 10000000 | tf_op jit(solution)/shard_map/pallas_call | solution.py:606
  96.8 0.5 collective-permute-start.7
  97.3 1.5 %collective-permute-done.7.other_ref = bf16[4,512,128]{2,1,0:T(8,128)(2,1)S(1)} collective-permute-done((bf16[4,512,128]{2,1,0:T(8,128)(2,1)S(1)}, bf16[4,512,128]{2,1,0:T(8,128)(2,1)S(1)}, u32[]{:S(2)}, u32[]{:S(2)}) %collective-permute-start.7) | collective-permute-done | bytes 524320 | tf_op jit(solution)/shard_map/ppermute | solution.py:478
  98.8 0.1 shard_map.114
  98.9 1.6 %collective-permute-start.10 = (bf16[512,128]{1,0:T(8,128)(2,1)S(1)}, bf16[512,128]{1,0:T(8,128)(2,1)S(1)}, u32[]{:S(2)}, u32[]{:S(2)}) collective-permute-start(bf16[512,128]{1,0:T(8,128)(2,1)S(1)} %get-tuple-element.34), channel_id=1, source_target_pairs={{0,6},{2,0},{4,2},{6,4},{1,7},{3,1},{5,3},{7,5},{8,14},{10,8},{12,... | collective-permute-start | bytes 393224 | tf_op jit(solution)/shard_map/ppermute | solution.py:478
  100.5 0.0 collective-permute-start.8
  100.5 1.3 %collective-permute-start.9 = (bf16[512,128]{1,0:T(8,128)(2,1)S(1)}, bf16[512,128]{1,0:T(8,128)(2,1)S(1)}, u32[]{:S(2)}, u32[]{:S(2)}) collective-permute-start(bf16[512,128]{1,0:T(8,128)(2,1)S(1)} %get-tuple-element.33), channel_id=1, source_target_pairs={{0,4},{2,6},{4,0},{6,2},{1,5},{3,7},{5,1},{7,3},{8,12},{10,14},{12... | collective-permute-start | bytes 393224 | tf_op jit(solution)/shard_map/ppermute | solution.py:478
  101.8 0.1 pad_maximum_fusion
  101.9 1.3 %copy.13 = bf16[1024,2,128]{2,1,0:T(2,128)(2,1)} copy(bf16[1024,2,128]{2,0,1:T(8,128)(2,1)S(1)} %pad_maximum_fusion) | data formatting | bytes 1048576
  103.2 0.5 collective-permute-done.10.p3
  103.7 5.5 %collective-permute-done.8.p1 = bf16[512,128]{1,0:T(8,128)(2,1)S(1)} collective-permute-done((bf16[512,128]{1,0:T(8,128)(2,1)S(1)}, bf16[512,128]{1,0:T(8,128)(2,1)S(1)}, u32[]{:S(2)}, u32[]{:S(2)}) %collective-permute-start.8) | collective-permute-done | bytes 131104 | tf_op jit(solution)/shard_map/ppermute | solution.py:478
  109.2 0.0 collective-permute-done.9.p2
  109.2 0.8 shard_map.115
  (14 shorter events, 0.0 us)
Async XLA Ops:
  0.6 17.6 %copy-start = (bf16[1024,1024]{1,0:T(8,128)(2,1)S(1)}, bf16[1024,1024]{1,0:T(8,128)(2,1)}, u32[]{:S(2)}) copy-start(bf16[1024,1024]{1,0:T(8,128)(2,1)} %x_ref.5) | copy-start | bytes 6291460
  3.3 20.6 %all-to-all-start = ((s32[32,1,128]{2,1,0:T(1,128)}), s32[32,1,128]{2,1,0:T(1,128)S(1)}, u32[]{:S(2)}, u32[]{:S(2)}) async-start(s32[32,1,128]{2,1,0:T(1,128)} %bitcast.14), calls=%async_computation | async-start | bytes 32768 | tf_op jit(solution)/shard_map/all_to_all | solution.py:493
  15.3 2.9 %copy-start.5 = (bf16[3,1024,128]{2,1,0:T(8,128)(2,1)S(1)}, bf16[3,1024,128]{2,1,0:T(8,128)(2,1)}, u32[]{:S(2)}) copy-start(bf16[3,1024,128]{2,1,0:T(8,128)(2,1)} %w_ref.3) | copy-start | bytes 2359300
  19.0 21.9 %copy-start.4 = (bf16[1024,128]{1,0:T(8,128)(2,1)}, bf16[1024,128]{1,0:T(8,128)(2,1)S(1)}, u32[]{:S(2)}) copy-start(bf16[1024,128]{1,0:T(8,128)(2,1)S(1)} %shard_map.105.q_ref) | copy-start | bytes 786436
  25.6 17.5 %all-to-all-start.1 = ((bf16[32,48,128]{2,1,0:T(8,128)(2,1)}), bf16[32,48,128]{2,1,0:T(8,128)(2,1)S(1)}, u32[]{:S(2)}, u32[]{:S(2)}) async-start(bf16[32,48,128]{2,1,0:T(8,128)(2,1)} %bitcast.12), calls=%async_computation.1 | async-start | bytes 786432 | tf_op jit(solution)/shard_map/all_to_all | solution.py:538
  30.0 47.3 %collective-permute-start.5 = (bf16[640,1024]{1,0:T(8,128)(2,1)}, bf16[640,1024]{1,0:T(8,128)(2,1)}, u32[]{:S(2)}, u32[]{:S(2)}) collective-permute-start(bf16[640,1024]{1,0:T(8,128)(2,1)} %get-tuple-element.22.after_ref), channel_id=1, source_target_pairs={{0,6},{2,0},{4,2},{6,4},{1,7},{3,1},{5,3},{7,5},{8,14},{10,8},{12,... | collective-permute-start | bytes 3932168 | tf_op jit(solution)/shard_map/ppermute | solution.py:478
  32.6 44.8 %collective-permute-start.4 = (bf16[640,1024]{1,0:T(8,128)(2,1)}, bf16[640,1024]{1,0:T(8,128)(2,1)}, u32[]{:S(2)}, u32[]{:S(2)}) collective-permute-start(bf16[640,1024]{1,0:T(8,128)(2,1)} %get-tuple-element.28), channel_id=1, source_target_pairs={{0,2},{2,4},{4,6},{6,0},{1,3},{3,5},{5,7},{7,1},{8,10},{10,12},{12... | collective-permute-start | bytes 3932168 | tf_op jit(solution)/shard_map/ppermute | solution.py:478
  43.0 12.8 %copy-start.3 = (bf16[128,1024]{1,0:T(8,128)(2,1)S(1)}, bf16[128,1024]{1,0:T(8,128)(2,1)}, u32[]{:S(2)}) copy-start(bf16[128,1024]{1,0:T(8,128)(2,1)} %own_ref.1) | copy-start | bytes 786436
  43.0 14.9 %copy-start.6 = (bf16[3,1024,128]{2,1,0:T(8,128)(2,1)S(1)}, bf16[3,1024,128]{2,1,0:T(8,128)(2,1)}, u32[]{:S(2)}) copy-start(bf16[3,1024,128]{2,1,0:T(8,128)(2,1)} %w_ref.3) | copy-start | bytes 2359300
  48.6 21.8 %all-to-all-start.2 = ((bf16[32,64,128]{2,1,0:T(8,128)(2,1)}), bf16[32,64,128]{2,1,0:T(8,128)(2,1)}, u32[]{:S(2)}, u32[]{:S(2)}) async-start(bf16[32,64,128]{2,1,0:T(8,128)(2,1)} %shard_map.110), calls=%async_computation.2 | async-start | bytes 1048576 | tf_op jit(solution)/shard_map/all_to_all | solution.py:566
  55.9 20.6 %collective-permute-start.3 = (bf16[128,1024]{1,0:T(8,128)(2,1)S(1)}, bf16[128,1024]{1,0:T(8,128)(2,1)S(1)}, u32[]{:S(2)}, u32[]{:S(2)}) collective-permute-start(bf16[128,1024]{1,0:T(8,128)(2,1)S(1)} %copy-done.3), channel_id=1, source_target_pairs={{0,4},{2,6},{4,0},{6,2},{1,5},{3,7},{5,1},{7,3},{8,12},{10,14},{12... | collective-permute-start | bytes 786440 | tf_op jit(solution)/shard_map/ppermute | solution.py:478
  63.0 0.7 copy-start.7
  73.7 5.1 %collective-permute-start = (bf16[512,128]{1,0:T(8,128)(2,1)S(1)}, bf16[512,128]{1,0:T(8,128)(2,1)S(1)}, u32[]{:S(2)}, u32[]{:S(2)}) collective-permute-start(bf16[512,128]{1,0:T(8,128)(2,1)S(1)} %get-tuple-element.27), channel_id=1, source_target_pairs={{0,2},{2,4},{4,6},{6,0},{1,3},{3,5},{5,7},{7,1},{8,10},{10,12},{12... | collective-permute-start | bytes 393224 | tf_op jit(solution)/shard_map/ppermute | solution.py:478
  73.8 5.0 %collective-permute-start.1 = (bf16[512,128]{1,0:T(8,128)(2,1)S(1)}, bf16[512,128]{1,0:T(8,128)(2,1)S(1)}, u32[]{:S(2)}, u32[]{:S(2)}) collective-permute-start(bf16[512,128]{1,0:T(8,128)(2,1)S(1)} %get-tuple-element.27), channel_id=1, source_target_pairs={{0,6},{2,0},{4,2},{6,4},{1,7},{3,1},{5,3},{7,5},{8,14},{10,8},{12,... | collective-permute-start | bytes 393224 | tf_op jit(solution)/shard_map/ppermute | solution.py:478
  76.5 15.6 %copy-start.1 = (bf16[1024,512]{1,0:T(8,128)(2,1)S(1)}, bf16[1024,512]{1,0:T(8,128)(2,1)}, u32[]{:S(2)}) copy-start(bf16[1024,512]{1,0:T(8,128)(2,1)} %up_ref.3) | copy-start | bytes 3145732
  76.5 15.6 %copy-start.2 = (bf16[512,1024]{1,0:T(8,128)(2,1)S(1)}, bf16[512,1024]{1,0:T(8,128)(2,1)}, u32[]{:S(2)}) copy-start(bf16[512,1024]{1,0:T(8,128)(2,1)} %down_ref.3) | copy-start | bytes 3145732
  76.5 5.3 %collective-permute-start.2 = (bf16[512,128]{1,0:T(8,128)(2,1)S(1)}, bf16[512,128]{1,0:T(8,128)(2,1)S(1)}, u32[]{:S(2)}, u32[]{:S(2)}) collective-permute-start(bf16[512,128]{1,0:T(8,128)(2,1)S(1)} %get-tuple-element.26.a0), channel_id=1, source_target_pairs={{0,4},{2,6},{4,0},{6,2},{1,5},{3,7},{5,1},{7,3},{8,12},{10,14},{12... | collective-permute-start | bytes 393224 | tf_op jit(solution)/shard_map/ppermute | solution.py:478
  83.6 18.2 %copy-start.8 = (bf16[1024,128]{1,0:T(8,128)(2,1)S(1)}, bf16[1024,128]{1,0:T(8,128)(2,1)}, u32[]{:S(2)}) copy-start(bf16[1024,128]{1,0:T(8,128)(2,1)} %copy-done.7) | copy-start | bytes 786436
  83.6 18.2 %copy-start.9 = (bf16[1024,128]{1,0:T(8,128)(2,1)S(1)}, bf16[1024,128]{1,0:T(8,128)(2,1)}, u32[]{:S(2)}) copy-start(bf16[1024,128]{1,0:T(8,128)(2,1)} %get-tuple-element.25.v_hbm) | copy-start | bytes 786436
  83.6 8.5 %collective-permute-start.6 = (bf16[512,1024]{1,0:T(8,128)(2,1)S(1)}, bf16[512,1024]{1,0:T(8,128)(2,1)S(1)}, u32[]{:S(2)}, u32[]{:S(2)}) collective-permute-start(bf16[512,1024]{1,0:T(8,128)(2,1)S(1)} %shard_map.112.p_ref), channel_id=1, source_target_pairs={{0,1},{1,0},{2,3},{3,2},{4,5},{5,4},{6,7},{7,6},{8,9},{9,8},{10,11... | collective-permute-start | bytes 3145736 | tf_op jit(solution)/shard_map/ppermute | solution.py:478
  96.8 2.0 %collective-permute-start.7 = (bf16[4,512,128]{2,1,0:T(8,128)(2,1)S(1)}, bf16[4,512,128]{2,1,0:T(8,128)(2,1)S(1)}, u32[]{:S(2)}, u32[]{:S(2)}) collective-permute-start(bf16[4,512,128]{2,1,0:T(8,128)(2,1)S(1)} %get-tuple-element.30), channel_id=1, source_target_pairs={{0,1},{1,0},{2,3},{3,2},{4,5},{5,4},{6,7},{7,6},{8,9},{9,8},{10,11... | collective-permute-start | bytes 1572872 | tf_op jit(solution)/shard_map/ppermute | solution.py:478
  98.9 4.8 %collective-permute-start.10 = (bf16[512,128]{1,0:T(8,128)(2,1)S(1)}, bf16[512,128]{1,0:T(8,128)(2,1)S(1)}, u32[]{:S(2)}, u32[]{:S(2)}) collective-permute-start(bf16[512,128]{1,0:T(8,128)(2,1)S(1)} %get-tuple-element.34), channel_id=1, source_target_pairs={{0,6},{2,0},{4,2},{6,4},{1,7},{3,1},{5,3},{7,5},{8,14},{10,8},{12,... | collective-permute-start | bytes 393224 | tf_op jit(solution)/shard_map/ppermute | solution.py:478
  100.5 8.7 %collective-permute-start.8 = (bf16[512,128]{1,0:T(8,128)(2,1)S(1)}, bf16[512,128]{1,0:T(8,128)(2,1)S(1)}, u32[]{:S(2)}, u32[]{:S(2)}) collective-permute-start(bf16[512,128]{1,0:T(8,128)(2,1)S(1)} %get-tuple-element.32), channel_id=1, source_target_pairs={{0,2},{2,4},{4,6},{6,0},{1,3},{3,5},{5,7},{7,1},{8,10},{10,12},{12... | collective-permute-start | bytes 393224 | tf_op jit(solution)/shard_map/ppermute | solution.py:478
  100.5 8.7 %collective-permute-start.9 = (bf16[512,128]{1,0:T(8,128)(2,1)S(1)}, bf16[512,128]{1,0:T(8,128)(2,1)S(1)}, u32[]{:S(2)}, u32[]{:S(2)}) collective-permute-start(bf16[512,128]{1,0:T(8,128)(2,1)S(1)} %get-tuple-element.33), channel_id=1, source_target_pairs={{0,4},{2,6},{4,0},{6,2},{1,5},{3,7},{5,1},{7,3},{8,12},{10,14},{12... | collective-permute-start | bytes 393224 | tf_op jit(solution)/shard_map/ppermute | solution.py:478

commit v6 on v5

--- a/solution.py
+++ b/solution.py
@@ -107,10 +107,11 @@
     high, low = total[3 * PEERS : 4 * PEERS], total[4 * PEERS :]
     rest = 32.0 * jnp.dot(chosen, high.astype(BF), preferred_element_type=F32)
     rest = rest + jnp.dot(chosen, low.astype(BF), preferred_element_type=F32)
-    par_ref[:PEERS, :LOW] = high[:, :LOW] * 32.0 + low[:, :LOW]
-    par_ref[:PEERS, LOW:] = jnp.zeros((PEERS, 128 - LOW), F32)
-    par_ref[PEERS:, :REST] = rest[:, LOW:]
-    par_ref[PEERS:, REST:] = jnp.zeros((FULL, 128 - REST), F32)
+    first = (high[:, :LOW] * 32.0 + low[:, :LOW]).astype(jnp.int32)
+    par_ref[:PEERS, :LOW] = first
+    par_ref[:PEERS, LOW:] = jnp.zeros((PEERS, 128 - LOW), jnp.int32)
+    par_ref[PEERS:, :REST] = rest[:, LOW:].astype(jnp.int32)
+    par_ref[PEERS:, REST:] = jnp.zeros((FULL, 128 - REST), jnp.int32)
 
 
 def pack_kernel(up_ref, down_ref, wo_ref, right_ref, left_ref, stage, sems):
@@ -150,38 +151,38 @@
     return jnp.sum(picked, axis=2, keepdims=True).reshape(count * depth, 1)
 
 
-def expand_kernel(par_ref, k_hbm, v_hbm, out_ref, raw, flat, hot_ref, stage, sems):
+def expand_kernel(par_hbm, k_hbm, v_hbm, out_ref, raw, got, stage, par, sems):
     n = 256
+    lists = pltpu.make_async_copy(par_hbm, par, sems.at[10])
+    lists.start()
     loads = [
         pltpu.make_async_copy(a, raw.at[t], sems.at[t]) for t, a in enumerate((k_hbm, v_hbm))
     ]
     for copy in loads:
         copy.start()
-    low = column(par_ref[:PEERS, :], PEERS, LOW)
-    rest = column(par_ref[PEERS:, :], FULL, REST)
-    parents = iota((n, ROWS), 1).astype(F32)
-    for i in range(4):
-        col = low[i * n : (i + 1) * n] if i < 2 else rest[(i - 2) * n : (i - 1) * n]
-        hot_ref[i] = (col == parents).astype(F32).astype(BF)
+    lists.wait()
     copies = []
-
-    def gather(t, i):
-        got = jnp.dot(hot_ref[i], flat[t], preferred_element_type=F32)
-        stage[t, i] = got.astype(BF)
-        to = out_ref.at[pl.ds(i * n, n), pl.ds(t * ROWS, ROWS)]
-        copies.append(pltpu.make_async_copy(stage.at[t, i], to, sems.at[2 + t * 4 + i]))
-        copies[-1].start()
-
-    loads[0].wait()
-    flat[0] = raw[0].reshape(ROWS, ROWS)
-    gather(0, 0)
-    gather(0, 1)
-    loads[1].wait()
-    flat[1] = raw[1].reshape(ROWS, ROWS)
-    gather(0, 2)
-    gather(0, 3)
-    for i in range(4):
-        gather(1, i)
+    for t in range(2):
+        loads[t].wait()
+
+        def first(o, carry):
+            for c in range(LOW):
+                got[t, o * LOW + c] = raw[t, par[o, c]]
+            return carry
+
+        def rest(k, carry):
+            for c in range(REST):
+                got[t, PEERS * LOW + k * REST + c] = raw[t, par[PEERS + k, c]]
+            return carry
+
+        lax.fori_loop(0, PEERS, first, 0)
+        lax.fori_loop(0, FULL, rest, 0)
+        for i in range(4):
+            stage[t, i] = got[t, i * n : (i + 1) * n].reshape(n, ROWS)
+            to = out_ref.at[pl.ds(i * n, n), pl.ds(t * ROWS, ROWS)]
+            copy = pltpu.make_async_copy(stage.at[t, i], to, sems.at[2 + t * 4 + i])
+            copy.start()
+            copies.append(copy)
     for copy in copies:
         copy.wait()
 
@@ -485,7 +486,7 @@
         plan_kernel,
         (
             pltpu.HBM((PEERS, 128), jnp.int32),
-            pltpu.HBM((PEERS + FULL, 128), F32),
+            pltpu.HBM((PEERS + FULL, 128), jnp.int32),
             pltpu.HBM((FULL, 128), jnp.int32),
         ),
         (4 * 10**8, 10**6),
@@ -521,14 +522,14 @@
         expand_kernel,
         pltpu.HBM((ROWS, 2 * ROWS), BF),
         (2 * ROWS * ROWS * ROWS * 2, 12 * 10**6),
-        in_specs=[vmem, hbm, hbm],
+        in_specs=[hbm, hbm, hbm],
         out_specs=hbm,
         scratch_shapes=[
             pltpu.VMEM((2, ROWS, 8, 128), BF),
-            pltpu.VMEM((2, ROWS, ROWS), BF),
-            pltpu.VMEM((4, 256, ROWS), BF),
+            pltpu.VMEM((2, ROWS, 8, 128), BF),
             pltpu.VMEM((2, 4, 256, ROWS), BF),
-            pltpu.SemaphoreType.DMA((10,)),
+            pltpu.SMEM((PEERS + FULL, 128), jnp.int32),
+            pltpu.SemaphoreType.DMA((11,)),
         ],
     )(*(keep(a, pltpu.HBM) for a in (par, keys, values)))
     left = shift(for_right, "x", 1, 4)

time: 111 us -> 109 us (0.982)
  Pallas kernels: 37.7 us -> 35.7 us
    pallas_call x1, Pallas kernels: 8.35 us -> 6.41 us  [body(): call(expand_kernel, pltpu.HBM((ROWS, 2 * ROWS), BF), (2 * ROWS * ROWS * R...]
    all_to_all x1, waiting for transfers between devices: 2.08 us -> 4 us  [body(): lax.all_to_all(q_send, SAMPLE, split_axis=0, concat_axis=0, tiled=True)]
    ppermute x11, starting transfers between devices: 17.8 us -> 19.4 us  [shift(): return lax.ppermute(x, axis, [(i, (i + by) % size) for i in range(size)])]
    all_to_all x1, starting transfers between devices: 7.27 us -> 5.7 us  [body(): lax.all_to_all(msg, SAMPLE, split_axis=0, concat_axis=0, tiled=True)]
  transfers between devices with their start and end apart: 14 -> 14, of which waited for: 9 -> 9; matrix products, arithmetic and copies ran while one was open for 1% -> 1% of each run, Pallas kernels for 24% -> 22%
where the time goes in v6:
time: 109 us; the launch traced here: 108 us
  starting transfers between devices  41.6 us (38%)
  Pallas kernels  35.7 us (33%)
  waiting for transfers between devices  27.9 us (26%)
  local copies, waits for them, and re-layouts  2.08 us (2%)
    ppermute x11, starting transfers between devices, shift(): return lax.ppermute(x, axis, [(i, (i + by) % size) for i in range(size)])  19.4 us
    ppermute x11, waiting for transfers between devices, shift(): return lax.ppermute(x, axis, [(i, (i + by) % size) for i in range(size)])  13.3 us
    all_to_all x1, starting transfers between devices, body(): lax.all_to_all(send.reshape(PEERS, 1, 128), SAMPLE, split_axis=0, concat_...  12 us
    pallas_call x1, Pallas kernels, body(): call(expand_kernel, pltpu.HBM((ROWS, 2 * ROWS), BF), (2 * ROWS * ROWS * R...  6.41 us
    all_to_all x1, waiting for transfers between devices, body(): lax.all_to_all(msg, SAMPLE, split_axis=0, concat_axis=0, tiled=True)  5.78 us
    all_to_all x1, starting transfers between devices, body(): lax.all_to_all(msg, SAMPLE, split_axis=0, concat_axis=0, tiled=True)  5.7 us
    pallas_call x1, Pallas kernels, body(): call(attend_kernel, pltpu.HBM((PEERS, MSG, 128), BF), (2 * ROWS * ROWS *...  5.51 us
    pallas_call x1, Pallas kernels, body(): call(place_kernel, (pltpu.HBM((ROWS, 128), BF), pltpu.HBM((FULL, 128), jn...  5.08 us
  transfers between devices with their start and end apart: 14, of which 9 were waited for; matrix products, arithmetic and copies ran while one was open for 1% of the time, Pallas kernels for 22%

profile of v6, /device:TPU:1, one launch (start us, length us, event | category | flops | bytes accessed | tf_op | source)
XLA Modules:
  0.0 108.1 jit_solution(2908706438364599905)
XLA Ops:
  0.6 2.6 %shard_map.104 = (s32[32,128]{1,0:T(8,128)}, s32[48,128]{1,0:T(8,128)}, s32[16,128]{1,0:T(8,128)}) custom-call(s32[1,1024]{1,0:T(1,128)} %bitcast.16, s32[4,1024]{1,0:T(4,128)} %bitcast.15), custom_call_target="tpu_custom_call" | custom-call | flops 400000000 | bytes 1000000 | tf_op jit(solution)/shard_map/pallas_call | solution.py:485
  3.3 12.0 %all-to-all-start = ((s32[32,1,128]{2,1,0:T(1,128)}), s32[32,1,128]{2,1,0:T(1,128)S(1)}, u32[]{:S(2)}, u32[]{:S(2)}) async-start(s32[32,1,128]{2,1,0:T(1,128)} %bitcast.14), calls=%async_computation | async-start | bytes 32768 | tf_op jit(solution)/shard_map/all_to_all | solution.py:494
  15.3 0.0 copy-start.5
  15.3 2.9 %shard_map.107 = (bf16[640,1024]{1,0:T(8,128)(2,1)}, bf16[640,1024]{1,0:T(8,128)(2,1)}) custom-call(bf16[1024,512]{1,0:T(8,128)(2,1)} %up_ref.3, bf16[512,1024]{1,0:T(8,128)(2,1)} %down_ref.3, bf16[128,1024]{1,0:T(8,128)(2,1)} %own_ref.1), custom_call_target="tpu_custom_call" | custom-call | bytes 5000000 | tf_op jit(solution)/shard_map/pallas_call | solution.py:505
  18.2 0.0 copy-done
  18.2 0.0 copy-done.5
  18.2 0.8 shard_map.105.q_ref
  19.0 0.0 copy-start.4
  19.0 4.8 %all-to-all-done = s32[32,1,128]{2,1,0:T(1,128)S(1)} async-done(((s32[32,1,128]{2,1,0:T(1,128)}), s32[32,1,128]{2,1,0:T(1,128)S(1)}, u32[]{:S(2)}, u32[]{:S(2)}) %all-to-all-start) | async-done | bytes 16416 | tf_op jit(solution)/shard_map/all_to_all | solution.py:494
  23.8 1.7 %shard_map.108 = bf16[1536,128]{1,0:T(8,128)(2,1)} custom-call(s32[32,128]{1,0:T(8,128)S(1)} %bitcast.10, bf16[1024,128]{1,0:T(8,128)(2,1)S(1)} %shard_map.105.q_ref, bf16[640,1024]{1,0:T(8,128)(2,1)} %get-tuple-element.22.after_ref), custom_call_target="tpu_custom_call" | custom-call | flops 402653184 | bytes 1000000 | tf_op jit(solution)/shard_map/pallas_call | solution.py:513
  25.6 4.4 %all-to-all-start.1 = ((bf16[32,48,128]{2,1,0:T(8,128)(2,1)}), bf16[32,48,128]{2,1,0:T(8,128)(2,1)S(1)}, u32[]{:S(2)}, u32[]{:S(2)}) async-start(bf16[32,48,128]{2,1,0:T(8,128)(2,1)} %bitcast.12), calls=%async_computation.1 | async-start | bytes 786432 | tf_op jit(solution)/shard_map/all_to_all | solution.py:539
  30.0 2.6 %collective-permute-start.5 = (bf16[640,1024]{1,0:T(8,128)(2,1)}, bf16[640,1024]{1,0:T(8,128)(2,1)}, u32[]{:S(2)}, u32[]{:S(2)}) collective-permute-start(bf16[640,1024]{1,0:T(8,128)(2,1)} %get-tuple-element.22.after_ref), channel_id=1, source_target_pairs={{0,6},{2,0},{4,2},{6,4},{1,7},{3,1},{5,3},{7,5},{8,14},{10,8},{12,... | collective-permute-start | bytes 3932168 | tf_op jit(solution)/shard_map/ppermute | solution.py:479
  32.6 0.0 collective-permute-start.4
  32.6 6.4 %shard_map.109.kv_ref = bf16[1024,2048]{1,0:T(8,128)(2,1)} custom-call(s32[48,128]{1,0:T(8,128)} %get-tuple-element.23.par_hbm, bf16[1024,8,128]{2,1,0:T(8,128)(2,1)} %k_hbm.1, bf16[1024,8,128]{2,1,0:T(8,128)(2,1)} %v_hbm.1), custom_call_target="tpu_custom_call" | custom-call | flops 4294967296 | bytes 12000000 | tf_op jit(solution)/shard_map/pallas_call | solution.py:521
  39.0 4.0 %all-to-all-done.1.q_ref = bf16[32,48,128]{2,1,0:T(8,128)(2,1)S(1)} async-done(((bf16[32,48,128]{2,1,0:T(8,128)(2,1)}), bf16[32,48,128]{2,1,0:T(8,128)(2,1)S(1)}, u32[]{:S(2)}, u32[]{:S(2)}) %all-to-all-start.1) | async-done | bytes 393248 | tf_op jit(solution)/shard_map/all_to_all | solution.py:539
  43.0 5.5 %shard_map.110 = bf16[32,64,128]{2,1,0:T(8,128)(2,1)} custom-call(s32[16,128]{1,0:T(8,128)} %get-tuple-element.21.full_hbm, bf16[32,48,128]{2,1,0:T(8,128)(2,1)S(1)} %all-to-all-done.1.q_ref, bf16[1024,2048]{1,0:T(8,128)(2,1)} %shard_map.109.kv_ref), custom_call_target="tpu_custom_call" | custom-call | flops 268435456 | bytes 8000000 | tf_op jit(solution)/shard_map/pallas_call | solution.py:553
  48.6 5.7 %all-to-all-start.2 = ((bf16[32,64,128]{2,1,0:T(8,128)(2,1)}), bf16[32,64,128]{2,1,0:T(8,128)(2,1)}, u32[]{:S(2)}, u32[]{:S(2)}) async-start(bf16[32,64,128]{2,1,0:T(8,128)(2,1)} %shard_map.110), calls=%async_computation.2 | async-start | bytes 1048576 | tf_op jit(solution)/shard_map/all_to_all | solution.py:567
  54.3 3.0 %collective-permute-start.3 = (bf16[128,1024]{1,0:T(8,128)(2,1)S(1)}, bf16[128,1024]{1,0:T(8,128)(2,1)S(1)}, u32[]{:S(2)}, u32[]{:S(2)}) collective-permute-start(bf16[128,1024]{1,0:T(8,128)(2,1)S(1)} %copy-done.3), channel_id=1, source_target_pairs={{0,4},{2,6},{4,0},{6,2},{1,5},{3,7},{5,1},{7,3},{8,12},{10,14},{12... | collective-permute-start | bytes 786440 | tf_op jit(solution)/shard_map/ppermute | solution.py:479
  57.3 5.1 %shard_map.106 = (bf16[1024,128]{1,0:T(8,128)(2,1)}, s32[16,128]{1,0:T(8,128)}, bf16[1024,128]{1,0:T(8,128)(2,1)S(1)}, bf16[1024,128]{1,0:T(8,128)(2,1)}) custom-call(s32[32,128]{1,0:T(8,128)S(1)} %bitcast.11, bf16[1024,1024]{1,0:T(8,128)(2,1)S(1)} %copy-done, bf16[3,1024,128]{2,1,0:T(8,128)(2,1)S(1)} %copy-done.6, bf16[1024,128]{1,0:T(8,128)(2,1)} %copy-done.4), custom_call_target="tpu_custom_call" | custom-call | flops 2000000000 | bytes 4000000 | tf_op jit(solution)/shard_map/pallas_call | solution.py:541
  62.3 0.7 copy-done.7
  63.0 5.8 %all-to-all-done.2.msg_hbm = bf16[32,64,128]{2,1,0:T(8,128)(2,1)} async-done(((bf16[32,64,128]{2,1,0:T(8,128)(2,1)}), bf16[32,64,128]{2,1,0:T(8,128)(2,1)}, u32[]{:S(2)}, u32[]{:S(2)}) %all-to-all-start.2) | async-done | bytes 524320 | tf_op jit(solution)/shard_map/all_to_all | solution.py:567
  68.8 3.3 %shard_map.111 = (bf16[512,128]{1,0:T(8,128)(2,1)S(1)}, bf16[512,128]{1,0:T(8,128)(2,1)S(1)}) custom-call(s32[16,128]{1,0:T(8,128)} %get-tuple-element.20.full_hbm, bf16[32,64,128]{2,1,0:T(8,128)(2,1)} %all-to-all-done.2.msg_hbm, bf16[1024,128]{1,0:T(8,128)(2,1)} %get-tuple-element.24.place_hbm, bf16[1024,128]{1,0:T(8,128)(2,1)} %get-tuple-element.25.v_hbm), custom_call_target="tpu_custom_call" | custom-call | flops 402653184 | bytes 5000000 | tf_op jit(solution)/shard_map/pallas_call | solution.py:569
  72.1 1.3 %collective-permute-start = (bf16[512,128]{1,0:T(8,128)(2,1)S(1)}, bf16[512,128]{1,0:T(8,128)(2,1)S(1)}, u32[]{:S(2)}, u32[]{:S(2)}) collective-permute-start(bf16[512,128]{1,0:T(8,128)(2,1)S(1)} %get-tuple-element.27), channel_id=1, source_target_pairs={{0,2},{2,4},{4,6},{6,0},{1,3},{3,5},{5,7},{7,1},{8,10},{10,12},{12... | collective-permute-start | bytes 393224 | tf_op jit(solution)/shard_map/ppermute | solution.py:479
  73.4 1.5 %collective-permute-start.1 = (bf16[512,128]{1,0:T(8,128)(2,1)S(1)}, bf16[512,128]{1,0:T(8,128)(2,1)S(1)}, u32[]{:S(2)}, u32[]{:S(2)}) collective-permute-start(bf16[512,128]{1,0:T(8,128)(2,1)S(1)} %get-tuple-element.27), channel_id=1, source_target_pairs={{0,6},{2,0},{4,2},{6,4},{1,7},{3,1},{5,3},{7,5},{8,14},{10,8},{12,... | collective-permute-start | bytes 393224 | tf_op jit(solution)/shard_map/ppermute | solution.py:479
  74.9 0.0 collective-permute-done.3.two_ref
  74.9 1.5 %collective-permute-start.2 = (bf16[512,128]{1,0:T(8,128)(2,1)S(1)}, bf16[512,128]{1,0:T(8,128)(2,1)S(1)}, u32[]{:S(2)}, u32[]{:S(2)}) collective-permute-start(bf16[512,128]{1,0:T(8,128)(2,1)S(1)} %get-tuple-element.26.a0), channel_id=1, source_target_pairs={{0,4},{2,6},{4,0},{6,2},{1,5},{3,7},{5,1},{7,3},{8,12},{10,14},{12... | collective-permute-start | bytes 393224 | tf_op jit(solution)/shard_map/ppermute | solution.py:479
  76.4 0.0 collective-permute-done.5.right_ref
  76.4 0.0 collective-permute-done.4.left_ref
  76.4 0.8 collective-permute-done.a1
  77.2 0.0 collective-permute-done.1.a2
  77.3 3.0 %collective-permute-done.2.a3 = bf16[512,128]{1,0:T(8,128)(2,1)S(1)} collective-permute-done((bf16[512,128]{1,0:T(8,128)(2,1)S(1)}, bf16[512,128]{1,0:T(8,128)(2,1)S(1)}, u32[]{:S(2)}, u32[]{:S(2)}) %collective-permute-start.2) | collective-permute-done | bytes 131104 | tf_op jit(solution)/shard_map/ppermute | solution.py:479
  80.2 1.8 %shard_map.112.p_ref = bf16[512,1024]{1,0:T(8,128)(2,1)S(1)} custom-call(bf16[512,128]{1,0:T(8,128)(2,1)S(1)} %get-tuple-element.26.a0, bf16[512,128]{1,0:T(8,128)(2,1)S(1)} %collective-permute-done.a1, bf16[512,128]{1,0:T(8,128)(2,1)S(1)} %collective-permute-done.1.a2, bf16[512,128]{1,0:T(8,128)(2,1)S(1)} %collective-permute-done.2.a3, ...), custom_call_target="tpu_custom_call" | custom-call | flops 600000000 | bytes 3000000 | tf_op jit(solution)/shard_map/pallas_call | solution.py:588
  82.0 0.0 copy-start.8
  82.0 6.0 %collective-permute-start.6 = (bf16[512,1024]{1,0:T(8,128)(2,1)S(1)}, bf16[512,1024]{1,0:T(8,128)(2,1)S(1)}, u32[]{:S(2)}, u32[]{:S(2)}) collective-permute-start(bf16[512,1024]{1,0:T(8,128)(2,1)S(1)} %shard_map.112.p_ref), channel_id=1, source_target_pairs={{0,1},{1,0},{2,3},{3,2},{4,5},{5,4},{6,7},{7,6},{8,9},{9,8},{10,11... | collective-permute-start | bytes 3145736 | tf_op jit(solution)/shard_map/ppermute | solution.py:479
  88.1 2.3 %collective-permute-done.6.r_ref = bf16[512,1024]{1,0:T(8,128)(2,1)S(1)} collective-permute-done((bf16[512,1024]{1,0:T(8,128)(2,1)S(1)}, bf16[512,1024]{1,0:T(8,128)(2,1)S(1)}, u32[]{:S(2)}, u32[]{:S(2)}) %collective-permute-start.6) | collective-permute-done | bytes 1048608 | tf_op jit(solution)/shard_map/ppermute | solution.py:479
  90.4 4.8 %shard_map.113 = (f32[4,512,128]{2,1,0:T(8,128)S(1)}, bf16[4,512,128]{2,1,0:T(8,128)(2,1)S(1)}) custom-call(bf16[1024,1024]{1,0:T(8,128)(2,1)S(1)} %copy-done, bf16[512,1024]{1,0:T(8,128)(2,1)S(1)} %shard_map.112.p_ref, bf16[512,1024]{1,0:T(8,128)(2,1)S(1)} %collective-permute-done.6.r_ref, bf16[1024,512]{1,0:T(8,128)(2,1)S(1)} %copy-done.1, ...), custom_call_target="tpu_custom_call" | custom-call | flops 2000000000 | bytes 10000000 | tf_op jit(solution)/shard_map/pallas_call | solution.py:607
  95.1 0.5 collective-permute-start.7
  95.6 1.5 %collective-permute-done.7.other_ref = bf16[4,512,128]{2,1,0:T(8,128)(2,1)S(1)} collective-permute-done((bf16[4,512,128]{2,1,0:T(8,128)(2,1)S(1)}, bf16[4,512,128]{2,1,0:T(8,128)(2,1)S(1)}, u32[]{:S(2)}, u32[]{:S(2)}) %collective-permute-start.7) | collective-permute-done | bytes 524320 | tf_op jit(solution)/shard_map/ppermute | solution.py:479
  97.1 0.1 shard_map.114
  97.2 1.5 %collective-permute-start.10 = (bf16[512,128]{1,0:T(8,128)(2,1)S(1)}, bf16[512,128]{1,0:T(8,128)(2,1)S(1)}, u32[]{:S(2)}, u32[]{:S(2)}) collective-permute-start(bf16[512,128]{1,0:T(8,128)(2,1)S(1)} %get-tuple-element.34), channel_id=1, source_target_pairs={{0,6},{2,0},{4,2},{6,4},{1,7},{3,1},{5,3},{7,5},{8,14},{10,8},{12,... | collective-permute-start | bytes 393224 | tf_op jit(solution)/shard_map/ppermute | solution.py:479
  98.7 0.1 collective-permute-start.8
  98.8 1.5 %collective-permute-start.9 = (bf16[512,128]{1,0:T(8,128)(2,1)S(1)}, bf16[512,128]{1,0:T(8,128)(2,1)S(1)}, u32[]{:S(2)}, u32[]{:S(2)}) collective-permute-start(bf16[512,128]{1,0:T(8,128)(2,1)S(1)} %get-tuple-element.33), channel_id=1, source_target_pairs={{0,4},{2,6},{4,0},{6,2},{1,5},{3,7},{5,1},{7,3},{8,12},{10,14},{12... | collective-permute-start | bytes 393224 | tf_op jit(solution)/shard_map/ppermute | solution.py:479
  100.3 0.1 pad_maximum_fusion
  100.3 1.3 %copy.13 = bf16[1024,2,128]{2,1,0:T(2,128)(2,1)} copy(bf16[1024,2,128]{2,0,1:T(8,128)(2,1)S(1)} %pad_maximum_fusion) | data formatting | bytes 1048576
  101.7 0.3 collective-permute-done.10.p3
  102.0 5.4 %collective-permute-done.8.p1 = bf16[512,128]{1,0:T(8,128)(2,1)S(1)} collective-permute-done((bf16[512,128]{1,0:T(8,128)(2,1)S(1)}, bf16[512,128]{1,0:T(8,128)(2,1)S(1)}, u32[]{:S(2)}, u32[]{:S(2)}) %collective-permute-start.8) | collective-permute-done | bytes 131104 | tf_op jit(solution)/shard_map/ppermute | solution.py:479
  107.4 0.0 collective-permute-done.9.p2
  107.4 0.8 shard_map.115
  (14 shorter events, 0.0 us)
Async XLA Ops:
  0.6 17.6 %copy-start = (bf16[1024,1024]{1,0:T(8,128)(2,1)S(1)}, bf16[1024,1024]{1,0:T(8,128)(2,1)}, u32[]{:S(2)}) copy-start(bf16[1024,1024]{1,0:T(8,128)(2,1)} %x_ref.5) | copy-start | bytes 6291460
  3.3 20.6 %all-to-all-start = ((s32[32,1,128]{2,1,0:T(1,128)}), s32[32,1,128]{2,1,0:T(1,128)S(1)}, u32[]{:S(2)}, u32[]{:S(2)}) async-start(s32[32,1,128]{2,1,0:T(1,128)} %bitcast.14), calls=%async_computation | async-start | bytes 32768 | tf_op jit(solution)/shard_map/all_to_all | solution.py:494
  15.3 2.9 %copy-start.5 = (bf16[3,1024,128]{2,1,0:T(8,128)(2,1)S(1)}, bf16[3,1024,128]{2,1,0:T(8,128)(2,1)}, u32[]{:S(2)}) copy-start(bf16[3,1024,128]{2,1,0:T(8,128)(2,1)} %w_ref.3) | copy-start | bytes 2359300
  19.0 20.0 %copy-start.4 = (bf16[1024,128]{1,0:T(8,128)(2,1)}, bf16[1024,128]{1,0:T(8,128)(2,1)S(1)}, u32[]{:S(2)}) copy-start(bf16[1024,128]{1,0:T(8,128)(2,1)S(1)} %shard_map.105.q_ref) | copy-start | bytes 786436
  25.6 17.4 %all-to-all-start.1 = ((bf16[32,48,128]{2,1,0:T(8,128)(2,1)}), bf16[32,48,128]{2,1,0:T(8,128)(2,1)S(1)}, u32[]{:S(2)}, u32[]{:S(2)}) async-start(bf16[32,48,128]{2,1,0:T(8,128)(2,1)} %bitcast.12), calls=%async_computation.1 | async-start | bytes 786432 | tf_op jit(solution)/shard_map/all_to_all | solution.py:539
  30.0 46.4 %collective-permute-start.5 = (bf16[640,1024]{1,0:T(8,128)(2,1)}, bf16[640,1024]{1,0:T(8,128)(2,1)}, u32[]{:S(2)}, u32[]{:S(2)}) collective-permute-start(bf16[640,1024]{1,0:T(8,128)(2,1)} %get-tuple-element.22.after_ref), channel_id=1, source_target_pairs={{0,6},{2,0},{4,2},{6,4},{1,7},{3,1},{5,3},{7,5},{8,14},{10,8},{12,... | collective-permute-start | bytes 3932168 | tf_op jit(solution)/shard_map/ppermute | solution.py:479
  32.6 43.8 %collective-permute-start.4 = (bf16[640,1024]{1,0:T(8,128)(2,1)}, bf16[640,1024]{1,0:T(8,128)(2,1)}, u32[]{:S(2)}, u32[]{:S(2)}) collective-permute-start(bf16[640,1024]{1,0:T(8,128)(2,1)} %get-tuple-element.28), channel_id=1, source_target_pairs={{0,2},{2,4},{4,6},{6,0},{1,3},{3,5},{5,7},{7,1},{8,10},{10,12},{12... | collective-permute-start | bytes 3932168 | tf_op jit(solution)/shard_map/ppermute | solution.py:479
  43.0 11.2 %copy-start.3 = (bf16[128,1024]{1,0:T(8,128)(2,1)S(1)}, bf16[128,1024]{1,0:T(8,128)(2,1)}, u32[]{:S(2)}) copy-start(bf16[128,1024]{1,0:T(8,128)(2,1)} %own_ref.1) | copy-start | bytes 786436
  43.0 14.2 %copy-start.6 = (bf16[3,1024,128]{2,1,0:T(8,128)(2,1)S(1)}, bf16[3,1024,128]{2,1,0:T(8,128)(2,1)}, u32[]{:S(2)}) copy-start(bf16[3,1024,128]{2,1,0:T(8,128)(2,1)} %w_ref.3) | copy-start | bytes 2359300
  48.6 20.3 %all-to-all-start.2 = ((bf16[32,64,128]{2,1,0:T(8,128)(2,1)}), bf16[32,64,128]{2,1,0:T(8,128)(2,1)}, u32[]{:S(2)}, u32[]{:S(2)}) async-start(bf16[32,64,128]{2,1,0:T(8,128)(2,1)} %shard_map.110), calls=%async_computation.2 | async-start | bytes 1048576 | tf_op jit(solution)/shard_map/all_to_all | solution.py:567
  54.3 20.6 %collective-permute-start.3 = (bf16[128,1024]{1,0:T(8,128)(2,1)S(1)}, bf16[128,1024]{1,0:T(8,128)(2,1)S(1)}, u32[]{:S(2)}, u32[]{:S(2)}) collective-permute-start(bf16[128,1024]{1,0:T(8,128)(2,1)S(1)} %copy-done.3), channel_id=1, source_target_pairs={{0,4},{2,6},{4,0},{6,2},{1,5},{3,7},{5,1},{7,3},{8,12},{10,14},{12... | collective-permute-start | bytes 786440 | tf_op jit(solution)/shard_map/ppermute | solution.py:479
  62.3 0.7 copy-start.7
  72.1 5.1 %collective-permute-start = (bf16[512,128]{1,0:T(8,128)(2,1)S(1)}, bf16[512,128]{1,0:T(8,128)(2,1)S(1)}, u32[]{:S(2)}, u32[]{:S(2)}) collective-permute-start(bf16[512,128]{1,0:T(8,128)(2,1)S(1)} %get-tuple-element.27), channel_id=1, source_target_pairs={{0,2},{2,4},{4,6},{6,0},{1,3},{3,5},{5,7},{7,1},{8,10},{10,12},{12... | collective-permute-start | bytes 393224 | tf_op jit(solution)/shard_map/ppermute | solution.py:479
  73.4 3.8 %collective-permute-start.1 = (bf16[512,128]{1,0:T(8,128)(2,1)S(1)}, bf16[512,128]{1,0:T(8,128)(2,1)S(1)}, u32[]{:S(2)}, u32[]{:S(2)}) collective-permute-start(bf16[512,128]{1,0:T(8,128)(2,1)S(1)} %get-tuple-element.27), channel_id=1, source_target_pairs={{0,6},{2,0},{4,2},{6,4},{1,7},{3,1},{5,3},{7,5},{8,14},{10,8},{12,... | collective-permute-start | bytes 393224 | tf_op jit(solution)/shard_map/ppermute | solution.py:479
  74.9 15.5 %copy-start.1 = (bf16[1024,512]{1,0:T(8,128)(2,1)S(1)}, bf16[1024,512]{1,0:T(8,128)(2,1)}, u32[]{:S(2)}) copy-start(bf16[1024,512]{1,0:T(8,128)(2,1)} %up_ref.3) | copy-start | bytes 3145732
  74.9 15.5 %copy-start.2 = (bf16[512,1024]{1,0:T(8,128)(2,1)S(1)}, bf16[512,1024]{1,0:T(8,128)(2,1)}, u32[]{:S(2)}) copy-start(bf16[512,1024]{1,0:T(8,128)(2,1)} %down_ref.3) | copy-start | bytes 3145732
  74.9 5.3 %collective-permute-start.2 = (bf16[512,128]{1,0:T(8,128)(2,1)S(1)}, bf16[512,128]{1,0:T(8,128)(2,1)S(1)}, u32[]{:S(2)}, u32[]{:S(2)}) collective-permute-start(bf16[512,128]{1,0:T(8,128)(2,1)S(1)} %get-tuple-element.26.a0), channel_id=1, source_target_pairs={{0,4},{2,6},{4,0},{6,2},{1,5},{3,7},{5,1},{7,3},{8,12},{10,14},{12... | collective-permute-start | bytes 393224 | tf_op jit(solution)/shard_map/ppermute | solution.py:479
  82.0 18.3 %copy-start.8 = (bf16[1024,128]{1,0:T(8,128)(2,1)S(1)}, bf16[1024,128]{1,0:T(8,128)(2,1)}, u32[]{:S(2)}) copy-start(bf16[1024,128]{1,0:T(8,128)(2,1)} %copy-done.7) | copy-start | bytes 786436
  82.0 18.3 %copy-start.9 = (bf16[1024,128]{1,0:T(8,128)(2,1)S(1)}, bf16[1024,128]{1,0:T(8,128)(2,1)}, u32[]{:S(2)}) copy-start(bf16[1024,128]{1,0:T(8,128)(2,1)} %get-tuple-element.25.v_hbm) | copy-start | bytes 786436
  82.0 8.3 %collective-permute-start.6 = (bf16[512,1024]{1,0:T(8,128)(2,1)S(1)}, bf16[512,1024]{1,0:T(8,128)(2,1)S(1)}, u32[]{:S(2)}, u32[]{:S(2)}) collective-permute-start(bf16[512,1024]{1,0:T(8,128)(2,1)S(1)} %shard_map.112.p_ref), channel_id=1, source_target_pairs={{0,1},{1,0},{2,3},{3,2},{4,5},{5,4},{6,7},{7,6},{8,9},{9,8},{10,11... | collective-permute-start | bytes 3145736 | tf_op jit(solution)/shard_map/ppermute | solution.py:479
  95.1 2.0 %collective-permute-start.7 = (bf16[4,512,128]{2,1,0:T(8,128)(2,1)S(1)}, bf16[4,512,128]{2,1,0:T(8,128)(2,1)S(1)}, u32[]{:S(2)}, u32[]{:S(2)}) collective-permute-start(bf16[4,512,128]{2,1,0:T(8,128)(2,1)S(1)} %get-tuple-element.30), channel_id=1, source_target_pairs={{0,1},{1,0},{2,3},{3,2},{4,5},{5,4},{6,7},{7,6},{8,9},{9,8},{10,11... | collective-permute-start | bytes 1572872 | tf_op jit(solution)/shard_map/ppermute | solution.py:479
  97.2 4.8 %collective-permute-start.10 = (bf16[512,128]{1,0:T(8,128)(2,1)S(1)}, bf16[512,128]{1,0:T(8,128)(2,1)S(1)}, u32[]{:S(2)}, u32[]{:S(2)}) collective-permute-start(bf16[512,128]{1,0:T(8,128)(2,1)S(1)} %get-tuple-element.34), channel_id=1, source_target_pairs={{0,6},{2,0},{4,2},{6,4},{1,7},{3,1},{5,3},{7,5},{8,14},{10,8},{12,... | collective-permute-start | bytes 393224 | tf_op jit(solution)/shard_map/ppermute | solution.py:479
  98.7 8.7 %collective-permute-start.8 = (bf16[512,128]{1,0:T(8,128)(2,1)S(1)}, bf16[512,128]{1,0:T(8,128)(2,1)S(1)}, u32[]{:S(2)}, u32[]{:S(2)}) collective-permute-start(bf16[512,128]{1,0:T(8,128)(2,1)S(1)} %get-tuple-element.32), channel_id=1, source_target_pairs={{0,2},{2,4},{4,6},{6,0},{1,3},{3,5},{5,7},{7,1},{8,10},{10,12},{12... | collective-permute-start | bytes 393224 | tf_op jit(solution)/shard_map/ppermute | solution.py:479
  98.8 8.6 %collective-permute-start.9 = (bf16[512,128]{1,0:T(8,128)(2,1)S(1)}, bf16[512,128]{1,0:T(8,128)(2,1)S(1)}, u32[]{:S(2)}, u32[]{:S(2)}) collective-permute-start(bf16[512,128]{1,0:T(8,128)(2,1)S(1)} %get-tuple-element.33), channel_id=1, source_target_pairs={{0,4},{2,6},{4,0},{6,2},{1,5},{3,7},{5,1},{7,3},{8,12},{10,14},{12... | collective-permute-start | bytes 393224 | tf_op jit(solution)/shard_map/ppermute | solution.py:479

commit v7 on v6

--- a/solution.py
+++ b/solution.py
@@ -12,7 +12,8 @@
 CAP = 48
 ROWS = 1024
 ITEMS = PEERS * CAP
-MSG = 64
+MSG = 56
+TAIL = MSG - CAP
 LOW = 16
 FULL = PEERS // 2
 REST = CAP - LOW
@@ -317,11 +318,11 @@
             parts.append(piece)
             lse = lse - piece
     weight = jnp.concatenate(weights, axis=0).astype(BF)
-    tail = jnp.concatenate(parts + [jnp.zeros((10, ROWS), F32)], axis=0)
+    tail = jnp.concatenate(parts + [jnp.zeros((TAIL - 6, ROWS), F32)], axis=0)
     stage[:, LOW:CAP, :] = jnp.zeros((PEERS, REST, 128), BF)
     for k in range(PEERS):
         piece = tail[:, k * LOW : (k + 1) * LOW]
-        piece = jnp.concatenate([piece, jnp.zeros((16, 128 - LOW), F32)], axis=1)
+        piece = jnp.concatenate([piece, jnp.zeros((TAIL, 128 - LOW), F32)], axis=1)
         stage[k, CAP:, :] = piece.astype(BF)
     for i in range(4):
         wide = lax.dot_general(
@@ -341,9 +342,9 @@
                 stage[peer, LOW:CAP, :] = ctx[k * REST : (k + 1) * REST].reshape(1, REST, 128)
     for k, peer in enumerate(peers):
         at = split + k * REST
-        before, after = jnp.zeros((16, LOW), F32), jnp.zeros((16, 128 - CAP), F32)
+        before, after = jnp.zeros((TAIL, LOW), F32), jnp.zeros((TAIL, 128 - CAP), F32)
         piece = jnp.concatenate([before, tail[:, at : at + REST], after], axis=1).astype(BF)
-        stage[peer, CAP:, :] = stage[peer, CAP:, :] + piece.reshape(1, 16, 128)
+        stage[peer, CAP:, :] = stage[peer, CAP:, :] + piece.reshape(1, TAIL, 128)
     end = pltpu.make_async_copy(stage, out_ref, sems.at[8])
     end.start()
     end.wait()
@@ -368,9 +369,9 @@
     use = use + jnp.where(scores & ((piece - 4) // 3 == head), 1.0, 0.0)
     use = use.astype(BF)
     lanes = iota((rows, 128), 1).astype(F32)
-    entry = iota((rows, PEERS * 16), 1)
-    of_source = (entry // 16).astype(F32)
-    of_head = entry % 16 // 3
+    entry = iota((rows, PEERS * TAIL), 1)
+    of_source = (entry // TAIL).astype(F32)
+    of_head = entry % TAIL // 3
     for copy in fetch:
         copy.wait()
     low = PEERS * LOW
@@ -378,7 +379,7 @@
     for k in range(FULL):
         got = msg_ref[pl.ds(full_ref[k, 0], 1), LOW:CAP, :].reshape(REST, 128)
         ctx_ref[low + k * REST : low + (k + 1) * REST, :] = got
-    parts = msg_ref[:, CAP:, :].reshape(PEERS * 16, 128)
+    parts = msg_ref[:, CAP:, :].reshape(PEERS * TAIL, 128)
     parity = lax.axis_index("x") % 2
     for i, out in enumerate(outs):
         block = (parity if i < 2 else 1 - parity) + 2 * (i % 2)
@@ -388,7 +389,7 @@
         hot = [(lanes + float(t * 128) == pos).astype(F32).astype(BF) for t in range(8)]
         hot = jnp.concatenate(hot, axis=1)
         ctx = jnp.dot(hot, ctx_ref[...], preferred_element_type=F32)
-        hit = of_source == jnp.concatenate([known[:, 256:384]] * 4, axis=1)
+        hit = of_source == jnp.concatenate([known[:, 256:384]] * (PEERS * TAIL // 128), axis=1)
         here = lanes == known[:, 128:256]
         cols = []
         for h in range(2):

time: 109 us -> 106 us (0.972)
  waiting for transfers between devices: 27.9 us -> 25.5 us
    ppermute x11, waiting for transfers between devices: 13.3 us -> 12 us  [shift(): return lax.ppermute(x, axis, [(i, (i + by) % size) for i in range(size)])]
  transfers between devices with their start and end apart: 14 -> 14, of which waited for: 9 -> 10; matrix products, arithmetic and copies ran while one was open for 1% -> 1% of each run, Pallas kernels for 22% -> 22%
where the time goes in v7:
time: 106 us; the launch traced here: 105 us
  starting transfers between devices  41.5 us (39%)
  Pallas kernels  35.4 us (33%)
  waiting for transfers between devices  25.5 us (24%)
  local copies, waits for them, and re-layouts  2.08 us (2%)
    ppermute x11, starting transfers between devices, shift(): return lax.ppermute(x, axis, [(i, (i + by) % size) for i in range(size)])  19.3 us
    all_to_all x1, starting transfers between devices, body(): lax.all_to_all(send.reshape(PEERS, 1, 128), SAMPLE, split_axis=0, concat_...  12 us
    ppermute x11, waiting for transfers between devices, shift(): return lax.ppermute(x, axis, [(i, (i + by) % size) for i in range(size)])  12 us
    pallas_call x1, Pallas kernels, body(): call(expand_kernel, pltpu.HBM((ROWS, 2 * ROWS), BF), (2 * ROWS * ROWS * R...  6.41 us
    all_to_all x1, starting transfers between devices, body(): lax.all_to_all(msg, SAMPLE, split_axis=0, concat_axis=0, tiled=True)  5.68 us
    pallas_call x1, Pallas kernels, body(): call(attend_kernel, pltpu.HBM((PEERS, MSG, 128), BF), (2 * ROWS * ROWS *...  5.46 us
    pallas_call x1, Pallas kernels, body(): call(place_kernel, (pltpu.HBM((ROWS, 128), BF), pltpu.HBM((FULL, 128), jn...  5.08 us
    all_to_all x1, waiting for transfers between devices, body(): lax.all_to_all(send.reshape(PEERS, 1, 128), SAMPLE, split_axis=0, concat_...  4.79 us
  transfers between devices with their start and end apart: 14, of which 10 were waited for; matrix products, arithmetic and copies ran while one was open for 1% of the time, Pallas kernels for 22%

profile of v7, /device:TPU:1, one launch (start us, length us, event | category | flops | bytes accessed | tf_op | source)
XLA Modules:
  0.0 105.3 jit_solution(17298581897220146321)
XLA Ops:
  0.6 2.6 %shard_map.104 = (s32[32,128]{1,0:T(8,128)}, s32[48,128]{1,0:T(8,128)}, s32[16,128]{1,0:T(8,128)}) custom-call(s32[1,1024]{1,0:T(1,128)} %bitcast.16, s32[4,1024]{1,0:T(4,128)} %bitcast.15), custom_call_target="tpu_custom_call" | custom-call | flops 400000000 | bytes 1000000 | tf_op jit(solution)/shard_map/pallas_call | solution.py:486
  3.3 12.0 %all-to-all-start = ((s32[32,1,128]{2,1,0:T(1,128)}), s32[32,1,128]{2,1,0:T(1,128)S(1)}, u32[]{:S(2)}, u32[]{:S(2)}) async-start(s32[32,1,128]{2,1,0:T(1,128)} %bitcast.14), calls=%async_computation | async-start | bytes 32768 | tf_op jit(solution)/shard_map/all_to_all | solution.py:495
  15.3 0.0 copy-start.5
  15.3 2.9 %shard_map.107 = (bf16[640,1024]{1,0:T(8,128)(2,1)}, bf16[640,1024]{1,0:T(8,128)(2,1)}) custom-call(bf16[1024,512]{1,0:T(8,128)(2,1)} %up_ref.3, bf16[512,1024]{1,0:T(8,128)(2,1)} %down_ref.3, bf16[128,1024]{1,0:T(8,128)(2,1)} %own_ref.1), custom_call_target="tpu_custom_call" | custom-call | bytes 5000000 | tf_op jit(solution)/shard_map/pallas_call | solution.py:506
  18.2 0.8 shard_map.105.q_ref
  19.0 0.0 copy-start.4
  19.0 4.8 %all-to-all-done = s32[32,1,128]{2,1,0:T(1,128)S(1)} async-done(((s32[32,1,128]{2,1,0:T(1,128)}), s32[32,1,128]{2,1,0:T(1,128)S(1)}, u32[]{:S(2)}, u32[]{:S(2)}) %all-to-all-start) | async-done | bytes 16416 | tf_op jit(solution)/shard_map/all_to_all | solution.py:495
  23.8 1.7 %shard_map.108 = bf16[1536,128]{1,0:T(8,128)(2,1)} custom-call(s32[32,128]{1,0:T(8,128)S(1)} %bitcast.10, bf16[1024,128]{1,0:T(8,128)(2,1)S(1)} %shard_map.105.q_ref, bf16[640,1024]{1,0:T(8,128)(2,1)} %get-tuple-element.22.after_ref), custom_call_target="tpu_custom_call" | custom-call | flops 402653184 | bytes 1000000 | tf_op jit(solution)/shard_map/pallas_call | solution.py:514
  25.6 4.4 %all-to-all-start.1 = ((bf16[32,48,128]{2,1,0:T(8,128)(2,1)}), bf16[32,48,128]{2,1,0:T(8,128)(2,1)S(1)}, u32[]{:S(2)}, u32[]{:S(2)}) async-start(bf16[32,48,128]{2,1,0:T(8,128)(2,1)} %bitcast.12), calls=%async_computation.1 | async-start | bytes 786432 | tf_op jit(solution)/shard_map/all_to_all | solution.py:540
  30.0 2.6 %collective-permute-start.5 = (bf16[640,1024]{1,0:T(8,128)(2,1)}, bf16[640,1024]{1,0:T(8,128)(2,1)}, u32[]{:S(2)}, u32[]{:S(2)}) collective-permute-start(bf16[640,1024]{1,0:T(8,128)(2,1)} %get-tuple-element.22.after_ref), channel_id=1, source_target_pairs={{0,6},{2,0},{4,2},{6,4},{1,7},{3,1},{5,3},{7,5},{8,14},{10,8},{12,... | collective-permute-start | bytes 3932168 | tf_op jit(solution)/shard_map/ppermute | solution.py:480
  32.6 0.0 collective-permute-start.4
  32.6 6.4 %shard_map.109.kv_ref = bf16[1024,2048]{1,0:T(8,128)(2,1)} custom-call(s32[48,128]{1,0:T(8,128)} %get-tuple-element.23.par_hbm, bf16[1024,8,128]{2,1,0:T(8,128)(2,1)} %k_hbm.1, bf16[1024,8,128]{2,1,0:T(8,128)(2,1)} %v_hbm.1), custom_call_target="tpu_custom_call" | custom-call | flops 4294967296 | bytes 12000000 | tf_op jit(solution)/shard_map/pallas_call | solution.py:522
  39.0 4.0 %all-to-all-done.1.q_ref = bf16[32,48,128]{2,1,0:T(8,128)(2,1)S(1)} async-done(((bf16[32,48,128]{2,1,0:T(8,128)(2,1)}), bf16[32,48,128]{2,1,0:T(8,128)(2,1)S(1)}, u32[]{:S(2)}, u32[]{:S(2)}) %all-to-all-start.1) | async-done | bytes 393248 | tf_op jit(solution)/shard_map/all_to_all | solution.py:540
  43.0 5.5 %shard_map.110 = bf16[32,56,128]{2,1,0:T(8,128)(2,1)} custom-call(s32[16,128]{1,0:T(8,128)} %get-tuple-element.21.full_hbm, bf16[32,48,128]{2,1,0:T(8,128)(2,1)S(1)} %all-to-all-done.1.q_ref, bf16[1024,2048]{1,0:T(8,128)(2,1)} %shard_map.109.kv_ref), custom_call_target="tpu_custom_call" | custom-call | flops 268435456 | bytes 8000000 | tf_op jit(solution)/shard_map/pallas_call | solution.py:554
  48.5 5.7 %all-to-all-start.2 = ((bf16[32,56,128]{2,1,0:T(8,128)(2,1)}), bf16[32,56,128]{2,1,0:T(8,128)(2,1)}, u32[]{:S(2)}, u32[]{:S(2)}) async-start(bf16[32,56,128]{2,1,0:T(8,128)(2,1)} %shard_map.110), calls=%async_computation.2 | async-start | bytes 917504 | tf_op jit(solution)/shard_map/all_to_all | solution.py:568
  54.2 0.0 copy-done.3
  54.2 3.0 %collective-permute-start.3 = (bf16[128,1024]{1,0:T(8,128)(2,1)S(1)}, bf16[128,1024]{1,0:T(8,128)(2,1)S(1)}, u32[]{:S(2)}, u32[]{:S(2)}) collective-permute-start(bf16[128,1024]{1,0:T(8,128)(2,1)S(1)} %copy-done.3), channel_id=1, source_target_pairs={{0,4},{2,6},{4,0},{6,2},{1,5},{3,7},{5,1},{7,3},{8,12},{10,14},{12... | collective-permute-start | bytes 786440 | tf_op jit(solution)/shard_map/ppermute | solution.py:480
  57.2 5.1 %shard_map.106 = (bf16[1024,128]{1,0:T(8,128)(2,1)}, s32[16,128]{1,0:T(8,128)}, bf16[1024,128]{1,0:T(8,128)(2,1)S(1)}, bf16[1024,128]{1,0:T(8,128)(2,1)}) custom-call(s32[32,128]{1,0:T(8,128)S(1)} %bitcast.11, bf16[1024,1024]{1,0:T(8,128)(2,1)S(1)} %copy-done, bf16[3,1024,128]{2,1,0:T(8,128)(2,1)S(1)} %copy-done.6, bf16[1024,128]{1,0:T(8,128)(2,1)} %copy-done.4), custom_call_target="tpu_custom_call" | custom-call | flops 2000000000 | bytes 4000000 | tf_op jit(solution)/shard_map/pallas_call | solution.py:542
  62.3 0.7 copy-done.7
  63.0 4.7 %all-to-all-done.2.msg_hbm = bf16[32,56,128]{2,1,0:T(8,128)(2,1)} async-done(((bf16[32,56,128]{2,1,0:T(8,128)(2,1)}), bf16[32,56,128]{2,1,0:T(8,128)(2,1)}, u32[]{:S(2)}, u32[]{:S(2)}) %all-to-all-start.2) | async-done | bytes 458784 | tf_op jit(solution)/shard_map/all_to_all | solution.py:568
  67.7 3.0 %shard_map.111 = (bf16[512,128]{1,0:T(8,128)(2,1)S(1)}, bf16[512,128]{1,0:T(8,128)(2,1)S(1)}) custom-call(s32[16,128]{1,0:T(8,128)} %get-tuple-element.20.full_hbm, bf16[32,56,128]{2,1,0:T(8,128)(2,1)} %all-to-all-done.2.msg_hbm, bf16[1024,128]{1,0:T(8,128)(2,1)} %get-tuple-element.24.place_hbm, bf16[1024,128]{1,0:T(8,128)(2,1)} %get-tuple-element.25.v_hbm), custom_call_target="tpu_custom_call" | custom-call | flops 402653184 | bytes 5000000 | tf_op jit(solution)/shard_map/pallas_call | solution.py:570
  70.7 1.2 %collective-permute-start = (bf16[512,128]{1,0:T(8,128)(2,1)S(1)}, bf16[512,128]{1,0:T(8,128)(2,1)S(1)}, u32[]{:S(2)}, u32[]{:S(2)}) collective-permute-start(bf16[512,128]{1,0:T(8,128)(2,1)S(1)} %get-tuple-element.27), channel_id=1, source_target_pairs={{0,2},{2,4},{4,6},{6,0},{1,3},{3,5},{5,7},{7,1},{8,10},{10,12},{12... | collective-permute-start | bytes 393224 | tf_op jit(solution)/shard_map/ppermute | solution.py:480
  72.0 1.5 %collective-permute-start.1 = (bf16[512,128]{1,0:T(8,128)(2,1)S(1)}, bf16[512,128]{1,0:T(8,128)(2,1)S(1)}, u32[]{:S(2)}, u32[]{:S(2)}) collective-permute-start(bf16[512,128]{1,0:T(8,128)(2,1)S(1)} %get-tuple-element.27), channel_id=1, source_target_pairs={{0,6},{2,0},{4,2},{6,4},{1,7},{3,1},{5,3},{7,5},{8,14},{10,8},{12,... | collective-permute-start | bytes 393224 | tf_op jit(solution)/shard_map/ppermute | solution.py:480
  73.5 0.0 collective-permute-done.3.two_ref
  73.5 1.5 %collective-permute-start.2 = (bf16[512,128]{1,0:T(8,128)(2,1)S(1)}, bf16[512,128]{1,0:T(8,128)(2,1)S(1)}, u32[]{:S(2)}, u32[]{:S(2)}) collective-permute-start(bf16[512,128]{1,0:T(8,128)(2,1)S(1)} %get-tuple-element.26.a0), channel_id=1, source_target_pairs={{0,4},{2,6},{4,0},{6,2},{1,5},{3,7},{5,1},{7,3},{8,12},{10,14},{12... | collective-permute-start | bytes 393224 | tf_op jit(solution)/shard_map/ppermute | solution.py:480
  75.0 0.0 collective-permute-done.5.right_ref
  75.0 0.0 collective-permute-done.4.left_ref
  75.0 0.9 collective-permute-done.a1
  75.8 0.0 collective-permute-done.1.a2
  75.8 3.0 %collective-permute-done.2.a3 = bf16[512,128]{1,0:T(8,128)(2,1)S(1)} collective-permute-done((bf16[512,128]{1,0:T(8,128)(2,1)S(1)}, bf16[512,128]{1,0:T(8,128)(2,1)S(1)}, u32[]{:S(2)}, u32[]{:S(2)}) %collective-permute-start.2) | collective-permute-done | bytes 131104 | tf_op jit(solution)/shard_map/ppermute | solution.py:480
  78.8 1.8 %shard_map.112.p_ref = bf16[512,1024]{1,0:T(8,128)(2,1)S(1)} custom-call(bf16[512,128]{1,0:T(8,128)(2,1)S(1)} %get-tuple-element.26.a0, bf16[512,128]{1,0:T(8,128)(2,1)S(1)} %collective-permute-done.a1, bf16[512,128]{1,0:T(8,128)(2,1)S(1)} %collective-permute-done.1.a2, bf16[512,128]{1,0:T(8,128)(2,1)S(1)} %collective-permute-done.2.a3, ...), custom_call_target="tpu_custom_call" | custom-call | flops 600000000 | bytes 3000000 | tf_op jit(solution)/shard_map/pallas_call | solution.py:589
  80.6 0.0 copy-start.8
  80.6 0.0 copy-start.9
  80.6 6.0 %collective-permute-start.6 = (bf16[512,1024]{1,0:T(8,128)(2,1)S(1)}, bf16[512,1024]{1,0:T(8,128)(2,1)S(1)}, u32[]{:S(2)}, u32[]{:S(2)}) collective-permute-start(bf16[512,1024]{1,0:T(8,128)(2,1)S(1)} %shard_map.112.p_ref), channel_id=1, source_target_pairs={{0,1},{1,0},{2,3},{3,2},{4,5},{5,4},{6,7},{7,6},{8,9},{9,8},{10,11... | collective-permute-start | bytes 3145736 | tf_op jit(solution)/shard_map/ppermute | solution.py:480
  86.6 2.3 %collective-permute-done.6.r_ref = bf16[512,1024]{1,0:T(8,128)(2,1)S(1)} collective-permute-done((bf16[512,1024]{1,0:T(8,128)(2,1)S(1)}, bf16[512,1024]{1,0:T(8,128)(2,1)S(1)}, u32[]{:S(2)}, u32[]{:S(2)}) %collective-permute-start.6) | collective-permute-done | bytes 1048608 | tf_op jit(solution)/shard_map/ppermute | solution.py:480
  88.9 4.8 %shard_map.113 = (f32[4,512,128]{2,1,0:T(8,128)S(1)}, bf16[4,512,128]{2,1,0:T(8,128)(2,1)S(1)}) custom-call(bf16[1024,1024]{1,0:T(8,128)(2,1)S(1)} %copy-done, bf16[512,1024]{1,0:T(8,128)(2,1)S(1)} %shard_map.112.p_ref, bf16[512,1024]{1,0:T(8,128)(2,1)S(1)} %collective-permute-done.6.r_ref, bf16[1024,512]{1,0:T(8,128)(2,1)S(1)} %copy-done.1, ...), custom_call_target="tpu_custom_call" | custom-call | flops 2000000000 | bytes 10000000 | tf_op jit(solution)/shard_map/pallas_call | solution.py:608
  93.7 0.5 collective-permute-start.7
  94.1 1.5 %collective-permute-done.7.other_ref = bf16[4,512,128]{2,1,0:T(8,128)(2,1)S(1)} collective-permute-done((bf16[4,512,128]{2,1,0:T(8,128)(2,1)S(1)}, bf16[4,512,128]{2,1,0:T(8,128)(2,1)S(1)}, u32[]{:S(2)}, u32[]{:S(2)}) %collective-permute-start.7) | collective-permute-done | bytes 524320 | tf_op jit(solution)/shard_map/ppermute | solution.py:480
  95.7 0.1 shard_map.114
  95.8 1.3 %collective-permute-start.10 = (bf16[512,128]{1,0:T(8,128)(2,1)S(1)}, bf16[512,128]{1,0:T(8,128)(2,1)S(1)}, u32[]{:S(2)}, u32[]{:S(2)}) collective-permute-start(bf16[512,128]{1,0:T(8,128)(2,1)S(1)} %get-tuple-element.34), channel_id=1, source_target_pairs={{0,6},{2,0},{4,2},{6,4},{1,7},{3,1},{5,3},{7,5},{8,14},{10,8},{12,... | collective-permute-start | bytes 393224 | tf_op jit(solution)/shard_map/ppermute | solution.py:480
  97.1 0.2 collective-permute-start.8
  97.3 1.5 %collective-permute-start.9 = (bf16[512,128]{1,0:T(8,128)(2,1)S(1)}, bf16[512,128]{1,0:T(8,128)(2,1)S(1)}, u32[]{:S(2)}, u32[]{:S(2)}) collective-permute-start(bf16[512,128]{1,0:T(8,128)(2,1)S(1)} %get-tuple-element.33), channel_id=1, source_target_pairs={{0,4},{2,6},{4,0},{6,2},{1,5},{3,7},{5,1},{7,3},{8,12},{10,14},{12... | collective-permute-start | bytes 393224 | tf_op jit(solution)/shard_map/ppermute | solution.py:480
  98.8 0.1 pad_maximum_fusion
  98.9 1.3 %copy.13 = bf16[1024,2,128]{2,1,0:T(2,128)(2,1)} copy(bf16[1024,2,128]{2,0,1:T(8,128)(2,1)S(1)} %pad_maximum_fusion) | data formatting | bytes 1048576
  100.2 0.3 collective-permute-done.10.p3
  100.5 3.5 %collective-permute-done.8.p1 = bf16[512,128]{1,0:T(8,128)(2,1)S(1)} collective-permute-done((bf16[512,128]{1,0:T(8,128)(2,1)S(1)}, bf16[512,128]{1,0:T(8,128)(2,1)S(1)}, u32[]{:S(2)}, u32[]{:S(2)}) %collective-permute-start.8) | collective-permute-done | bytes 131104 | tf_op jit(solution)/shard_map/ppermute | solution.py:480
  104.0 0.5 collective-permute-done.9.p2
  104.5 0.8 shard_map.115
  (14 shorter events, 0.0 us)
Async XLA Ops:
  0.6 17.6 %copy-start = (bf16[1024,1024]{1,0:T(8,128)(2,1)S(1)}, bf16[1024,1024]{1,0:T(8,128)(2,1)}, u32[]{:S(2)}) copy-start(bf16[1024,1024]{1,0:T(8,128)(2,1)} %x_ref.5) | copy-start | bytes 6291460
  3.3 20.6 %all-to-all-start = ((s32[32,1,128]{2,1,0:T(1,128)}), s32[32,1,128]{2,1,0:T(1,128)S(1)}, u32[]{:S(2)}, u32[]{:S(2)}) async-start(s32[32,1,128]{2,1,0:T(1,128)} %bitcast.14), calls=%async_computation | async-start | bytes 32768 | tf_op jit(solution)/shard_map/all_to_all | solution.py:495
  15.3 2.9 %copy-start.5 = (bf16[3,1024,128]{2,1,0:T(8,128)(2,1)S(1)}, bf16[3,1024,128]{2,1,0:T(8,128)(2,1)}, u32[]{:S(2)}) copy-start(bf16[3,1024,128]{2,1,0:T(8,128)(2,1)} %w_ref.3) | copy-start | bytes 2359300
  19.0 20.0 %copy-start.4 = (bf16[1024,128]{1,0:T(8,128)(2,1)}, bf16[1024,128]{1,0:T(8,128)(2,1)S(1)}, u32[]{:S(2)}) copy-start(bf16[1024,128]{1,0:T(8,128)(2,1)S(1)} %shard_map.105.q_ref) | copy-start | bytes 786436
  25.6 17.4 %all-to-all-start.1 = ((bf16[32,48,128]{2,1,0:T(8,128)(2,1)}), bf16[32,48,128]{2,1,0:T(8,128)(2,1)S(1)}, u32[]{:S(2)}, u32[]{:S(2)}) async-start(bf16[32,48,128]{2,1,0:T(8,128)(2,1)} %bitcast.12), calls=%async_computation.1 | async-start | bytes 786432 | tf_op jit(solution)/shard_map/all_to_all | solution.py:540
  30.0 44.9 %collective-permute-start.5 = (bf16[640,1024]{1,0:T(8,128)(2,1)}, bf16[640,1024]{1,0:T(8,128)(2,1)}, u32[]{:S(2)}, u32[]{:S(2)}) collective-permute-start(bf16[640,1024]{1,0:T(8,128)(2,1)} %get-tuple-element.22.after_ref), channel_id=1, source_target_pairs={{0,6},{2,0},{4,2},{6,4},{1,7},{3,1},{5,3},{7,5},{8,14},{10,8},{12,... | collective-permute-start | bytes 3932168 | tf_op jit(solution)/shard_map/ppermute | solution.py:480
  32.6 42.4 %collective-permute-start.4 = (bf16[640,1024]{1,0:T(8,128)(2,1)}, bf16[640,1024]{1,0:T(8,128)(2,1)}, u32[]{:S(2)}, u32[]{:S(2)}) collective-permute-start(bf16[640,1024]{1,0:T(8,128)(2,1)} %get-tuple-element.28), channel_id=1, source_target_pairs={{0,2},{2,4},{4,6},{6,0},{1,3},{3,5},{5,7},{7,1},{8,10},{10,12},{12... | collective-permute-start | bytes 3932168 | tf_op jit(solution)/shard_map/ppermute | solution.py:480
  43.0 11.2 %copy-start.3 = (bf16[128,1024]{1,0:T(8,128)(2,1)S(1)}, bf16[128,1024]{1,0:T(8,128)(2,1)}, u32[]{:S(2)}) copy-start(bf16[128,1024]{1,0:T(8,128)(2,1)} %own_ref.1) | copy-start | bytes 786436
  43.0 14.2 %copy-start.6 = (bf16[3,1024,128]{2,1,0:T(8,128)(2,1)S(1)}, bf16[3,1024,128]{2,1,0:T(8,128)(2,1)}, u32[]{:S(2)}) copy-start(bf16[3,1024,128]{2,1,0:T(8,128)(2,1)} %w_ref.3) | copy-start | bytes 2359300
  48.5 19.2 %all-to-all-start.2 = ((bf16[32,56,128]{2,1,0:T(8,128)(2,1)}), bf16[32,56,128]{2,1,0:T(8,128)(2,1)}, u32[]{:S(2)}, u32[]{:S(2)}) async-start(bf16[32,56,128]{2,1,0:T(8,128)(2,1)} %shard_map.110), calls=%async_computation.2 | async-start | bytes 917504 | tf_op jit(solution)/shard_map/all_to_all | solution.py:568
  54.2 19.3 %collective-permute-start.3 = (bf16[128,1024]{1,0:T(8,128)(2,1)S(1)}, bf16[128,1024]{1,0:T(8,128)(2,1)S(1)}, u32[]{:S(2)}, u32[]{:S(2)}) collective-permute-start(bf16[128,1024]{1,0:T(8,128)(2,1)S(1)} %copy-done.3), channel_id=1, source_target_pairs={{0,4},{2,6},{4,0},{6,2},{1,5},{3,7},{5,1},{7,3},{8,12},{10,14},{12... | collective-permute-start | bytes 786440 | tf_op jit(solution)/shard_map/ppermute | solution.py:480
  62.3 0.7 copy-start.7
  70.7 5.1 %collective-permute-start = (bf16[512,128]{1,0:T(8,128)(2,1)S(1)}, bf16[512,128]{1,0:T(8,128)(2,1)S(1)}, u32[]{:S(2)}, u32[]{:S(2)}) collective-permute-start(bf16[512,128]{1,0:T(8,128)(2,1)S(1)} %get-tuple-element.27), channel_id=1, source_target_pairs={{0,2},{2,4},{4,6},{6,0},{1,3},{3,5},{5,7},{7,1},{8,10},{10,12},{12... | collective-permute-start | bytes 393224 | tf_op jit(solution)/shard_map/ppermute | solution.py:480
  72.0 3.9 %collective-permute-start.1 = (bf16[512,128]{1,0:T(8,128)(2,1)S(1)}, bf16[512,128]{1,0:T(8,128)(2,1)S(1)}, u32[]{:S(2)}, u32[]{:S(2)}) collective-permute-start(bf16[512,128]{1,0:T(8,128)(2,1)S(1)} %get-tuple-element.27), channel_id=1, source_target_pairs={{0,6},{2,0},{4,2},{6,4},{1,7},{3,1},{5,3},{7,5},{8,14},{10,8},{12,... | collective-permute-start | bytes 393224 | tf_op jit(solution)/shard_map/ppermute | solution.py:480
  73.5 15.4 %copy-start.1 = (bf16[1024,512]{1,0:T(8,128)(2,1)S(1)}, bf16[1024,512]{1,0:T(8,128)(2,1)}, u32[]{:S(2)}) copy-start(bf16[1024,512]{1,0:T(8,128)(2,1)} %up_ref.3) | copy-start | bytes 3145732
  73.5 15.4 %copy-start.2 = (bf16[512,1024]{1,0:T(8,128)(2,1)S(1)}, bf16[512,1024]{1,0:T(8,128)(2,1)}, u32[]{:S(2)}) copy-start(bf16[512,1024]{1,0:T(8,128)(2,1)} %down_ref.3) | copy-start | bytes 3145732
  73.5 5.3 %collective-permute-start.2 = (bf16[512,128]{1,0:T(8,128)(2,1)S(1)}, bf16[512,128]{1,0:T(8,128)(2,1)S(1)}, u32[]{:S(2)}, u32[]{:S(2)}) collective-permute-start(bf16[512,128]{1,0:T(8,128)(2,1)S(1)} %get-tuple-element.26.a0), channel_id=1, source_target_pairs={{0,4},{2,6},{4,0},{6,2},{1,5},{3,7},{5,1},{7,3},{8,12},{10,14},{12... | collective-permute-start | bytes 393224 | tf_op jit(solution)/shard_map/ppermute | solution.py:480
  80.6 18.3 %copy-start.8 = (bf16[1024,128]{1,0:T(8,128)(2,1)S(1)}, bf16[1024,128]{1,0:T(8,128)(2,1)}, u32[]{:S(2)}) copy-start(bf16[1024,128]{1,0:T(8,128)(2,1)} %copy-done.7) | copy-start | bytes 786436
  80.6 18.2 %copy-start.9 = (bf16[1024,128]{1,0:T(8,128)(2,1)S(1)}, bf16[1024,128]{1,0:T(8,128)(2,1)}, u32[]{:S(2)}) copy-start(bf16[1024,128]{1,0:T(8,128)(2,1)} %get-tuple-element.25.v_hbm) | copy-start | bytes 786436
  80.6 8.3 %collective-permute-start.6 = (bf16[512,1024]{1,0:T(8,128)(2,1)S(1)}, bf16[512,1024]{1,0:T(8,128)(2,1)S(1)}, u32[]{:S(2)}, u32[]{:S(2)}) collective-permute-start(bf16[512,1024]{1,0:T(8,128)(2,1)S(1)} %shard_map.112.p_ref), channel_id=1, source_target_pairs={{0,1},{1,0},{2,3},{3,2},{4,5},{5,4},{6,7},{7,6},{8,9},{9,8},{10,11... | collective-permute-start | bytes 3145736 | tf_op jit(solution)/shard_map/ppermute | solution.py:480
  93.7 2.0 %collective-permute-start.7 = (bf16[4,512,128]{2,1,0:T(8,128)(2,1)S(1)}, bf16[4,512,128]{2,1,0:T(8,128)(2,1)S(1)}, u32[]{:S(2)}, u32[]{:S(2)}) collective-permute-start(bf16[4,512,128]{2,1,0:T(8,128)(2,1)S(1)} %get-tuple-element.30), channel_id=1, source_target_pairs={{0,1},{1,0},{2,3},{3,2},{4,5},{5,4},{6,7},{7,6},{8,9},{9,8},{10,11... | collective-permute-start | bytes 1572872 | tf_op jit(solution)/shard_map/ppermute | solution.py:480
  95.8 4.8 %collective-permute-start.10 = (bf16[512,128]{1,0:T(8,128)(2,1)S(1)}, bf16[512,128]{1,0:T(8,128)(2,1)S(1)}, u32[]{:S(2)}, u32[]{:S(2)}) collective-permute-start(bf16[512,128]{1,0:T(8,128)(2,1)S(1)} %get-tuple-element.34), channel_id=1, source_target_pairs={{0,6},{2,0},{4,2},{6,4},{1,7},{3,1},{5,3},{7,5},{8,14},{10,8},{12,... | collective-permute-start | bytes 393224 | tf_op jit(solution)/shard_map/ppermute | solution.py:480
  97.1 6.9 %collective-permute-start.8 = (bf16[512,128]{1,0:T(8,128)(2,1)S(1)}, bf16[512,128]{1,0:T(8,128)(2,1)S(1)}, u32[]{:S(2)}, u32[]{:S(2)}) collective-permute-start(bf16[512,128]{1,0:T(8,128)(2,1)S(1)} %get-tuple-element.32), channel_id=1, source_target_pairs={{0,2},{2,4},{4,6},{6,0},{1,3},{3,5},{5,7},{7,1},{8,10},{10,12},{12... | collective-permute-start | bytes 393224 | tf_op jit(solution)/shard_map/ppermute | solution.py:480
  97.3 7.2 %collective-permute-start.9 = (bf16[512,128]{1,0:T(8,128)(2,1)S(1)}, bf16[512,128]{1,0:T(8,128)(2,1)S(1)}, u32[]{:S(2)}, u32[]{:S(2)}) collective-permute-start(bf16[512,128]{1,0:T(8,128)(2,1)S(1)} %get-tuple-element.33), channel_id=1, source_target_pairs={{0,4},{2,6},{4,0},{6,2},{1,5},{3,7},{5,1},{7,3},{8,12},{10,14},{12... | collective-permute-start | bytes 393224 | tf_op jit(solution)/shard_map/ppermute | solution.py:480

commit v8 on v7

--- a/solution.py
+++ b/solution.py
@@ -180,7 +180,7 @@
         lax.fori_loop(0, FULL, rest, 0)
         for i in range(4):
             stage[t, i] = got[t, i * n : (i + 1) * n].reshape(n, ROWS)
-            to = out_ref.at[pl.ds(i * n, n), pl.ds(t * ROWS, ROWS)]
+            to = out_ref.at[t, pl.ds(i * n, n)]
             copy = pltpu.make_async_copy(stage.at[t, i], to, sems.at[2 + t * 4 + i])
             copy.start()
             copies.append(copy)
@@ -269,8 +269,7 @@
     copies = []
     for part in range(2):
         for i in range(4):
-            src = kv_ref.at[pl.ds(i * n, n), pl.ds(part * ROWS, ROWS)]
-            dst = kv.at[i, :, pl.ds(part * ROWS, ROWS)]
+            src, dst = kv_ref.at[part, pl.ds(i * n, n)], kv.at[part, i]
             copies.append(pltpu.make_async_copy(src, dst, sems.at[part * 4 + i]))
     for copy in copies:
         copy.start()
@@ -295,7 +294,7 @@
         for p in range(0, 8, 2):
             highs, lows = [], []
             for t in (p, p + 1):
-                prod = q * kv[i, :, t * 128 : (t + 1) * 128].astype(F32)
+                prod = q * kv[0, i, :, t * 128 : (t + 1) * 128].astype(F32)
                 high = prod.astype(BF)
                 highs.append(high)
                 lows.append((prod - high.astype(F32)).astype(BF))
@@ -331,7 +330,7 @@
         copies[4 + i].wait()
         ctx = jnp.zeros((n, 128), F32)
         for p in range(8):
-            value = kv[i, :, ROWS + p * 128 : ROWS + (p + 1) * 128].astype(F32)
+            value = kv[1, i, :, p * 128 : (p + 1) * 128].astype(F32)
             ctx = ctx + wide[:, p * 128 : (p + 1) * 128] * value
         ctx = ctx.astype(BF)
         if i < 2:
@@ -354,8 +353,7 @@
     full_hbm, msg_hbm, place_hbm, v_hbm, mine_ref, theirs_ref, msg_ref, place_ref, v_ref, ctx_ref,
     full_ref, sems
 ):
-    rows = 256
-    outs = [r.at[pl.ds(n * rows, rows)] for r in (mine_ref, theirs_ref) for n in range(2)]
+    rows = 512
     pairs = [(full_hbm, full_ref), (msg_hbm, msg_ref), (place_hbm, place_ref), (v_hbm, v_ref)]
     fetch = [pltpu.make_async_copy(a, b, sems.at[i]) for i, (a, b) in enumerate(pairs)]
     for copy in fetch:
@@ -381,10 +379,12 @@
         ctx_ref[low + k * REST : low + (k + 1) * REST, :] = got
     parts = msg_ref[:, CAP:, :].reshape(PEERS * TAIL, 128)
     parity = lax.axis_index("x") % 2
-    for i, out in enumerate(outs):
-        block = (parity if i < 2 else 1 - parity) + 2 * (i % 2)
-        at = pl.ds(pl.multiple_of(block * rows, rows), rows)
-        known = jnp.dot(place_ref[at, :], use, preferred_element_type=F32)
+    for i, out in enumerate((mine_ref, theirs_ref)):
+        first = parity if i == 0 else 1 - parity
+        at = [pl.ds(pl.multiple_of((first + 2 * n) * 256, 256), 256) for n in range(2)]
+        known = jnp.concatenate([place_ref[a, :] for a in at], axis=0)
+        value = jnp.concatenate([v_ref[a, :] for a in at], axis=0).astype(F32)
+        known = jnp.dot(known, use, preferred_element_type=F32)
         pos, own = known[:, :128], known[:, 384:]
         hot = [(lanes + float(t * 128) == pos).astype(F32).astype(BF) for t in range(8)]
         hot = jnp.concatenate(hot, axis=1)
@@ -400,7 +400,7 @@
         top = jnp.maximum(lse, own)
         a = jnp.exp(lse - top)
         b = jnp.exp(own - top)
-        out[...] = ((a * ctx + b * v_ref[at, :].astype(F32)) / (a + b)).astype(BF)
+        out[...] = ((a * ctx + b * value) / (a + b)).astype(BF)
 
 
 def project_kernel(a0, a1, a2, a3, own_ref, two_ref, left_ref, right_ref, out_ref, near, sems):
@@ -521,7 +521,7 @@
     )(recv, query, keep(for_left, pltpu.HBM))
     kv = call(
         expand_kernel,
-        pltpu.HBM((ROWS, 2 * ROWS), BF),
+        pltpu.HBM((2, ROWS, ROWS), BF),
         (2 * ROWS * ROWS * ROWS * 2, 12 * 10**6),
         in_specs=[hbm, hbm, hbm],
         out_specs=hbm,
@@ -558,7 +558,7 @@
         in_specs=[hbm, vmem, hbm],
         out_specs=hbm,
         scratch_shapes=[
-            pltpu.VMEM((4, 256, 2 * ROWS), BF),
+            pltpu.VMEM((2, 4, 256, ROWS), BF),
             pltpu.VMEM((ROWS, 128), BF),
             pltpu.VMEM((PEERS, MSG, 128), BF),
             pltpu.SMEM((FULL, 128), jnp.int32),

time: 106 us -> 106 us (level)
  no operation moved by 1% of the time
where the time goes in v8:
time: 106 us; the launch traced here: 105 us
  starting transfers between devices  41.6 us (39%)
  Pallas kernels  35.1 us (33%)
  waiting for transfers between devices  25.5 us (24%)
  local copies, waits for them, and re-layouts  2.08 us (2%)
    ppermute x11, starting transfers between devices, shift(): return lax.ppermute(x, axis, [(i, (i + by) % size) for i in range(size)])  19.4 us
    all_to_all x1, starting transfers between devices, body(): lax.all_to_all(send.reshape(PEERS, 1, 128), SAMPLE, split_axis=0, concat_...  12 us
    ppermute x11, waiting for transfers between devices, shift(): return lax.ppermute(x, axis, [(i, (i + by) % size) for i in range(size)])  12 us
    pallas_call x1, Pallas kernels, body(): call(expand_kernel, pltpu.HBM((2, ROWS, ROWS), BF), (2 * ROWS * ROWS * RO...  6.36 us
    all_to_all x1, starting transfers between devices, body(): lax.all_to_all(msg, SAMPLE, split_axis=0, concat_axis=0, tiled=True)  5.67 us
    pallas_call x1, Pallas kernels, body(): call(attend_kernel, pltpu.HBM((PEERS, MSG, 128), BF), (2 * ROWS * ROWS *...  5.44 us
    pallas_call x1, Pallas kernels, body(): call(place_kernel, (pltpu.HBM((ROWS, 128), BF), pltpu.HBM((FULL, 128), jn...  5.07 us
    all_to_all x1, waiting for transfers between devices, body(): lax.all_to_all(send.reshape(PEERS, 1, 128), SAMPLE, split_axis=0, concat_...  4.79 us
  transfers between devices with their start and end apart: 14, of which 10 were waited for; matrix products, arithmetic and copies ran while one was open for 1% of the time, Pallas kernels for 22%

profile of v8, /device:TPU:1, one launch (start us, length us, event | category | flops | bytes accessed | tf_op | source)
XLA Modules:
  0.0 105.1 jit_solution(10282798110595045247)
XLA Ops:
  0.6 0.0 copy-start
  0.6 2.6 %shard_map.104 = (s32[32,128]{1,0:T(8,128)}, s32[48,128]{1,0:T(8,128)}, s32[16,128]{1,0:T(8,128)}) custom-call(s32[1,1024]{1,0:T(1,128)} %bitcast.16, s32[4,1024]{1,0:T(4,128)} %bitcast.15), custom_call_target="tpu_custom_call" | custom-call | flops 400000000 | bytes 1000000 | tf_op jit(solution)/shard_map/pallas_call | solution.py:486
  3.3 12.0 %all-to-all-start = ((s32[32,1,128]{2,1,0:T(1,128)}), s32[32,1,128]{2,1,0:T(1,128)S(1)}, u32[]{:S(2)}, u32[]{:S(2)}) async-start(s32[32,1,128]{2,1,0:T(1,128)} %bitcast.14), calls=%async_computation | async-start | bytes 32768 | tf_op jit(solution)/shard_map/all_to_all | solution.py:495
  15.3 0.0 copy-start.5
  15.3 2.9 %shard_map.107 = (bf16[640,1024]{1,0:T(8,128)(2,1)}, bf16[640,1024]{1,0:T(8,128)(2,1)}) custom-call(bf16[1024,512]{1,0:T(8,128)(2,1)} %up_ref.3, bf16[512,1024]{1,0:T(8,128)(2,1)} %down_ref.3, bf16[128,1024]{1,0:T(8,128)(2,1)} %own_ref.1), custom_call_target="tpu_custom_call" | custom-call | bytes 5000000 | tf_op jit(solution)/shard_map/pallas_call | solution.py:506
  18.2 0.8 shard_map.105.q_ref
  19.0 0.0 copy-start.4
  19.0 4.8 %all-to-all-done = s32[32,1,128]{2,1,0:T(1,128)S(1)} async-done(((s32[32,1,128]{2,1,0:T(1,128)}), s32[32,1,128]{2,1,0:T(1,128)S(1)}, u32[]{:S(2)}, u32[]{:S(2)}) %all-to-all-start) | async-done | bytes 16416 | tf_op jit(solution)/shard_map/all_to_all | solution.py:495
  23.8 1.7 %shard_map.108 = bf16[1536,128]{1,0:T(8,128)(2,1)} custom-call(s32[32,128]{1,0:T(8,128)S(1)} %bitcast.10, bf16[1024,128]{1,0:T(8,128)(2,1)S(1)} %shard_map.105.q_ref, bf16[640,1024]{1,0:T(8,128)(2,1)} %get-tuple-element.22.after_ref), custom_call_target="tpu_custom_call" | custom-call | flops 402653184 | bytes 1000000 | tf_op jit(solution)/shard_map/pallas_call | solution.py:514
  25.6 4.4 %all-to-all-start.1 = ((bf16[32,48,128]{2,1,0:T(8,128)(2,1)}), bf16[32,48,128]{2,1,0:T(8,128)(2,1)S(1)}, u32[]{:S(2)}, u32[]{:S(2)}) async-start(bf16[32,48,128]{2,1,0:T(8,128)(2,1)} %bitcast.12), calls=%async_computation.1 | async-start | bytes 786432 | tf_op jit(solution)/shard_map/all_to_all | solution.py:540
  30.0 2.6 %collective-permute-start.5 = (bf16[640,1024]{1,0:T(8,128)(2,1)}, bf16[640,1024]{1,0:T(8,128)(2,1)}, u32[]{:S(2)}, u32[]{:S(2)}) collective-permute-start(bf16[640,1024]{1,0:T(8,128)(2,1)} %get-tuple-element.22.after_ref), channel_id=1, source_target_pairs={{0,6},{2,0},{4,2},{6,4},{1,7},{3,1},{5,3},{7,5},{8,14},{10,8},{12,... | collective-permute-start | bytes 3932168 | tf_op jit(solution)/shard_map/ppermute | solution.py:480
  32.6 0.0 collective-permute-start.4
  32.6 6.4 %shard_map.109.kv_ref = bf16[2,1024,1024]{2,1,0:T(8,128)(2,1)} custom-call(s32[48,128]{1,0:T(8,128)} %get-tuple-element.23.par_hbm, bf16[1024,8,128]{2,1,0:T(8,128)(2,1)} %k_hbm.1, bf16[1024,8,128]{2,1,0:T(8,128)(2,1)} %v_hbm.1), custom_call_target="tpu_custom_call" | custom-call | flops 4294967296 | bytes 12000000 | tf_op jit(solution)/shard_map/pallas_call | solution.py:522
  39.0 4.0 %all-to-all-done.1.q_ref = bf16[32,48,128]{2,1,0:T(8,128)(2,1)S(1)} async-done(((bf16[32,48,128]{2,1,0:T(8,128)(2,1)}), bf16[32,48,128]{2,1,0:T(8,128)(2,1)S(1)}, u32[]{:S(2)}, u32[]{:S(2)}) %all-to-all-start.1) | async-done | bytes 393248 | tf_op jit(solution)/shard_map/all_to_all | solution.py:540
  43.0 5.4 %shard_map.110 = bf16[32,56,128]{2,1,0:T(8,128)(2,1)} custom-call(s32[16,128]{1,0:T(8,128)} %get-tuple-element.21.full_hbm, bf16[32,48,128]{2,1,0:T(8,128)(2,1)S(1)} %all-to-all-done.1.q_ref, bf16[2,1024,1024]{2,1,0:T(8,128)(2,1)} %shard_map.109.kv_ref), custom_call_target="tpu_custom_call" | custom-call | flops 268435456 | bytes 8000000 | tf_op jit(solution)/shard_map/pallas_call | solution.py:554
  48.5 5.7 %all-to-all-start.2 = ((bf16[32,56,128]{2,1,0:T(8,128)(2,1)}), bf16[32,56,128]{2,1,0:T(8,128)(2,1)}, u32[]{:S(2)}, u32[]{:S(2)}) async-start(bf16[32,56,128]{2,1,0:T(8,128)(2,1)} %shard_map.110), calls=%async_computation.2 | async-start | bytes 917504 | tf_op jit(solution)/shard_map/all_to_all | solution.py:568
  54.2 0.0 copy-done.3
  54.2 3.0 %collective-permute-start.3 = (bf16[128,1024]{1,0:T(8,128)(2,1)S(1)}, bf16[128,1024]{1,0:T(8,128)(2,1)S(1)}, u32[]{:S(2)}, u32[]{:S(2)}) collective-permute-start(bf16[128,1024]{1,0:T(8,128)(2,1)S(1)} %copy-done.3), channel_id=1, source_target_pairs={{0,4},{2,6},{4,0},{6,2},{1,5},{3,7},{5,1},{7,3},{8,12},{10,14},{12... | collective-permute-start | bytes 786440 | tf_op jit(solution)/shard_map/ppermute | solution.py:480
  57.2 5.1 %shard_map.106 = (bf16[1024,128]{1,0:T(8,128)(2,1)}, s32[16,128]{1,0:T(8,128)}, bf16[1024,128]{1,0:T(8,128)(2,1)S(1)}, bf16[1024,128]{1,0:T(8,128)(2,1)}) custom-call(s32[32,128]{1,0:T(8,128)S(1)} %bitcast.11, bf16[1024,1024]{1,0:T(8,128)(2,1)S(1)} %copy-done, bf16[3,1024,128]{2,1,0:T(8,128)(2,1)S(1)} %copy-done.6, bf16[1024,128]{1,0:T(8,128)(2,1)} %copy-done.4), custom_call_target="tpu_custom_call" | custom-call | flops 2000000000 | bytes 4000000 | tf_op jit(solution)/shard_map/pallas_call | solution.py:542
  62.3 0.7 copy-done.7
  63.0 4.7 %all-to-all-done.2.msg_hbm = bf16[32,56,128]{2,1,0:T(8,128)(2,1)} async-done(((bf16[32,56,128]{2,1,0:T(8,128)(2,1)}), bf16[32,56,128]{2,1,0:T(8,128)(2,1)}, u32[]{:S(2)}, u32[]{:S(2)}) %all-to-all-start.2) | async-done | bytes 458784 | tf_op jit(solution)/shard_map/all_to_all | solution.py:568
  67.7 2.8 %shard_map.111 = (bf16[512,128]{1,0:T(8,128)(2,1)S(1)}, bf16[512,128]{1,0:T(8,128)(2,1)S(1)}) custom-call(s32[16,128]{1,0:T(8,128)} %get-tuple-element.20.full_hbm, bf16[32,56,128]{2,1,0:T(8,128)(2,1)} %all-to-all-done.2.msg_hbm, bf16[1024,128]{1,0:T(8,128)(2,1)} %get-tuple-element.24.place_hbm, bf16[1024,128]{1,0:T(8,128)(2,1)} %get-tuple-element.25.v_hbm), custom_call_target="tpu_custom_call" | custom-call | flops 402653184 | bytes 5000000 | tf_op jit(solution)/shard_map/pallas_call | solution.py:570
  70.5 1.3 %collective-permute-start = (bf16[512,128]{1,0:T(8,128)(2,1)S(1)}, bf16[512,128]{1,0:T(8,128)(2,1)S(1)}, u32[]{:S(2)}, u32[]{:S(2)}) collective-permute-start(bf16[512,128]{1,0:T(8,128)(2,1)S(1)} %get-tuple-element.27), channel_id=1, source_target_pairs={{0,2},{2,4},{4,6},{6,0},{1,3},{3,5},{5,7},{7,1},{8,10},{10,12},{12... | collective-permute-start | bytes 393224 | tf_op jit(solution)/shard_map/ppermute | solution.py:480
  71.8 1.5 %collective-permute-start.1 = (bf16[512,128]{1,0:T(8,128)(2,1)S(1)}, bf16[512,128]{1,0:T(8,128)(2,1)S(1)}, u32[]{:S(2)}, u32[]{:S(2)}) collective-permute-start(bf16[512,128]{1,0:T(8,128)(2,1)S(1)} %get-tuple-element.27), channel_id=1, source_target_pairs={{0,6},{2,0},{4,2},{6,4},{1,7},{3,1},{5,3},{7,5},{8,14},{10,8},{12,... | collective-permute-start | bytes 393224 | tf_op jit(solution)/shard_map/ppermute | solution.py:480
  73.2 0.0 collective-permute-done.3.two_ref
  73.3 1.5 %collective-permute-start.2 = (bf16[512,128]{1,0:T(8,128)(2,1)S(1)}, bf16[512,128]{1,0:T(8,128)(2,1)S(1)}, u32[]{:S(2)}, u32[]{:S(2)}) collective-permute-start(bf16[512,128]{1,0:T(8,128)(2,1)S(1)} %get-tuple-element.26.a0), channel_id=1, source_target_pairs={{0,4},{2,6},{4,0},{6,2},{1,5},{3,7},{5,1},{7,3},{8,12},{10,14},{12... | collective-permute-start | bytes 393224 | tf_op jit(solution)/shard_map/ppermute | solution.py:480
  74.8 0.0 collective-permute-done.5.right_ref
  74.8 0.0 collective-permute-done.4.left_ref
  74.8 0.8 collective-permute-done.a1
  75.6 0.0 collective-permute-done.1.a2
  75.6 3.0 %collective-permute-done.2.a3 = bf16[512,128]{1,0:T(8,128)(2,1)S(1)} collective-permute-done((bf16[512,128]{1,0:T(8,128)(2,1)S(1)}, bf16[512,128]{1,0:T(8,128)(2,1)S(1)}, u32[]{:S(2)}, u32[]{:S(2)}) %collective-permute-start.2) | collective-permute-done | bytes 131104 | tf_op jit(solution)/shard_map/ppermute | solution.py:480
  78.6 1.8 %shard_map.112.p_ref = bf16[512,1024]{1,0:T(8,128)(2,1)S(1)} custom-call(bf16[512,128]{1,0:T(8,128)(2,1)S(1)} %get-tuple-element.26.a0, bf16[512,128]{1,0:T(8,128)(2,1)S(1)} %collective-permute-done.a1, bf16[512,128]{1,0:T(8,128)(2,1)S(1)} %collective-permute-done.1.a2, bf16[512,128]{1,0:T(8,128)(2,1)S(1)} %collective-permute-done.2.a3, ...), custom_call_target="tpu_custom_call" | custom-call | flops 600000000 | bytes 3000000 | tf_op jit(solution)/shard_map/pallas_call | solution.py:589
  80.3 0.0 copy-start.8
  80.4 6.0 %collective-permute-start.6 = (bf16[512,1024]{1,0:T(8,128)(2,1)S(1)}, bf16[512,1024]{1,0:T(8,128)(2,1)S(1)}, u32[]{:S(2)}, u32[]{:S(2)}) collective-permute-start(bf16[512,1024]{1,0:T(8,128)(2,1)S(1)} %shard_map.112.p_ref), channel_id=1, source_target_pairs={{0,1},{1,0},{2,3},{3,2},{4,5},{5,4},{6,7},{7,6},{8,9},{9,8},{10,11... | collective-permute-start | bytes 3145736 | tf_op jit(solution)/shard_map/ppermute | solution.py:480
  86.4 2.3 %collective-permute-done.6.r_ref = bf16[512,1024]{1,0:T(8,128)(2,1)S(1)} collective-permute-done((bf16[512,1024]{1,0:T(8,128)(2,1)S(1)}, bf16[512,1024]{1,0:T(8,128)(2,1)S(1)}, u32[]{:S(2)}, u32[]{:S(2)}) %collective-permute-start.6) | collective-permute-done | bytes 1048608 | tf_op jit(solution)/shard_map/ppermute | solution.py:480
  88.7 4.8 %shard_map.113 = (f32[4,512,128]{2,1,0:T(8,128)S(1)}, bf16[4,512,128]{2,1,0:T(8,128)(2,1)S(1)}) custom-call(bf16[1024,1024]{1,0:T(8,128)(2,1)S(1)} %copy-done, bf16[512,1024]{1,0:T(8,128)(2,1)S(1)} %shard_map.112.p_ref, bf16[512,1024]{1,0:T(8,128)(2,1)S(1)} %collective-permute-done.6.r_ref, bf16[1024,512]{1,0:T(8,128)(2,1)S(1)} %copy-done.1, ...), custom_call_target="tpu_custom_call" | custom-call | flops 2000000000 | bytes 10000000 | tf_op jit(solution)/shard_map/pallas_call | solution.py:608
  93.5 0.5 collective-permute-start.7
  93.9 1.5 %collective-permute-done.7.other_ref = bf16[4,512,128]{2,1,0:T(8,128)(2,1)S(1)} collective-permute-done((bf16[4,512,128]{2,1,0:T(8,128)(2,1)S(1)}, bf16[4,512,128]{2,1,0:T(8,128)(2,1)S(1)}, u32[]{:S(2)}, u32[]{:S(2)}) %collective-permute-start.7) | collective-permute-done | bytes 524320 | tf_op jit(solution)/shard_map/ppermute | solution.py:480
  95.5 0.1 shard_map.114
  95.5 1.3 %collective-permute-start.10 = (bf16[512,128]{1,0:T(8,128)(2,1)S(1)}, bf16[512,128]{1,0:T(8,128)(2,1)S(1)}, u32[]{:S(2)}, u32[]{:S(2)}) collective-permute-start(bf16[512,128]{1,0:T(8,128)(2,1)S(1)} %get-tuple-element.34), channel_id=1, source_target_pairs={{0,6},{2,0},{4,2},{6,4},{1,7},{3,1},{5,3},{7,5},{8,14},{10,8},{12,... | collective-permute-start | bytes 393224 | tf_op jit(solution)/shard_map/ppermute | solution.py:480
  96.9 0.2 collective-permute-start.8
  97.1 1.5 %collective-permute-start.9 = (bf16[512,128]{1,0:T(8,128)(2,1)S(1)}, bf16[512,128]{1,0:T(8,128)(2,1)S(1)}, u32[]{:S(2)}, u32[]{:S(2)}) collective-permute-start(bf16[512,128]{1,0:T(8,128)(2,1)S(1)} %get-tuple-element.33), channel_id=1, source_target_pairs={{0,4},{2,6},{4,0},{6,2},{1,5},{3,7},{5,1},{7,3},{8,12},{10,14},{12... | collective-permute-start | bytes 393224 | tf_op jit(solution)/shard_map/ppermute | solution.py:480
  98.6 0.1 pad_maximum_fusion
  98.7 1.3 %copy.13 = bf16[1024,2,128]{2,1,0:T(2,128)(2,1)} copy(bf16[1024,2,128]{2,0,1:T(8,128)(2,1)S(1)} %pad_maximum_fusion) | data formatting | bytes 1048576
  100.0 0.3 collective-permute-done.10.p3
  100.3 3.5 %collective-permute-done.8.p1 = bf16[512,128]{1,0:T(8,128)(2,1)S(1)} collective-permute-done((bf16[512,128]{1,0:T(8,128)(2,1)S(1)}, bf16[512,128]{1,0:T(8,128)(2,1)S(1)}, u32[]{:S(2)}, u32[]{:S(2)}) %collective-permute-start.8) | collective-permute-done | bytes 131104 | tf_op jit(solution)/shard_map/ppermute | solution.py:480
  103.8 0.5 collective-permute-done.9.p2
  104.3 0.8 shard_map.115
  (14 shorter events, 0.0 us)
Async XLA Ops:
  0.6 17.6 %copy-start = (bf16[1024,1024]{1,0:T(8,128)(2,1)S(1)}, bf16[1024,1024]{1,0:T(8,128)(2,1)}, u32[]{:S(2)}) copy-start(bf16[1024,1024]{1,0:T(8,128)(2,1)} %x_ref.5) | copy-start | bytes 6291460
  3.3 20.6 %all-to-all-start = ((s32[32,1,128]{2,1,0:T(1,128)}), s32[32,1,128]{2,1,0:T(1,128)S(1)}, u32[]{:S(2)}, u32[]{:S(2)}) async-start(s32[32,1,128]{2,1,0:T(1,128)} %bitcast.14), calls=%async_computation | async-start | bytes 32768 | tf_op jit(solution)/shard_map/all_to_all | solution.py:495
  15.3 2.9 %copy-start.5 = (bf16[3,1024,128]{2,1,0:T(8,128)(2,1)S(1)}, bf16[3,1024,128]{2,1,0:T(8,128)(2,1)}, u32[]{:S(2)}) copy-start(bf16[3,1024,128]{2,1,0:T(8,128)(2,1)} %w_ref.3) | copy-start | bytes 2359300
  19.0 20.0 %copy-start.4 = (bf16[1024,128]{1,0:T(8,128)(2,1)}, bf16[1024,128]{1,0:T(8,128)(2,1)S(1)}, u32[]{:S(2)}) copy-start(bf16[1024,128]{1,0:T(8,128)(2,1)S(1)} %shard_map.105.q_ref) | copy-start | bytes 786436
  25.6 17.4 %all-to-all-start.1 = ((bf16[32,48,128]{2,1,0:T(8,128)(2,1)}), bf16[32,48,128]{2,1,0:T(8,128)(2,1)S(1)}, u32[]{:S(2)}, u32[]{:S(2)}) async-start(bf16[32,48,128]{2,1,0:T(8,128)(2,1)} %bitcast.12), calls=%async_computation.1 | async-start | bytes 786432 | tf_op jit(solution)/shard_map/all_to_all | solution.py:540
  30.0 44.7 %collective-permute-start.5 = (bf16[640,1024]{1,0:T(8,128)(2,1)}, bf16[640,1024]{1,0:T(8,128)(2,1)}, u32[]{:S(2)}, u32[]{:S(2)}) collective-permute-start(bf16[640,1024]{1,0:T(8,128)(2,1)} %get-tuple-element.22.after_ref), channel_id=1, source_target_pairs={{0,6},{2,0},{4,2},{6,4},{1,7},{3,1},{5,3},{7,5},{8,14},{10,8},{12,... | collective-permute-start | bytes 3932168 | tf_op jit(solution)/shard_map/ppermute | solution.py:480
  32.6 42.2 %collective-permute-start.4 = (bf16[640,1024]{1,0:T(8,128)(2,1)}, bf16[640,1024]{1,0:T(8,128)(2,1)}, u32[]{:S(2)}, u32[]{:S(2)}) collective-permute-start(bf16[640,1024]{1,0:T(8,128)(2,1)} %get-tuple-element.28), channel_id=1, source_target_pairs={{0,2},{2,4},{4,6},{6,0},{1,3},{3,5},{5,7},{7,1},{8,10},{10,12},{12... | collective-permute-start | bytes 3932168 | tf_op jit(solution)/shard_map/ppermute | solution.py:480
  43.0 11.1 %copy-start.3 = (bf16[128,1024]{1,0:T(8,128)(2,1)S(1)}, bf16[128,1024]{1,0:T(8,128)(2,1)}, u32[]{:S(2)}) copy-start(bf16[128,1024]{1,0:T(8,128)(2,1)} %own_ref.1) | copy-start | bytes 786436
  43.0 14.2 %copy-start.6 = (bf16[3,1024,128]{2,1,0:T(8,128)(2,1)S(1)}, bf16[3,1024,128]{2,1,0:T(8,128)(2,1)}, u32[]{:S(2)}) copy-start(bf16[3,1024,128]{2,1,0:T(8,128)(2,1)} %w_ref.3) | copy-start | bytes 2359300
  48.5 19.2 %all-to-all-start.2 = ((bf16[32,56,128]{2,1,0:T(8,128)(2,1)}), bf16[32,56,128]{2,1,0:T(8,128)(2,1)}, u32[]{:S(2)}, u32[]{:S(2)}) async-start(bf16[32,56,128]{2,1,0:T(8,128)(2,1)} %shard_map.110), calls=%async_computation.2 | async-start | bytes 917504 | tf_op jit(solution)/shard_map/all_to_all | solution.py:568
  54.2 19.1 %collective-permute-start.3 = (bf16[128,1024]{1,0:T(8,128)(2,1)S(1)}, bf16[128,1024]{1,0:T(8,128)(2,1)S(1)}, u32[]{:S(2)}, u32[]{:S(2)}) collective-permute-start(bf16[128,1024]{1,0:T(8,128)(2,1)S(1)} %copy-done.3), channel_id=1, source_target_pairs={{0,4},{2,6},{4,0},{6,2},{1,5},{3,7},{5,1},{7,3},{8,12},{10,14},{12... | collective-permute-start | bytes 786440 | tf_op jit(solution)/shard_map/ppermute | solution.py:480
  62.3 0.7 copy-start.7
  70.5 5.1 %collective-permute-start = (bf16[512,128]{1,0:T(8,128)(2,1)S(1)}, bf16[512,128]{1,0:T(8,128)(2,1)S(1)}, u32[]{:S(2)}, u32[]{:S(2)}) collective-permute-start(bf16[512,128]{1,0:T(8,128)(2,1)S(1)} %get-tuple-element.27), channel_id=1, source_target_pairs={{0,2},{2,4},{4,6},{6,0},{1,3},{3,5},{5,7},{7,1},{8,10},{10,12},{12... | collective-permute-start | bytes 393224 | tf_op jit(solution)/shard_map/ppermute | solution.py:480
  71.8 3.8 %collective-permute-start.1 = (bf16[512,128]{1,0:T(8,128)(2,1)S(1)}, bf16[512,128]{1,0:T(8,128)(2,1)S(1)}, u32[]{:S(2)}, u32[]{:S(2)}) collective-permute-start(bf16[512,128]{1,0:T(8,128)(2,1)S(1)} %get-tuple-element.27), channel_id=1, source_target_pairs={{0,6},{2,0},{4,2},{6,4},{1,7},{3,1},{5,3},{7,5},{8,14},{10,8},{12,... | collective-permute-start | bytes 393224 | tf_op jit(solution)/shard_map/ppermute | solution.py:480
  73.3 15.4 %copy-start.1 = (bf16[1024,512]{1,0:T(8,128)(2,1)S(1)}, bf16[1024,512]{1,0:T(8,128)(2,1)}, u32[]{:S(2)}) copy-start(bf16[1024,512]{1,0:T(8,128)(2,1)} %up_ref.3) | copy-start | bytes 3145732
  73.3 15.4 %copy-start.2 = (bf16[512,1024]{1,0:T(8,128)(2,1)S(1)}, bf16[512,1024]{1,0:T(8,128)(2,1)}, u32[]{:S(2)}) copy-start(bf16[512,1024]{1,0:T(8,128)(2,1)} %down_ref.3) | copy-start | bytes 3145732
  73.3 5.3 %collective-permute-start.2 = (bf16[512,128]{1,0:T(8,128)(2,1)S(1)}, bf16[512,128]{1,0:T(8,128)(2,1)S(1)}, u32[]{:S(2)}, u32[]{:S(2)}) collective-permute-start(bf16[512,128]{1,0:T(8,128)(2,1)S(1)} %get-tuple-element.26.a0), channel_id=1, source_target_pairs={{0,4},{2,6},{4,0},{6,2},{1,5},{3,7},{5,1},{7,3},{8,12},{10,14},{12... | collective-permute-start | bytes 393224 | tf_op jit(solution)/shard_map/ppermute | solution.py:480
  80.3 18.3 %copy-start.8 = (bf16[1024,128]{1,0:T(8,128)(2,1)S(1)}, bf16[1024,128]{1,0:T(8,128)(2,1)}, u32[]{:S(2)}) copy-start(bf16[1024,128]{1,0:T(8,128)(2,1)} %copy-done.7) | copy-start | bytes 786436
  80.4 18.3 %copy-start.9 = (bf16[1024,128]{1,0:T(8,128)(2,1)S(1)}, bf16[1024,128]{1,0:T(8,128)(2,1)}, u32[]{:S(2)}) copy-start(bf16[1024,128]{1,0:T(8,128)(2,1)} %get-tuple-element.25.v_hbm) | copy-start | bytes 786436
  80.4 8.3 %collective-permute-start.6 = (bf16[512,1024]{1,0:T(8,128)(2,1)S(1)}, bf16[512,1024]{1,0:T(8,128)(2,1)S(1)}, u32[]{:S(2)}, u32[]{:S(2)}) collective-permute-start(bf16[512,1024]{1,0:T(8,128)(2,1)S(1)} %shard_map.112.p_ref), channel_id=1, source_target_pairs={{0,1},{1,0},{2,3},{3,2},{4,5},{5,4},{6,7},{7,6},{8,9},{9,8},{10,11... | collective-permute-start | bytes 3145736 | tf_op jit(solution)/shard_map/ppermute | solution.py:480
  93.5 2.0 %collective-permute-start.7 = (bf16[4,512,128]{2,1,0:T(8,128)(2,1)S(1)}, bf16[4,512,128]{2,1,0:T(8,128)(2,1)S(1)}, u32[]{:S(2)}, u32[]{:S(2)}) collective-permute-start(bf16[4,512,128]{2,1,0:T(8,128)(2,1)S(1)} %get-tuple-element.30), channel_id=1, source_target_pairs={{0,1},{1,0},{2,3},{3,2},{4,5},{5,4},{6,7},{7,6},{8,9},{9,8},{10,11... | collective-permute-start | bytes 1572872 | tf_op jit(solution)/shard_map/ppermute | solution.py:480
  95.5 4.8 %collective-permute-start.10 = (bf16[512,128]{1,0:T(8,128)(2,1)S(1)}, bf16[512,128]{1,0:T(8,128)(2,1)S(1)}, u32[]{:S(2)}, u32[]{:S(2)}) collective-permute-start(bf16[512,128]{1,0:T(8,128)(2,1)S(1)} %get-tuple-element.34), channel_id=1, source_target_pairs={{0,6},{2,0},{4,2},{6,4},{1,7},{3,1},{5,3},{7,5},{8,14},{10,8},{12,... | collective-permute-start | bytes 393224 | tf_op jit(solution)/shard_map/ppermute | solution.py:480
  96.9 6.9 %collective-permute-start.8 = (bf16[512,128]{1,0:T(8,128)(2,1)S(1)}, bf16[512,128]{1,0:T(8,128)(2,1)S(1)}, u32[]{:S(2)}, u32[]{:S(2)}) collective-permute-start(bf16[512,128]{1,0:T(8,128)(2,1)S(1)} %get-tuple-element.32), channel_id=1, source_target_pairs={{0,2},{2,4},{4,6},{6,0},{1,3},{3,5},{5,7},{7,1},{8,10},{10,12},{12... | collective-permute-start | bytes 393224 | tf_op jit(solution)/shard_map/ppermute | solution.py:480
  97.1 7.3 %collective-permute-start.9 = (bf16[512,128]{1,0:T(8,128)(2,1)S(1)}, bf16[512,128]{1,0:T(8,128)(2,1)S(1)}, u32[]{:S(2)}, u32[]{:S(2)}) collective-permute-start(bf16[512,128]{1,0:T(8,128)(2,1)S(1)} %get-tuple-element.33), channel_id=1, source_target_pairs={{0,4},{2,6},{4,0},{6,2},{1,5},{3,7},{5,1},{7,3},{8,12},{10,14},{12... | collective-permute-start | bytes 393224 | tf_op jit(solution)/shard_map/ppermute | solution.py:480
